TPU v7x, 32 devices: a whole 2x2x4 slice. The times are simulated.
32 devices in a mesh: seq: 8 (over z, y), chrom: 4 (over x, core).
Axes of the slice: x: 2, y: 2, z: 4, core: 2. Of those that a mesh axis runs over, the one named last changes fastest.
Arguments:
- features: bfloat16 [4, 5120, 768], P('chrom', 'seq'), may hold values from -6 to 6
- first_dilated_taps: bfloat16 [3, 768, 384], replicated, may hold values from -0.125 to 0.125
- first_norm_scale: float32 [384], replicated, may hold values from 0.5 to 2
- first_norm_offset: float32 [384], replicated, may hold values from -3 to 3
- first_pointwise_weight: bfloat16 [384, 768], replicated, may hold values from -0.3125 to 0.3125
- second_dilated_taps: bfloat16 [3, 768, 384], replicated, may hold values from -0.125 to 0.125
- second_norm_scale: float32 [384], replicated, may hold values from 0.5 to 2
- second_norm_offset: float32 [384], replicated, may hold values from -3 to 3
- second_pointwise_weight: bfloat16 [384, 768], replicated, may hold values from -0.3125 to 0.3125
- cotangent: bfloat16 [4, 5120, 768], P('chrom', 'seq'), may hold values from -6 to 6
Outputs:
- grad_input: bfloat16 [4, 5120, 768], P('chrom', 'seq')
- grad_conv_a: float32 [3, 768, 384], P(None, 'seq')
- grad_point_a: float32 [384, 768], P(None, 'seq')
- grad_scale_a: float32 [384], replicated
- grad_shift_a: float32 [384], replicated
- grad_conv_b: float32 [3, 768, 384], P(None, 'seq')
- grad_point_b: float32 [384, 768], P(None, 'seq')
- grad_scale_b: float32 [384], replicated
- grad_shift_b: float32 [384], replicated
All inputs are finite; a program needn't handle non-finite values.
Results may differ from a plain program's by a relative error of at most 0.018.
Values may be sent and summed in bfloat16 or wider, within the bound.
No kernel may reach another device: no remote copies, remote signals or barrier semaphores. Data moves between devices by JAX's collectives and lax.ppermute only.
A program may use at most 128 MiB of HBM per device.

v0:
```python
import math

import jax
import jax.numpy as jnp
from jax import lax
from jax.sharding import PartitionSpec as P

DILATION_FIRST = 4096
DILATION_SECOND = 2048


def passed_along(value, axis, steps):
    count = lax.axis_size(axis)
    initial, last = (max(0, -steps), min(count, count - steps))
    return lax.ppermute(value, axis, [(source, source + steps) for source in range(initial, last)])


def smooth_value(normed):
    return normed * jax.nn.sigmoid(1.702 * normed)


def smooth_slope(normed):
    sigmoid_part = jax.nn.sigmoid(1.702 * normed)
    return sigmoid_part * (1.0 + 1.702 * normed * (1.0 - sigmoid_part))


def reach_inputs(field, offset):
    rows_dev = field.shape[0]
    whole_hops = offset // rows_dev
    remainder = offset % rows_dev
    near_rows = passed_along(field[remainder:], "seq", -whole_hops)
    far_rows = passed_along(field[:remainder], "seq", -(whole_hops + 1))
    return jnp.concatenate([near_rows, far_rows], 0)


def reach_products(field, offset):
    rows_dev = field.shape[0]
    whole_hops = offset // rows_dev
    remainder = offset % rows_dev
    near_rows = passed_along(field[remainder:].astype(jnp.bfloat16), "seq", -whole_hops).astype(
        jnp.float32
    )
    far_rows = passed_along(
        field[:remainder].astype(jnp.bfloat16), "seq", -(whole_hops + 1)
    ).astype(jnp.float32)
    return jnp.concatenate([near_rows, far_rows], 0)


def bottleneck_block_ahead(inputs, conv_weight, bn_scale, bn_shift, dilation):
    before = reach_inputs(inputs, -dilation)
    after = reach_inputs(inputs, dilation)
    pre_act = jnp.dot(before, conv_weight[0], preferred_element_type=jnp.float32)
    pre_act = pre_act + jnp.dot(inputs, conv_weight[1], preferred_element_type=jnp.float32)
    pre_act = pre_act + jnp.dot(after, conv_weight[2], preferred_element_type=jnp.float32)
    normed = bn_scale * pre_act + bn_shift
    activated = smooth_value(normed).astype(jnp.bfloat16)
    return (before, after, pre_act, normed, activated)


def bottleneck_block_reverse(
    inputs, saved, conv_weight, bn_scale, point_weight, upstream, dilation
):
    before, after, pre_act, normed, activated = saved
    grad_act = jnp.dot(upstream, point_weight.T, preferred_element_type=jnp.float32)
    grad_norm = grad_act * smooth_slope(normed)
    grad_pre = (grad_norm * bn_scale).astype(jnp.bfloat16)
    grad_point = jnp.dot(activated.T, upstream, preferred_element_type=jnp.float32)
    grad_scale = jnp.sum(grad_norm * pre_act, 0)
    grad_shift = jnp.sum(grad_norm, 0)
    grad_conv = jnp.stack(
        [
            jnp.dot(before.T, grad_pre, preferred_element_type=jnp.float32),
            jnp.dot(inputs.T, grad_pre, preferred_element_type=jnp.float32),
            jnp.dot(after.T, grad_pre, preferred_element_type=jnp.float32),
        ]
    )
    grad_in = upstream.astype(jnp.float32) + jnp.dot(
        grad_pre, conv_weight[1].T, preferred_element_type=jnp.float32
    )
    outer_first = jnp.dot(grad_pre, conv_weight[0].T, preferred_element_type=jnp.float32)
    outer_last = jnp.dot(grad_pre, conv_weight[2].T, preferred_element_type=jnp.float32)
    grad_in = grad_in + reach_products(outer_first, dilation)
    grad_in = grad_in + reach_products(outer_last, -dilation)
    return (grad_in.astype(jnp.bfloat16), (grad_conv, grad_point, grad_scale, grad_shift))


def settle_joint(first_block_partials, second_block_partials, factor):
    parts = (
        lax.psum_scatter(first_block_partials[0], "seq", scatter_dimension=1, tiled=True),
        lax.psum_scatter(first_block_partials[1], "seq", scatter_dimension=1, tiled=True),
        lax.psum_scatter(second_block_partials[0], "seq", scatter_dimension=1, tiled=True),
        lax.psum_scatter(second_block_partials[1], "seq", scatter_dimension=1, tiled=True),
    )
    parts = (
        lax.psum(parts[0].astype(jnp.bfloat16), "chrom").astype(jnp.float32),
        lax.psum(parts[1].astype(jnp.bfloat16), "chrom").astype(jnp.float32),
        lax.psum(parts[2].astype(jnp.bfloat16), "chrom").astype(jnp.float32),
        lax.psum(parts[3].astype(jnp.bfloat16), "chrom").astype(jnp.float32),
    )
    norms = lax.psum(
        (
            first_block_partials[2],
            first_block_partials[3],
            second_block_partials[2],
            second_block_partials[3],
        ),
        ("seq", "chrom"),
    )
    settled_a = (parts[0] * factor, parts[1] * factor, norms[0] * factor, norms[1] * factor)
    settled_b = (parts[2] * factor, parts[3] * factor, norms[2] * factor, norms[3] * factor)
    return (settled_a, settled_b)


def body(
    features,
    first_dilated_taps,
    first_norm_scale,
    first_norm_offset,
    first_pointwise_weight,
    second_dilated_taps,
    second_norm_scale,
    second_norm_offset,
    second_pointwise_weight,
    cotangent,
):
    first_block_output = features[0]
    rows_dev = first_block_output.shape[0]
    factor = 1.0 / math.sqrt(rows_dev * lax.axis_size("seq") * lax.axis_size("chrom"))
    first_block_stash = bottleneck_block_ahead(
        first_block_output, first_dilated_taps, first_norm_scale, first_norm_offset, DILATION_FIRST
    )
    second_block_output = (
        first_block_output.astype(jnp.float32)
        + jnp.dot(first_block_stash[4], first_pointwise_weight, preferred_element_type=jnp.float32)
    ).astype(jnp.bfloat16)
    second_block_stash = bottleneck_block_ahead(
        second_block_output,
        second_dilated_taps,
        second_norm_scale,
        second_norm_offset,
        DILATION_SECOND,
    )
    second_block_gradient, second_block_partials = bottleneck_block_reverse(
        second_block_output,
        second_block_stash,
        second_dilated_taps,
        second_norm_scale,
        second_pointwise_weight,
        cotangent[0],
        DILATION_SECOND,
    )
    first_block_gradient, first_block_partials = bottleneck_block_reverse(
        first_block_output,
        first_block_stash,
        first_dilated_taps,
        first_norm_scale,
        first_pointwise_weight,
        second_block_gradient,
        DILATION_FIRST,
    )
    first_block_partials, second_block_partials = settle_joint(
        first_block_partials, second_block_partials, factor
    )
    return (
        first_block_gradient[None],
        first_block_partials[0],
        first_block_partials[1],
        first_block_partials[2],
        first_block_partials[3],
        second_block_partials[0],
        second_block_partials[1],
        second_block_partials[2],
        second_block_partials[3],
    )


def solution(mesh):
    in_specs = (
        P("chrom", "seq", None),
        P(),
        P(),
        P(),
        P(),
        P(),
        P(),
        P(),
        P(),
        P("chrom", "seq", None),
    )
    out_specs = (
        P("chrom", "seq", None),
        P(None, "seq", None),
        P(None, "seq"),
        P(),
        P(),
        P(None, "seq", None),
        P(None, "seq"),
        P(),
        P(),
    )
    return jax.shard_map(body, mesh=mesh, in_specs=in_specs, out_specs=out_specs, check_vma=False)
```

profile of v0, /device:TPU:0, one launch (start us, length us, event | category | flops | bytes accessed | tf_op | source)
XLA Modules:
  0.0 480.9 jit_solution(13874408115608537342)
XLA Ops:
  7.3 1.5 slice_bitcast_fusion.1
  8.7 1.3 collective-permute-start.2
  10.1 8.8 %collective-permute-start = (bf16[256,768]{1,0:T(8,128)(2,1)S(1)}, bf16[256,768]{1,0:T(8,128)(2,1)S(1)}, u32[]{:S(2)}, u32[]{:S(2)}) collective-permute-start(bf16[256,768]{1,0:T(8,128)(2,1)S(1)} %get-tuple-element.29), channel_id=1, source_target_pairs={{0,28},{1,29},{2,30},{3,31}} | collective-permute-start | bytes 1179656 | tf_op jit(solution)/shard_map/ppermute | solution.py:15
  18.9 1.3 collective-permute-start.3
  20.2 1.3 collective-permute-start.1
  21.6 0.7 fusion.4
  22.2 6.2 %collective-permute-done = bf16[256,768]{1,0:T(8,128)(2,1)S(1)} collective-permute-done((bf16[256,768]{1,0:T(8,128)(2,1)S(1)}, bf16[256,768]{1,0:T(8,128)(2,1)S(1)}, u32[]{:S(2)}, u32[]{:S(2)}) %collective-permute-start) | collective-permute-done | bytes 393248 | tf_op jit(solution)/shard_map/ppermute | solution.py:15
  28.5 9.9 %collective-permute-done.3 = bf16[256,768]{1,0:T(8,128)(2,1)S(1)} collective-permute-done((bf16[256,768]{1,0:T(8,128)(2,1)S(1)}, bf16[256,768]{1,0:T(8,128)(2,1)S(1)}, u32[]{:S(2)}, u32[]{:S(2)}) %collective-permute-start.3) | collective-permute-done | bytes 393248 | tf_op jit(solution)/shard_map/ppermute | solution.py:15
  38.5 0.7 fusion.21
  39.7 0.7 fusion
  40.7 0.8 add_convert_fusion.2
  41.7 1.4 collective-permute-start.6
  43.2 5.1 %collective-permute-start.4 = (bf16[128,768]{1,0:T(8,128)(2,1)S(1)}, bf16[128,768]{1,0:T(8,128)(2,1)S(1)}, u32[]{:S(2)}, u32[]{:S(2)}) collective-permute-start(bf16[128,768]{1,0:T(8,128)(2,1)S(1)} %get-tuple-element.25), channel_id=1, source_target_pairs={{0,16},{4,20},{8,24},{12,28},{1,17},{5,21},{9,25},{13,29},{2,18},{... | collective-permute-start | bytes 589832 | tf_op jit(solution)/shard_map/ppermute | solution.py:15
  48.2 1.3 collective-permute-start.7
  49.5 3.3 collective-permute-start.5
  52.9 0.7 fusion.14
  53.6 13.4 %collective-permute-done.6 = bf16[512,768]{1,0:T(8,128)(2,1)S(1)} collective-permute-done((bf16[512,768]{1,0:T(8,128)(2,1)S(1)}, bf16[512,768]{1,0:T(8,128)(2,1)S(1)}, u32[]{:S(2)}, u32[]{:S(2)}) %collective-permute-start.6) | collective-permute-done | bytes 786464 | tf_op jit(solution)/shard_map/ppermute | solution.py:15
  67.0 20.0 %collective-permute-done.7 = bf16[128,768]{1,0:T(8,128)(2,1)S(1)} collective-permute-done((bf16[128,768]{1,0:T(8,128)(2,1)S(1)}, bf16[128,768]{1,0:T(8,128)(2,1)S(1)}, u32[]{:S(2)}, u32[]{:S(2)}) %collective-permute-start.7) | collective-permute-done | bytes 196640 | tf_op jit(solution)/shard_map/ppermute | solution.py:15
  87.0 0.7 fusion.10
  87.8 0.7 fusion.1
  88.8 0.9 copy-done.16
  89.7 2.0 fusion.6
  91.8 2.8 fusion.49
  94.6 0.7 convolution_convert_fusion.2
  95.4 2.8 collective-permute-start.11
  98.2 0.7 convolution_convert_fusion.3
  99.0 1.3 collective-permute-start.8
  100.4 5.3 %collective-permute-start.10 = (bf16[128,768]{1,0:T(8,128)(2,1)S(1)}, bf16[128,768]{1,0:T(8,128)(2,1)S(1)}, u32[]{:S(2)}, u32[]{:S(2)}) collective-permute-start(bf16[128,768]{1,0:T(8,128)(2,1)S(1)} %slice.124), channel_id=1, source_target_pairs={{0,16},{4,20},{8,24},{12,28},{1,17},{5,21},{9,25},{13,29},{2,18},{... | collective-permute-start | bytes 589832 | tf_op jit(solution)/shard_map/ppermute | solution.py:15
  105.7 1.3 collective-permute-start.9
  107.0 23.1 %collective-permute-done.10 = bf16[128,768]{1,0:T(8,128)(2,1)S(1)} collective-permute-done((bf16[128,768]{1,0:T(8,128)(2,1)S(1)}, bf16[128,768]{1,0:T(8,128)(2,1)S(1)}, u32[]{:S(2)}, u32[]{:S(2)}) %collective-permute-start.10) | collective-permute-done | bytes 196640 | tf_op jit(solution)/shard_map/ppermute | solution.py:15
  130.1 22.1 %collective-permute-done.9 = bf16[128,768]{1,0:T(8,128)(2,1)S(1)} collective-permute-done((bf16[128,768]{1,0:T(8,128)(2,1)S(1)}, bf16[128,768]{1,0:T(8,128)(2,1)S(1)}, u32[]{:S(2)}, u32[]{:S(2)}) %collective-permute-start.9) | collective-permute-done | bytes 196640 | tf_op jit(solution)/shard_map/ppermute | solution.py:15
  152.2 0.8 add_convert_fusion.1
  153.0 0.9 copy-done.25
  154.0 1.9 fusion.48
  156.2 1.9 convolution_bitcast_fusion
  158.1 0.8 convolution_bitcast_fusion.1
  159.3 0.8 convolution_bitcast_fusion.2
  160.1 2.0 pad_maximum_fusion.1
  162.1 1.1 copy-done.15
  163.2 2.2 fusion.50
  165.5 0.8 convolution_bitcast_fusion.4
  166.7 0.8 convolution_bitcast_fusion.3
  167.9 0.8 convolution_bitcast_fusion.5
  168.7 2.0 pad_maximum_fusion
  170.8 1.8 convolution_convert_fusion
  172.6 2.1 collective-permute-start.15
  174.7 1.8 convolution_convert_fusion.1
  176.5 1.3 collective-permute-start.12
  177.9 5.0 %collective-permute-start.14 = (bf16[256,768]{1,0:T(8,128)(2,1)S(1)}, bf16[256,768]{1,0:T(8,128)(2,1)S(1)}, u32[]{:S(2)}, u32[]{:S(2)}) collective-permute-start(bf16[256,768]{1,0:T(8,128)(2,1)S(1)} %slice.128), channel_id=1, source_target_pairs={{0,28},{1,29},{2,30},{3,31}} | collective-permute-start | bytes 1179656 | tf_op jit(solution)/shard_map/ppermute | solution.py:15
  182.9 1.3 collective-permute-start.13
  184.2 45.2 %all-reduce = (f32[384]{0:T(512)S(1)}, f32[384]{0:T(512)S(1)}, f32[384]{0:T(512)S(1)}, f32[384]{0:T(512)S(1)}) all-reduce(f32[384]{0:T(512)S(1)} %get-tuple-element.12, f32[384]{0:T(512)S(1)} %get-tuple-element.11, f32[384]{0:T(512)S(1)} %get-tuple-element.10, ...), channel_id=1, replica_groups=mesh['seq'=8,'chrom'=4] {'seq','chrom'}, use_global_device_ids=true, to_apply=%region_5.0 | all-reduce | flops 1536 | bytes 12288 | tf_op jit(solution)/shard_map/psum | solution.py:100
  229.4 0.6 broadcast_multiply_fusion.2
  230.0 0.6 broadcast_multiply_fusion
  230.6 1.6 convert_element_type.86
  232.1 38.1 %reduce-scatter.7.cloned.1.call-done = f32[384,96]{0,1:T(8,128)} async-done(((f32[384,768]{0,1:T(8,128)}), f32[384,96]{0,1:T(8,128)}) %reduce-scatter.7.cloned.1.call-update) | async-done | bytes 147472 | tf_op jit(solution)/shard_map/reduce_scatter | solution.py:90
  270.2 1.6 convert_element_type.81
  271.7 80.3 %reduce-scatter.9.cloned.1.call-done = f32[3,96,384]{2,1,0:T(8,128)} async-done(((f32[3,768,384]{2,1,0:T(8,128)}), f32[3,96,384]{2,1,0:T(8,128)}) %reduce-scatter.9.cloned.1.call-update) | async-done | bytes 442384 | tf_op jit(solution)/shard_map/reduce_scatter | solution.py:91
  352.0 1.7 convert_element_type.83
  353.7 80.5 %reduce-scatter.5.cloned.1.call-done = f32[3,96,384]{2,1,0:T(8,128)} async-done(((f32[3,768,384]{2,1,0:T(8,128)}), f32[3,96,384]{2,1,0:T(8,128)}) %reduce-scatter.5.cloned.1.call-update) | async-done | bytes 442384 | tf_op jit(solution)/shard_map/reduce_scatter | solution.py:89
  434.2 1.7 convert_element_type.79
  436.0 3.6 fusion.2
  439.6 31.1 %all-reduce.4.cloned.1.call-done = (bf16[3,96,384]{2,1,0:T(8,128)(2,1)}, bf16[384,96]{0,1:T(8,128)(2,1)}, bf16[3,96,384]{2,1,0:T(8,128)(2,1)}, bf16[384,96]{0,1:T(8,128)(2,1)}) async-done(((bf16[3,96,384]{2,1,0:T(8,128)(2,1)}, bf16[384,96]{0,1:T(8,128)(2,1)}, bf16[3,96,384]{2,1,0:T(8,128)(2,1)}, bf16[384,96]{0,1:T(8,128)(2,1)}), (bf16[3,96,384]{2,1,0:T(8,128)(2,1)}, bf16[384,96]{0,1:T(8,128)(2,1)}, ...) | async-done | bytes 589840 | tf_op jit(solution)/shard_map/psum | solution.py:95
  470.7 1.7 convert_multiply_fusion.2
  472.3 2.0 convert_multiply_fusion
  (89 shorter events, 3.7 us)
Async XLA Ops:
  7.2 33.5 %copy-start = (bf16[384,768]{1,0:T(8,128)(2,1)S(1)}, bf16[384,768]{1,0:T(8,128)(2,1)}, u32[]{:S(2)}) copy-start(bf16[384,768]{1,0:T(8,128)(2,1)} %param.14) | copy-start | bytes 1769476
  7.2 2.8 copy-start.1
  7.2 14.4 %copy-start.12 = (bf16[3,768,384]{2,1,0:T(8,128)(2,1)S(1)}, bf16[3,768,384]{2,1,0:T(8,128)(2,1)}, u32[]{:S(2)}) copy-start(bf16[3,768,384]{2,1,0:T(8,128)(2,1)} %param.11) | copy-start | bytes 5308420
  7.2 223.4 %reduce-scatter.11.cloned.1.call-start = ((), (), s32[]{:S(2)}) async-start(), calls=%async_computation.7 | async-start | bytes 1327104 | tf_op jit(solution)/shard_map/reduce_scatter | solution.py:92
  8.7 19.7 %collective-permute-start.2 = (bf16[384,768]{1,0:T(8,128)(2,1)S(1)}, bf16[384,768]{1,0:T(8,128)(2,1)S(1)}, u32[]{:S(2)}, u32[]{:S(2)}) collective-permute-start(bf16[384,768]{1,0:T(8,128)(2,1)S(1)} %get-tuple-element.28), channel_id=1, source_target_pairs={{24,0},{28,4},{25,1},{29,5},{26,2},{30,6},{27,3},{31,7}} | collective-permute-start | bytes 1769480 | tf_op jit(solution)/shard_map/ppermute | solution.py:15
  10.1 18.3 %collective-permute-start = (bf16[256,768]{1,0:T(8,128)(2,1)S(1)}, bf16[256,768]{1,0:T(8,128)(2,1)S(1)}, u32[]{:S(2)}, u32[]{:S(2)}) collective-permute-start(bf16[256,768]{1,0:T(8,128)(2,1)S(1)} %get-tuple-element.29), channel_id=1, source_target_pairs={{0,28},{1,29},{2,30},{3,31}} | collective-permute-start | bytes 1179656 | tf_op jit(solution)/shard_map/ppermute | solution.py:15
  18.9 19.5 %collective-permute-start.3 = (bf16[256,768]{1,0:T(8,128)(2,1)S(1)}, bf16[256,768]{1,0:T(8,128)(2,1)S(1)}, u32[]{:S(2)}, u32[]{:S(2)}) collective-permute-start(bf16[256,768]{1,0:T(8,128)(2,1)S(1)} %get-tuple-element.30), channel_id=1, source_target_pairs={{28,0},{29,1},{30,2},{31,3}} | collective-permute-start | bytes 1179656 | tf_op jit(solution)/shard_map/ppermute | solution.py:15
  20.2 19.4 %collective-permute-start.1 = (bf16[384,768]{1,0:T(8,128)(2,1)S(1)}, bf16[384,768]{1,0:T(8,128)(2,1)S(1)}, u32[]{:S(2)}, u32[]{:S(2)}) collective-permute-start(bf16[384,768]{1,0:T(8,128)(2,1)S(1)} %get-tuple-element.27), channel_id=1, source_target_pairs={{0,24},{4,28},{1,25},{5,29},{2,26},{6,30},{3,27},{7,31}} | collective-permute-start | bytes 1769480 | tf_op jit(solution)/shard_map/ppermute | solution.py:15
  38.5 1.2 copy-start.2
  39.7 1.0 copy-start.4
  39.7 1.0 copy-start.21
  39.7 1.0 copy-start.23
  40.6 0.9 copy-start.13
  41.6 11.3 %copy-start.10 = (bf16[3,768,384]{2,1,0:T(8,128)(2,1)S(1)}, bf16[3,768,384]{2,1,0:T(8,128)(2,1)}, u32[]{:S(2)}) copy-start(bf16[3,768,384]{2,1,0:T(8,128)(2,1)} %param.15) | copy-start | bytes 5308420
  41.7 25.2 %collective-permute-start.6 = (bf16[512,768]{1,0:T(8,128)(2,1)S(1)}, bf16[512,768]{1,0:T(8,128)(2,1)S(1)}, u32[]{:S(2)}, u32[]{:S(2)}) collective-permute-start(bf16[512,768]{1,0:T(8,128)(2,1)S(1)} %get-tuple-element.24), channel_id=1, source_target_pairs={{12,0},{16,4},{20,8},{24,12},{28,16},{13,1},{17,5},{21,9},{25,13},... | collective-permute-start | bytes 2359304 | tf_op jit(solution)/shard_map/ppermute | solution.py:15
  43.2 10.4 %collective-permute-start.4 = (bf16[128,768]{1,0:T(8,128)(2,1)S(1)}, bf16[128,768]{1,0:T(8,128)(2,1)S(1)}, u32[]{:S(2)}, u32[]{:S(2)}) collective-permute-start(bf16[128,768]{1,0:T(8,128)(2,1)S(1)} %get-tuple-element.25), channel_id=1, source_target_pairs={{0,16},{4,20},{8,24},{12,28},{1,17},{5,21},{9,25},{13,29},{2,18},{... | collective-permute-start | bytes 589832 | tf_op jit(solution)/shard_map/ppermute | solution.py:15
  48.2 38.8 %collective-permute-start.7 = (bf16[128,768]{1,0:T(8,128)(2,1)S(1)}, bf16[128,768]{1,0:T(8,128)(2,1)S(1)}, u32[]{:S(2)}, u32[]{:S(2)}) collective-permute-start(bf16[128,768]{1,0:T(8,128)(2,1)S(1)} %get-tuple-element.26), channel_id=1, source_target_pairs={{16,0},{20,4},{24,8},{28,12},{17,1},{21,5},{25,9},{29,13},{18,2},{... | collective-permute-start | bytes 589832 | tf_op jit(solution)/shard_map/ppermute | solution.py:15
  49.5 38.2 %collective-permute-start.5 = (bf16[512,768]{1,0:T(8,128)(2,1)S(1)}, bf16[512,768]{1,0:T(8,128)(2,1)S(1)}, u32[]{:S(2)}, u32[]{:S(2)}) collective-permute-start(bf16[512,768]{1,0:T(8,128)(2,1)S(1)} %get-tuple-element.23), channel_id=1, source_target_pairs={{0,12},{4,16},{8,20},{12,24},{16,28},{1,13},{5,17},{9,21},{13,25},... | collective-permute-start | bytes 2359304 | tf_op jit(solution)/shard_map/ppermute | solution.py:15
  87.8 1.0 copy-start.6
  87.8 1.9 copy-start.17
  87.8 1.9 copy-start.19
  87.8 1.9 copy-start.20
  88.8 0.9 copy-start.16
  91.7 178.5 %reduce-scatter.7.cloned.1.call-start = ((), (), s32[]{:S(2)}) async-start(), calls=%async_computation.5 | async-start | bytes 1327104 | tf_op jit(solution)/shard_map/reduce_scatter | solution.py:90
  91.8 2.9 copy-start.11
  94.6 57.6 %copy-start.8 = (bf16[640,384]{1,0:T(8,128)(2,1)}, bf16[640,384]{1,0:T(8,128)(2,1)S(1)}, u32[]{:S(2)}) copy-start(bf16[640,384]{1,0:T(8,128)(2,1)S(1)} %get-tuple-element.21) | copy-start | bytes 1474564
  95.4 56.8 %copy-start.18 = (bf16[1,640,768]{2,1,0:T(8,128)(2,1)S(1)}, bf16[1,640,768]{2,1,0:T(8,128)(2,1)}, u32[]{:S(2)}) copy-start(bf16[1,640,768]{2,1,0:T(8,128)(2,1)} %param.19) | copy-start | bytes 2949124
  95.4 56.8 %collective-permute-start.11 = (bf16[512,768]{1,0:T(8,128)(2,1)S(1)}, bf16[512,768]{1,0:T(8,128)(2,1)S(1)}, u32[]{:S(2)}, u32[]{:S(2)}) collective-permute-start(bf16[512,768]{1,0:T(8,128)(2,1)S(1)} %slice.125), channel_id=1, source_target_pairs={{0,12},{4,16},{8,20},{12,24},{16,28},{1,13},{5,17},{9,21},{13,25},... | collective-permute-start | bytes 2359304 | tf_op jit(solution)/shard_map/ppermute | solution.py:15
  99.0 53.2 %collective-permute-start.8 = (bf16[512,768]{1,0:T(8,128)(2,1)S(1)}, bf16[512,768]{1,0:T(8,128)(2,1)S(1)}, u32[]{:S(2)}, u32[]{:S(2)}) collective-permute-start(bf16[512,768]{1,0:T(8,128)(2,1)S(1)} %slice.122), channel_id=1, source_target_pairs={{12,0},{16,4},{20,8},{24,12},{28,16},{13,1},{17,5},{21,9},{25,13},... | collective-permute-start | bytes 2359304 | tf_op jit(solution)/shard_map/ppermute | solution.py:15
  100.3 53.6 %copy-start.14 = (f32[640,384]{1,0:T(8,128)S(1)}, f32[640,384]{1,0:T(8,128)}, u32[]{:S(2)}) copy-start(f32[640,384]{1,0:T(8,128)} %copy-done.13) | copy-start | bytes 2949124
  100.3 53.6 %copy-start.22 = (f32[384]{0:T(512)S(1)}, f32[384]{0:T(512)}, u32[]{:S(2)}) copy-start(f32[384]{0:T(512)} %param.13) | copy-start | bytes 4612
  100.3 53.6 %copy-start.24 = (f32[384]{0:T(512)S(1)}, f32[384]{0:T(512)}, u32[]{:S(2)}) copy-start(f32[384]{0:T(512)} %param.12) | copy-start | bytes 4612
  100.4 29.7 %collective-permute-start.10 = (bf16[128,768]{1,0:T(8,128)(2,1)S(1)}, bf16[128,768]{1,0:T(8,128)(2,1)S(1)}, u32[]{:S(2)}, u32[]{:S(2)}) collective-permute-start(bf16[128,768]{1,0:T(8,128)(2,1)S(1)} %slice.124), channel_id=1, source_target_pairs={{0,16},{4,20},{8,24},{12,28},{1,17},{5,21},{9,25},{13,29},{2,18},{... | collective-permute-start | bytes 589832 | tf_op jit(solution)/shard_map/ppermute | solution.py:15
  105.7 46.5 %collective-permute-start.9 = (bf16[128,768]{1,0:T(8,128)(2,1)S(1)}, bf16[128,768]{1,0:T(8,128)(2,1)S(1)}, u32[]{:S(2)}, u32[]{:S(2)}) collective-permute-start(bf16[128,768]{1,0:T(8,128)(2,1)S(1)} %slice.123), channel_id=1, source_target_pairs={{16,0},{20,4},{24,8},{28,12},{17,1},{21,5},{25,9},{29,13},{18,2},{... | collective-permute-start | bytes 589832 | tf_op jit(solution)/shard_map/ppermute | solution.py:15
  153.0 0.9 copy-start.25
  155.9 196.1 %reduce-scatter.9.cloned.1.call-start = ((), (), s32[]{:S(2)}) async-start(), calls=%async_computation.6 | async-start | bytes 3981312 | tf_op jit(solution)/shard_map/reduce_scatter | solution.py:91
  156.1 1.9 copy-start.9
  158.1 1.2 copy-start.7
  162.0 1.2 copy-start.15
  162.1 272.2 %reduce-scatter.5.cloned.1.call-start = ((), (), s32[]{:S(2)}) async-start(), calls=%async_computation.4 | async-start | bytes 3981312 | tf_op jit(solution)/shard_map/reduce_scatter | solution.py:89
  165.5 1.2 copy-start.3
  166.7 1.2 copy-start.5
  170.7 300.0 %all-reduce.4.cloned.1.call-start = ((), (), s32[]{:S(2)}) async-start(), calls=%async_computation.8 | async-start | bytes 1179648 | tf_op jit(solution)/shard_map/psum | solution.py:95
  172.6 263.4 %collective-permute-start.15 = (bf16[384,768]{1,0:T(8,128)(2,1)S(1)}, bf16[384,768]{1,0:T(8,128)(2,1)}, u32[]{:S(2)}, u32[]{:S(2)}) collective-permute-start(bf16[384,768]{1,0:T(8,128)(2,1)S(1)} %slice.129), channel_id=1, source_target_pairs={{0,24},{4,28},{1,25},{5,29},{2,26},{6,30},{3,27},{7,31}} | collective-permute-start | bytes 1769480 | tf_op jit(solution)/shard_map/ppermute | solution.py:15
  176.5 259.5 %collective-permute-start.12 = (bf16[384,768]{1,0:T(8,128)(2,1)S(1)}, bf16[384,768]{1,0:T(8,128)(2,1)}, u32[]{:S(2)}, u32[]{:S(2)}) collective-permute-start(bf16[384,768]{1,0:T(8,128)(2,1)S(1)} %slice.126), channel_id=1, source_target_pairs={{24,0},{28,4},{25,1},{29,5},{26,2},{30,6},{27,3},{31,7}} | collective-permute-start | bytes 1769480 | tf_op jit(solution)/shard_map/ppermute | solution.py:15
  177.9 258.1 %collective-permute-start.14 = (bf16[256,768]{1,0:T(8,128)(2,1)S(1)}, bf16[256,768]{1,0:T(8,128)(2,1)S(1)}, u32[]{:S(2)}, u32[]{:S(2)}) collective-permute-start(bf16[256,768]{1,0:T(8,128)(2,1)S(1)} %slice.128), channel_id=1, source_target_pairs={{0,28},{1,29},{2,30},{3,31}} | collective-permute-start | bytes 1179656 | tf_op jit(solution)/shard_map/ppermute | solution.py:15
  182.9 253.1 %collective-permute-start.13 = (bf16[256,768]{1,0:T(8,128)(2,1)S(1)}, bf16[256,768]{1,0:T(8,128)(2,1)}, u32[]{:S(2)}, u32[]{:S(2)}) collective-permute-start(bf16[256,768]{1,0:T(8,128)(2,1)S(1)} %slice.127), channel_id=1, source_target_pairs={{28,0},{29,1},{30,2},{31,3}} | collective-permute-start | bytes 1179656 | tf_op jit(solution)/shard_map/ppermute | solution.py:15
Sparse Core Ops, SparseCore 0:
  91.8 105.8 reduce-scatter.10
  201.2 68.9 reduce-scatter.6
  273.8 78.1 reduce-scatter.8
  355.5 78.6 reduce-scatter.4
  437.2 33.4 all-reduce.3
where the time goes:
time: 482 us; the launch traced here: 481 us
  waiting for transfers between devices  325 us (67%)
  blocking collectives  45.2 us (9%)
  starting transfers between devices  44.6 us (9%)
  matrix products  28.9 us (6%)
  other arithmetic  15.4 us (3%)
  between operations  14.5 us (3%)
  local copies, waits for them, and re-layouts  7.18 us (1%)
    ppermute x16, waiting for transfers between devices, passed_along(): lax.ppermute(value, axis, [(source, source + steps) for source in range(i...  95.2 us
    reduce_scatter x1, waiting for transfers between devices, settle_joint(): lax.psum_scatter(first_block_partials[0], 'seq', scatter_dimension=1, til...  80.5 us
    reduce_scatter x1, waiting for transfers between devices, settle_joint(): lax.psum_scatter(second_block_partials[0], 'seq', scatter_dimension=1, ti...  80.3 us
    psum x1, blocking collectives, settle_joint(): lax.psum((first_block_partials[2], first_block_partials[3], second_block_...  45.2 us
    ppermute x16, starting transfers between devices, passed_along(): lax.ppermute(value, axis, [(source, source + steps) for source in range(i...  44.2 us
    reduce_scatter x1, waiting for transfers between devices, settle_joint(): lax.psum_scatter(first_block_partials[1], 'seq', scatter_dimension=1, til...  38.1 us
    psum x1, waiting for transfers between devices, settle_joint(): lax.psum(parts[0].astype(jnp.bfloat16), 'chrom').astype(jnp.float32)  31.1 us
  transfers between devices with their start and end apart: 21, of which 11 were waited for; matrix products, arithmetic and copies ran while one was open for 8% of the time, Pallas kernels for 0%

commit v1 on v0

v1 whole, which is shorter than its diff:
```python
import math

import jax
import jax.numpy as jnp
from jax import lax
from jax.sharding import PartitionSpec as P

DILATION_FIRST = 4096
DILATION_SECOND = 2048
NORM_ROWS = 16


def smooth_value(normed):
    return normed * jax.nn.sigmoid(1.702 * normed)


def smooth_slope(normed):
    sigmoid_part = jax.nn.sigmoid(1.702 * normed)
    return sigmoid_part * (1.0 + 1.702 * normed * (1.0 - sigmoid_part))


def dot(left, right):
    return jnp.dot(left, right, preferred_element_type=jnp.float32)


def to_classes(field, group):
    count = lax.axis_size("seq")
    rows, width = field.shape
    pieces = field.reshape(rows // group, count, group // count, width).transpose(1, 0, 2, 3)
    return lax.all_to_all(pieces, "seq", 0, 0).reshape(rows, width)


def from_classes(field, group):
    count = lax.axis_size("seq")
    rows, width = field.shape
    pieces = field.reshape(count, rows // group, group // count, width)
    pieces = lax.all_to_all(pieces, "seq", 0, 0)
    return pieces.transpose(1, 0, 2, 3).reshape(rows, width)


def add_displaced(middle, from_before, from_after, shift):
    blank = jnp.zeros((shift, middle.shape[1]), middle.dtype)
    middle = middle + jnp.concatenate([blank, from_before], 0)
    return middle + jnp.concatenate([from_after, blank], 0)


def block_ahead(inputs, taps, scale, offset, shift):
    pre = add_displaced(
        dot(inputs, taps[1]), dot(inputs[:-shift], taps[0]), dot(inputs[shift:], taps[2]), shift
    )
    normed = scale * pre + offset
    return pre, normed, smooth_value(normed).astype(jnp.bfloat16)


def block_reverse(inputs, saved, taps, scale, point, upstream, shift):
    pre, normed, activated = saved
    grad_norm = dot(upstream, point.T) * smooth_slope(normed)
    grad_pre = (grad_norm * scale).astype(jnp.bfloat16)
    grads = jnp.stack(
        [
            dot(inputs[:-shift].T, grad_pre[shift:]),
            dot(inputs.T, grad_pre),
            dot(inputs[shift:].T, grad_pre[:-shift]),
            dot(upstream.T, activated),
        ]
    )
    norms = jnp.stack([jnp.sum(grad_norm * pre, 0), jnp.sum(grad_norm, 0)])
    grad_in = add_displaced(
        upstream.astype(jnp.float32) + dot(grad_pre, taps[1].T),
        dot(grad_pre[:-shift], taps[2].T),
        dot(grad_pre[shift:], taps[0].T),
        shift,
    )
    return grad_in.astype(jnp.bfloat16), grads, norms


def split_norms(norms):
    high = lax.reduce_precision(norms, 8, 7)
    parts = jnp.concatenate([high, norms - high], 0).astype(jnp.bfloat16)
    blank = jnp.zeros((NORM_ROWS - parts.shape[0], parts.shape[1]), jnp.bfloat16)
    return jnp.concatenate([parts, blank], 0)


def join_norms(rows):
    rows = rows.astype(jnp.float32)
    return rows[..., 0:2, :] + rows[..., 2:4, :]


def partners(axis, bit):
    return [(i, i ^ bit) for i in range(lax.axis_size(axis))]


def halve(grads, norms, where, axis, bit):
    width = grads.shape[-1]
    kept = lax.dynamic_index_in_dim(grads, where, 0, False)
    sent = lax.dynamic_index_in_dim(grads, 1 - where, 0, False)
    packed = jnp.concatenate([sent.reshape(-1, width), split_norms(norms)], 0)
    came = lax.ppermute(packed, axis, partners(axis, bit))
    other = came[:-NORM_ROWS].reshape(kept.shape)
    total = kept.astype(jnp.float32) + other.astype(jnp.float32)
    return total.astype(jnp.bfloat16), norms + join_norms(came[-NORM_ROWS:])


def settle(grads, norms, seq_first, factor):
    count = lax.axis_size("seq")
    chrom = lax.axis_index("chrom")
    core, across = chrom % 2, chrom // 2
    odd = lax.axis_index("seq") % 2
    kinds, channels, width = grads.shape
    share = channels // count
    grads = grads.astype(jnp.bfloat16).reshape(2, 2, count // 2, 2, share, width)
    grads, norms = halve(grads, norms, core, "chrom", 1)
    if seq_first:
        grads, norms = halve(jnp.moveaxis(grads, 2, 0), norms, odd, "seq", 1)
        grads, norms = halve(grads, norms, across, "chrom", 2)
    else:
        grads, norms = halve(grads, norms, across, "chrom", 2)
        grads, norms = halve(jnp.moveaxis(grads, 1, 0), norms, odd, "seq", 1)
    extra = jnp.broadcast_to(split_norms(norms)[None], (count // 2, NORM_ROWS, width))
    packed = jnp.concatenate([grads, extra], 1)
    groups = [[i for i in range(count) if i % 2 == parity] for parity in range(2)]
    came = lax.all_to_all(packed, "seq", 0, 0, axis_index_groups=groups)
    norms = jnp.sum(join_norms(came[:, share:]), 0)
    mine = jnp.sum(came[:, :share].astype(jnp.float32), 0).astype(jnp.bfloat16)
    other = lax.ppermute(mine, "chrom", partners("chrom", 2))
    pair = jnp.where(across == 0, jnp.stack([mine, other]), jnp.stack([other, mine]))
    other = lax.ppermute(pair, "chrom", partners("chrom", 1))
    full = jnp.where(core == 0, jnp.stack([pair, other]), jnp.stack([other, pair]))
    full = full.reshape(kinds, share, width).astype(jnp.float32) * factor
    norms = norms * factor
    return full[:3], full[3].T, norms[0], norms[1]


def body(
    features,
    first_dilated_taps,
    first_norm_scale,
    first_norm_offset,
    first_pointwise_weight,
    second_dilated_taps,
    second_norm_scale,
    second_norm_offset,
    second_pointwise_weight,
    cotangent,
):
    count = lax.axis_size("seq")
    rows = features.shape[1]
    factor = 1.0 / math.sqrt(rows * count * lax.axis_size("chrom"))
    group = math.gcd(rows, DILATION_SECOND)
    shift_first, shift_second = DILATION_FIRST // count, DILATION_SECOND // count

    inputs = to_classes(features[0], group)
    upstream = to_classes(cotangent[0], group)
    first = block_ahead(
        inputs, first_dilated_taps, first_norm_scale, first_norm_offset, shift_first
    )
    second_inputs = (inputs.astype(jnp.float32) + dot(first[2], first_pointwise_weight)).astype(
        jnp.bfloat16
    )
    second = block_ahead(
        second_inputs, second_dilated_taps, second_norm_scale, second_norm_offset, shift_second
    )
    upstream, grads_b, norms_b = block_reverse(
        second_inputs,
        second,
        second_dilated_taps,
        second_norm_scale,
        second_pointwise_weight,
        upstream,
        shift_second,
    )
    grad_input, grads_a, norms_a = block_reverse(
        inputs,
        first,
        first_dilated_taps,
        first_norm_scale,
        first_pointwise_weight,
        upstream,
        shift_first,
    )
    out_b = settle(grads_b, norms_b, False, factor)
    out_a = settle(grads_a, norms_a, True, factor)
    return (from_classes(grad_input, group)[None], *out_a, *out_b)


def solution(mesh):
    in_specs = (
        P("chrom", "seq", None),
        P(),
        P(),
        P(),
        P(),
        P(),
        P(),
        P(),
        P(),
        P("chrom", "seq", None),
    )
    out_specs = (
        P("chrom", "seq", None),
        P(None, "seq", None),
        P(None, "seq"),
        P(),
        P(),
        P(None, "seq", None),
        P(None, "seq"),
        P(),
        P(),
    )
    return jax.shard_map(body, mesh=mesh, in_specs=in_specs, out_specs=out_specs, check_vma=False)
```

time: 482 us -> 186 us (0.39)
  waiting for transfers between devices: 325 us -> 74.2 us
  blocking collectives: 45.2 us -> 0 us
  local copies, waits for them, and re-layouts: 7.18 us -> 38.6 us
  between operations: 14.5 us -> 1.29 us
  starting transfers between devices: 44.6 us -> 33.1 us
    reduce_scatter x4 -> x0, waiting for transfers between devices: 199 us -> none  [the longest x1 80.5 us: settle_joint(): lax.psum_scatter(first_block_partials[0], 'seq', scatter_dimension=1, til...]
    ppermute x16 -> x10, waiting for transfers between devices: 95.2 us -> 18.7 us  [the longest x6 17.1 us: halve(): came = lax.ppermute(packed, axis, partners(axis, bit))]
    all_to_all x0 -> x5, waiting for transfers between devices: none -> 55.5 us  [the longest x2 37.7 us: to_classes(): return lax.all_to_all(pieces, 'seq', 0, 0).reshape(rows, width)]
    psum x1 -> x0, blocking collectives: 45.2 us -> none  [settle_joint(): lax.psum((first_block_partials[2], first_block_partials[3], second_block_...]
    ppermute x16 -> x10, starting transfers between devices: 44.2 us -> 11.6 us  [the longest x6 7.06 us: halve(): came = lax.ppermute(packed, axis, partners(axis, bit))]
    psum x1 -> x0, waiting for transfers between devices: 31.1 us -> none  [settle_joint(): lax.psum(parts[0].astype(jnp.bfloat16), 'chrom').astype(jnp.float32)]
    all_to_all x0 -> x5, starting transfers between devices: none -> 21.4 us  [the longest x2 10.8 us: to_classes(): return lax.all_to_all(pieces, 'seq', 0, 0).reshape(rows, width)]
    concatenate x4 -> x2, local copies, waits for them, and re-layouts: 0.13 us -> 15.5 us  [halve(): packed = jnp.concatenate([sent.reshape(-1, width), split_norms(norms)], 0)]
  transfers between devices with their start and end apart: 21 -> 15, of which waited for: 11 -> 11; matrix products, arithmetic and copies ran while one was open for 8% -> 17% of each run, Pallas kernels for 0% -> 0%
where the time goes in v1:
time: 186 us; the launch traced here: 184 us
  waiting for transfers between devices  74.2 us (40%)
  local copies, waits for them, and re-layouts  38.6 us (21%)
  starting transfers between devices  33.1 us (18%)
  matrix products  25.2 us (14%)
  other arithmetic  11.7 us (6%)
    all_to_all x2, waiting for transfers between devices, to_classes(): return lax.all_to_all(pieces, 'seq', 0, 0).reshape(rows, width)  37.7 us
    dot_general x23, matrix products, dot(): return jnp.dot(left, right, preferred_element_type=jnp.float32)  25.2 us
    ppermute x6, waiting for transfers between devices, halve(): came = lax.ppermute(packed, axis, partners(axis, bit))  17.1 us
    concatenate x2, local copies, waits for them, and re-layouts, halve(): packed = jnp.concatenate([sent.reshape(-1, width), split_norms(norms)], 0)  15.5 us
    all_to_all x2, waiting for transfers between devices, settle(): came = lax.all_to_all(packed, 'seq', 0, 0, axis_index_groups=groups)  14.4 us
    all_to_all x2, starting transfers between devices, to_classes(): return lax.all_to_all(pieces, 'seq', 0, 0).reshape(rows, width)  10.8 us
    ppermute x6, starting transfers between devices, halve(): came = lax.ppermute(packed, axis, partners(axis, bit))  7.06 us
    all_to_all x2, starting transfers between devices, settle(): came = lax.all_to_all(packed, 'seq', 0, 0, axis_index_groups=groups)  6.91 us
  transfers between devices with their start and end apart: 15, of which 11 were waited for; matrix products, arithmetic and copies ran while one was open for 17% of the time, Pallas kernels for 0%

profile of v1, /device:TPU:0, one launch (start us, length us, event | category | flops | bytes accessed | tf_op | source)
XLA Modules:
  0.0 184.1 jit_solution(7995013151379327273)
XLA Ops:
  0.7 2.3 %copy.37 = bf16[5,8,16,768]{3,2,0,1:T(8,128)(2,1)} copy(bf16[5,8,16,768]{3,2,1,0:T(8,128)(2,1)} %bitcast.171) | data formatting | bytes 1966080 | tf_op jit(solution)/shard_map/reshape;squeeze | solution.py:29
  3.0 7.3 %all-to-all-start.1 = ((bf16[8,5,16,768]{3,2,1,0:T(8,128)(2,1)}), bf16[8,5,16,768]{3,2,1,0:T(8,128)(2,1)S(1)}, u32[]{:S(2)}, u32[]{:S(2)}) async-start(bf16[8,5,16,768]{3,2,1,0:T(8,128)(2,1)} %bitcast.138), calls=%async_computation.1 | async-start | bytes 1966080 | tf_op jit(solution)/shard_map/all_to_all | solution.py:30
  10.3 1.0 copy.38
  11.3 23.4 %all-to-all-done.1 = bf16[8,5,16,768]{3,2,1,0:T(8,128)(2,1)S(1)} async-done(((bf16[8,5,16,768]{3,2,1,0:T(8,128)(2,1)}), bf16[8,5,16,768]{3,2,1,0:T(8,128)(2,1)S(1)}, u32[]{:S(2)}, u32[]{:S(2)}) %all-to-all-start.1) | async-done | bytes 983072 | tf_op jit(solution)/shard_map/all_to_all | solution.py:30
  34.7 3.6 %all-to-all-start = ((bf16[8,5,16,768]{3,2,1,0:T(8,128)(2,1)}), bf16[8,5,16,768]{3,2,1,0:T(8,128)(2,1)S(1)}, u32[]{:S(2)}, u32[]{:S(2)}) async-start(bf16[8,5,16,768]{3,2,1,0:T(8,128)(2,1)} %bitcast.139), calls=%async_computation | async-start | bytes 1966080 | tf_op jit(solution)/shard_map/all_to_all | solution.py:30
  38.2 1.3 fusion.28
  39.6 1.3 fusion.32
  40.9 1.7 fusion.2
  42.7 0.9 copy-done.29
  43.6 2.1 %add_convert_fusion.2 = bf16[640,768]{1,0:T(8,128)(2,1)S(1)} fusion(bf16[640,768]{1,0:T(8,128)(2,1)} %bitcast.163, bf16[384,768]{1,0:T(8,128)(2,1)S(1)} %copy-done, f32[640,384]{1,0:T(8,128)S(1)} %fusion.2, f32[384]{0:T(512)S(1)} %copy-done.28, f32[384]{0:T(512)S(1)} %copy-done.27), kind=kOutput, calls=%fused_computation.8 | convolution fusion | flops 380928000 | bytes 3542016 | tf_op jit(solution)/shard_map/dot_general | solution.py:23
  46.8 1.6 fusion.3
  48.4 14.3 %all-to-all-done = bf16[8,5,16,768]{3,2,1,0:T(8,128)(2,1)S(1)} async-done(((bf16[8,5,16,768]{3,2,1,0:T(8,128)(2,1)}), bf16[8,5,16,768]{3,2,1,0:T(8,128)(2,1)S(1)}, u32[]{:S(2)}, u32[]{:S(2)}) %all-to-all-start) | async-done | bytes 983072 | tf_op jit(solution)/shard_map/all_to_all | solution.py:30
  62.8 3.0 %fusion.7 = bf16[1,768,384]{2,1,0:T(8,128)(2,1)} fusion(bf16[640,768]{1,0:T(8,128)(2,1)S(1)} %bitcast.149, f32[640,384]{1,0:T(8,128)} %fusion.3, f32[384]{0:T(512)S(1)} %copy-done.26, f32[384]{0:T(512)S(1)} %copy-done.25), kind=kOutput, calls=%fused_computation.26 | convolution fusion | flops 379748352 | bytes 2558976 | tf_op jit(solution)/shard_map/dot_general | solution.py:23
  65.8 1.0 multiply_reduce_fusion
  67.0 1.4 fusion.11
  68.4 1.4 fusion.10
  69.8 1.6 fusion.6
  72.4 0.7 add_convert_fusion.1
  73.6 1.6 multiply_reduce_fusion.1
  75.2 0.8 fusion.5
  77.3 0.7 fusion.4
  78.0 1.7 pad_maximum_fusion
  79.7 3.1 %copy.31 = bf16[4,768,384]{2,1,0:T(8,128)(2,1)S(1)} copy(bf16[4,768,384]{1,2,0:T(8,128)(2,1)} %pad_maximum_fusion) | data formatting | bytes 4718592 | tf_op jit(solution)/shard_map/stack | solution.py:59
  82.8 1.8 pad_maximum_fusion.1
  84.6 1.8 constant_dynamic-slice_fusion.2
  86.7 7.8 %concatenate.122 = bf16[1552,384]{1,0:T(8,128)(2,1)} concatenate(bf16[1536,384]{1,0:T(8,128)(2,1)} %bitcast.145, bf16[2,384]{1,0:T(2,128)(2,1)S(1)} %get-tuple-element.36, bf16[2,384]{1,0:T(2,128)(2,1)S(1)} %get-tuple-element.35, bf16[12,384]{1,0:T(8,128)(2,1)S(1)} %broadcast.68), dimensions={0} | concatenate | bytes 2383872 | tf_op jit(solution)/shard_map/concatenate | solution.py:97
  94.5 7.7 %concatenate.116 = bf16[1552,384]{1,0:T(8,128)(2,1)} concatenate(bf16[1536,384]{1,0:T(8,128)(2,1)} %bitcast.144, bf16[2,384]{1,0:T(2,128)(2,1)S(1)} %get-tuple-element.38, bf16[2,384]{1,0:T(2,128)(2,1)S(1)} %get-tuple-element.37, bf16[12,384]{1,0:T(8,128)(2,1)S(1)} %broadcast.68), dimensions={0} | concatenate | bytes 2383872 | tf_op jit(solution)/shard_map/concatenate | solution.py:97
  102.7 0.9 slice_convert_fusion.4
  103.6 1.9 %collective-permute-done = bf16[1552,384]{1,0:T(8,128)(2,1)} collective-permute-done((bf16[1552,384]{1,0:T(8,128)(2,1)}, bf16[1552,384]{1,0:T(8,128)(2,1)}, u32[]{:S(2)}, u32[]{:S(2)}) %collective-permute-start) | collective-permute-done | bytes 1191968 | tf_op jit(solution)/shard_map/ppermute | solution.py:98
  105.6 0.7 slice_convert_fusion.7
  106.3 1.4 slice.258
  108.0 1.8 slice.238
  110.4 1.2 pad_maximum_fusion.2
  111.6 1.5 collective-permute-start.6
  113.4 1.5 collective-permute-start.1
  115.2 1.6 add_convert_fusion
  116.9 3.7 %all-to-all-start.2 = ((bf16[8,5,16,768]{3,2,1,0:T(8,128)(2,1)}), bf16[8,5,16,768]{3,2,1,0:T(8,128)(2,1)S(1)}, u32[]{:S(2)}, u32[]{:S(2)}) async-start(bf16[8,5,16,768]{3,2,1,0:T(8,128)(2,1)} %bitcast.174), calls=%async_computation.2 | async-start | bytes 1966080 | tf_op jit(solution)/shard_map/all_to_all | solution.py:37
  120.6 7.1 %collective-permute-done.6 = bf16[784,384]{1,0:T(8,128)(2,1)S(1)} collective-permute-done((bf16[784,384]{1,0:T(8,128)(2,1)}, bf16[784,384]{1,0:T(8,128)(2,1)S(1)}, u32[]{:S(2)}, u32[]{:S(2)}) %collective-permute-start.6) | collective-permute-done | bytes 602144 | tf_op jit(solution)/shard_map/ppermute | solution.py:98
  127.7 0.8 copy-done.17
  128.7 7.0 %collective-permute-done.1 = bf16[784,384]{1,0:T(8,128)(2,1)} collective-permute-done((bf16[784,384]{1,0:T(8,128)(2,1)}, bf16[784,384]{1,0:T(8,128)(2,1)}, u32[]{:S(2)}, u32[]{:S(2)}) %collective-permute-start.1) | collective-permute-done | bytes 602144 | tf_op jit(solution)/shard_map/ppermute | solution.py:98
  135.7 1.1 slice.242
  137.0 0.7 slice_convert_fusion.3
  137.8 0.7 slice_convert_fusion.6
  138.6 0.9 pad_maximum_fusion.4
  139.4 2.3 %collective-permute-start.7 = (bf16[400,384]{1,0:T(8,128)(2,1)}, bf16[400,384]{1,0:T(8,128)(2,1)S(1)}, u32[]{:S(2)}, u32[]{:S(2)}) collective-permute-start(bf16[400,384]{1,0:T(8,128)(2,1)} %get-tuple-element.31), channel_id=1, source_target_pairs={{0,4},{4,0},{8,12},{12,8},{16,20},{20,16},{24,28},{28,24},{1,5},{5... | collective-permute-start | bytes 921608 | tf_op jit(solution)/shard_map/ppermute | solution.py:98
  141.7 3.4 %all-to-all-done.2 = bf16[8,5,16,768]{3,2,1,0:T(8,128)(2,1)S(1)} async-done(((bf16[8,5,16,768]{3,2,1,0:T(8,128)(2,1)}), bf16[8,5,16,768]{3,2,1,0:T(8,128)(2,1)S(1)}, u32[]{:S(2)}, u32[]{:S(2)}) %all-to-all-start.2) | async-done | bytes 983072 | tf_op jit(solution)/shard_map/all_to_all | solution.py:37
  145.1 1.0 copy.29
  146.1 1.3 collective-permute-start.2
  147.4 0.8 collective-permute-done.7
  148.2 0.7 copy-done.21
  148.9 1.0 slice.266
  150.0 0.8 pad_maximum_fusion.7
  150.8 3.5 %all-to-all-start.4 = ((bf16[4,112,384]{2,1,0:T(8,128)(2,1)}), bf16[4,112,384]{2,1,0:T(8,128)(2,1)S(1)}, u32[]{:S(2)}, u32[]{:S(2)}) async-start(bf16[4,112,384]{2,1,0:T(8,128)(2,1)} %pad_maximum_fusion.7), calls=%async_computation.4 | async-start | bytes 688128 | tf_op jit(solution)/shard_map/all_to_all | solution.py:122
  154.7 0.8 pad_maximum_fusion.6
  155.5 8.4 %all-to-all-done.4 = bf16[4,112,384]{2,1,0:T(8,128)(2,1)S(1)} async-done(((bf16[4,112,384]{2,1,0:T(8,128)(2,1)}), bf16[4,112,384]{2,1,0:T(8,128)(2,1)S(1)}, u32[]{:S(2)}, u32[]{:S(2)}) %all-to-all-start.4) | async-done | bytes 344096 | tf_op jit(solution)/shard_map/all_to_all | solution.py:122
  163.8 3.5 %all-to-all-start.3 = ((bf16[4,112,384]{2,1,0:T(8,128)(2,1)}), bf16[4,112,384]{2,1,0:T(8,128)(2,1)S(1)}, u32[]{:S(2)}, u32[]{:S(2)}) async-start(bf16[4,112,384]{2,1,0:T(8,128)(2,1)} %pad_maximum_fusion.6), calls=%async_computation.3 | async-start | bytes 688128 | tf_op jit(solution)/shard_map/all_to_all | solution.py:122
  167.4 2.2 %collective-permute-start.8 = (bf16[96,384]{1,0:T(8,128)(2,1)S(1)}, bf16[96,384]{1,0:T(8,128)(2,1)S(1)}, u32[]{:S(2)}, u32[]{:S(2)}) collective-permute-start(bf16[96,384]{1,0:T(8,128)(2,1)S(1)} %slice_reduce_fusion), channel_id=1, source_target_pairs={{0,2},{1,3},{2,0},{3,1},{4,6},{5,7},{6,4},{7,5},{8,10},{9,11},{10,... | collective-permute-start | bytes 221192 | tf_op jit(solution)/shard_map/ppermute | solution.py:125
  170.2 6.0 %all-to-all-done.3 = bf16[4,112,384]{2,1,0:T(8,128)(2,1)S(1)} async-done(((bf16[4,112,384]{2,1,0:T(8,128)(2,1)}), bf16[4,112,384]{2,1,0:T(8,128)(2,1)S(1)}, u32[]{:S(2)}, u32[]{:S(2)}) %all-to-all-start.3) | async-done | bytes 344096 | tf_op jit(solution)/shard_map/all_to_all | solution.py:122
  176.3 2.2 %collective-permute-start.3 = (bf16[96,384]{1,0:T(8,128)(2,1)S(1)}, bf16[96,384]{1,0:T(8,128)(2,1)S(1)}, u32[]{:S(2)}, u32[]{:S(2)}) collective-permute-start(bf16[96,384]{1,0:T(8,128)(2,1)S(1)} %slice_reduce_fusion.1), channel_id=1, source_target_pairs={{0,2},{1,3},{2,0},{3,1},{4,6},{5,7},{6,4},{7,5},{8,10},{9,11},{10,... | collective-permute-start | bytes 221192 | tf_op jit(solution)/shard_map/ppermute | solution.py:125
  179.2 1.6 collective-permute-done.3
  181.1 0.8 slice.271
  181.9 0.7 slice_bitcast_fusion
  182.7 0.7 slice_bitcast_fusion.1
  183.3 0.8 slice.251
  (129 shorter events, 9.1 us)
Async XLA Ops:
  0.6 43.0 %copy-start = (bf16[384,768]{1,0:T(8,128)(2,1)S(1)}, bf16[384,768]{1,0:T(8,128)(2,1)}, u32[]{:S(2)}) copy-start(bf16[384,768]{1,0:T(8,128)(2,1)} %param.14) | copy-start | bytes 1769476
  0.7 9.6 %copy-start.13 = (bf16[1,640,768]{2,1,0:T(8,128)(2,1)S(1)}, bf16[1,640,768]{2,1,0:T(8,128)(2,1)}, u32[]{:S(2)}) copy-start(bf16[1,640,768]{2,1,0:T(8,128)(2,1)} %param.19) | copy-start | bytes 2949124
  3.0 31.7 %all-to-all-start.1 = ((bf16[8,5,16,768]{3,2,1,0:T(8,128)(2,1)}), bf16[8,5,16,768]{3,2,1,0:T(8,128)(2,1)S(1)}, u32[]{:S(2)}, u32[]{:S(2)}) async-start(bf16[8,5,16,768]{3,2,1,0:T(8,128)(2,1)} %bitcast.138), calls=%async_computation.1 | async-start | bytes 1966080 | tf_op jit(solution)/shard_map/all_to_all | solution.py:30
  34.7 6.2 %copy-start.8 = (bf16[8,5,16,768]{3,2,1,0:T(8,128)(2,1)}, bf16[8,5,16,768]{3,2,1,0:T(8,128)(2,1)S(1)}, u32[]{:S(2)}) copy-start(bf16[8,5,16,768]{3,2,1,0:T(8,128)(2,1)S(1)} %all-to-all-done.1) | copy-start | bytes 2949124
  34.7 28.1 %all-to-all-start = ((bf16[8,5,16,768]{3,2,1,0:T(8,128)(2,1)}), bf16[8,5,16,768]{3,2,1,0:T(8,128)(2,1)S(1)}, u32[]{:S(2)}, u32[]{:S(2)}) async-start(bf16[8,5,16,768]{3,2,1,0:T(8,128)(2,1)} %bitcast.139), calls=%async_computation | async-start | bytes 1966080 | tf_op jit(solution)/shard_map/all_to_all | solution.py:30
  40.9 2.7 %copy-start.27 = (f32[384]{0:T(512)S(1)}, f32[384]{0:T(512)}, u32[]{:S(2)}) copy-start(f32[384]{0:T(512)} %param.12) | copy-start | bytes 4612
  40.9 2.7 %copy-start.28 = (f32[384]{0:T(512)S(1)}, f32[384]{0:T(512)}, u32[]{:S(2)}) copy-start(f32[384]{0:T(512)} %param.13) | copy-start | bytes 4612
  42.7 0.9 copy-start.29
  43.6 2.1 %copy-start.7 = (bf16[3,768,384]{2,1,0:T(8,128)(2,1)S(1)}, bf16[3,768,384]{2,1,0:T(8,128)(2,1)}, u32[]{:S(2)}) copy-start(bf16[3,768,384]{2,1,0:T(8,128)(2,1)} %param.15) | copy-start | bytes 5308420
  45.8 1.0 copy-start.10
  46.8 16.0 %copy-start.25 = (f32[384]{0:T(512)S(1)}, f32[384]{0:T(512)}, u32[]{:S(2)}) copy-start(f32[384]{0:T(512)} %param.16) | copy-start | bytes 4612
  46.8 16.0 %copy-start.26 = (f32[384]{0:T(512)S(1)}, f32[384]{0:T(512)}, u32[]{:S(2)}) copy-start(f32[384]{0:T(512)} %param.17) | copy-start | bytes 4612
  62.8 3.0 %copy-start.12 = (f32[640,384]{1,0:T(8,128)S(1)}, f32[640,384]{1,0:T(8,128)}, u32[]{:S(2)}) copy-start(f32[640,384]{1,0:T(8,128)} %fusion.3) | copy-start | bytes 2949124
  62.8 3.0 %copy-start.24 = (bf16[384,768]{1,0:T(8,128)(2,1)S(1)}, bf16[384,768]{1,0:T(8,128)(2,1)}, u32[]{:S(2)}) copy-start(bf16[384,768]{1,0:T(8,128)(2,1)} %param.18) | copy-start | bytes 1769476
  65.8 1.2 copy-start.11
  72.4 1.2 copy-start.30
  73.6 1.6 copy-start.14
  75.2 2.1 %copy-start.19 = (bf16[640,384]{1,0:T(8,128)(2,1)}, bf16[640,384]{1,0:T(8,128)(2,1)S(1)}, u32[]{:S(2)}) copy-start(bf16[640,384]{1,0:T(8,128)(2,1)S(1)} %get-tuple-element.30) | copy-start | bytes 1474564
  75.2 1.4 copy-start.9
  79.7 3.1 %copy-start.18 = (bf16[1,768,384]{2,1,0:T(8,128)(2,1)S(1)}, bf16[1,768,384]{2,1,0:T(8,128)(2,1)}, u32[]{:S(2)}) copy-start(bf16[1,768,384]{2,1,0:T(8,128)(2,1)} %fusion.7) | copy-start | bytes 1769476
  84.6 2.1 %copy-start.1 = (bf16[4,768,384]{2,1,0:T(8,128)(2,1)}, bf16[4,768,384]{2,1,0:T(8,128)(2,1)S(1)}, u32[]{:S(2)}) copy-start(bf16[4,768,384]{2,1,0:T(8,128)(2,1)S(1)} %pad_maximum_fusion.1) | copy-start | bytes 7077892
  86.7 7.8 %copy-start.23 = (f32[384]{0:T(512)S(1)}, f32[384]{0:T(512)}, u32[]{:S(2)}) copy-start(f32[384]{0:T(512)} %get-tuple-element.11) | copy-start | bytes 4612
  86.7 7.8 %copy-start.22 = (f32[384]{0:T(512)S(1)}, f32[384]{0:T(512)}, u32[]{:S(2)}) copy-start(f32[384]{0:T(512)} %get-tuple-element.12) | copy-start | bytes 4612
  94.5 8.3 %collective-permute-start.5 = (bf16[1552,384]{1,0:T(8,128)(2,1)}, bf16[1552,384]{1,0:T(8,128)(2,1)}, u32[]{:S(2)}, u32[]{:S(2)}) collective-permute-start(bf16[1552,384]{1,0:T(8,128)(2,1)} %concatenate.122), channel_id=1, source_target_pairs={{0,1},{1,0},{2,3},{3,2},{4,5},{5,4},{6,7},{7,6},{8,9},{9,8},{10,11... | collective-permute-start | bytes 3575816 | tf_op jit(solution)/shard_map/ppermute | solution.py:98
  102.2 3.3 %collective-permute-start = (bf16[1552,384]{1,0:T(8,128)(2,1)}, bf16[1552,384]{1,0:T(8,128)(2,1)}, u32[]{:S(2)}, u32[]{:S(2)}) collective-permute-start(bf16[1552,384]{1,0:T(8,128)(2,1)} %concatenate.116), channel_id=1, source_target_pairs={{0,1},{1,0},{2,3},{3,2},{4,5},{5,4},{6,7},{7,6},{8,9},{9,8},{10,11... | collective-permute-start | bytes 3575816 | tf_op jit(solution)/shard_map/ppermute | solution.py:98
  102.7 5.0 %copy-start.2 = (bf16[4,768,384]{2,1,0:T(8,128)(2,1)S(1)}, bf16[4,768,384]{2,1,0:T(8,128)(2,1)}, u32[]{:S(2)}) copy-start(bf16[4,768,384]{2,1,0:T(8,128)(2,1)} %copy-done.1) | copy-start | bytes 7077892
  108.0 2.2 %copy-start.5 = (bf16[2,4,2,96,384]{4,3,2,1,0:T(8,128)(2,1)}, bf16[2,4,2,96,384]{4,3,2,1,0:T(8,128)(2,1)S(1)}, u32[]{:S(2)}) copy-start(bf16[2,4,2,96,384]{4,3,2,1,0:T(8,128)(2,1)S(1)} %fusion) | copy-start | bytes 3538948
  110.2 1.4 copy-start.3
  110.3 2.8 %copy-start.16 = (bf16[3,768,384]{2,1,0:T(8,128)(2,1)S(1)}, bf16[3,768,384]{2,1,0:T(8,128)(2,1)}, u32[]{:S(2)}) copy-start(bf16[3,768,384]{2,1,0:T(8,128)(2,1)} %param.11) | copy-start | bytes 5308420
  110.3 2.8 %copy-start.20 = (bf16[640,384]{1,0:T(8,128)(2,1)S(1)}, bf16[640,384]{1,0:T(8,128)(2,1)}, u32[]{:S(2)}) copy-start(bf16[640,384]{1,0:T(8,128)(2,1)} %copy-done.19) | copy-start | bytes 1474564
  110.4 4.9 %copy-start.15 = (bf16[640,768]{1,0:T(8,128)(2,1)S(1)}, bf16[640,768]{1,0:T(8,128)(2,1)}, u32[]{:S(2)}) copy-start(bf16[640,768]{1,0:T(8,128)(2,1)} %copy-done.14) | copy-start | bytes 2949124
  111.6 16.1 %collective-permute-start.6 = (bf16[784,384]{1,0:T(8,128)(2,1)}, bf16[784,384]{1,0:T(8,128)(2,1)S(1)}, u32[]{:S(2)}, u32[]{:S(2)}) collective-permute-start(bf16[784,384]{1,0:T(8,128)(2,1)} %get-tuple-element.33), channel_id=1, source_target_pairs={{0,2},{1,3},{2,0},{3,1},{4,6},{5,7},{6,4},{7,5},{8,10},{9,11},{10,... | collective-permute-start | bytes 1806344 | tf_op jit(solution)/shard_map/ppermute | solution.py:98
  113.4 22.3 %collective-permute-start.1 = (bf16[784,384]{1,0:T(8,128)(2,1)}, bf16[784,384]{1,0:T(8,128)(2,1)}, u32[]{:S(2)}, u32[]{:S(2)}) collective-permute-start(bf16[784,384]{1,0:T(8,128)(2,1)} %get-tuple-element.34), channel_id=1, source_target_pairs={{0,4},{4,0},{8,12},{12,8},{16,20},{20,16},{24,28},{28,24},{1,5},{5... | collective-permute-start | bytes 1806344 | tf_op jit(solution)/shard_map/ppermute | solution.py:98
  116.9 11.6 %copy-start.6 = (bf16[2,4,2,96,384]{4,3,2,1,0:T(8,128)(2,1)S(1)}, bf16[2,4,2,96,384]{4,3,2,1,0:T(8,128)(2,1)}, u32[]{:S(2)}) copy-start(bf16[2,4,2,96,384]{4,3,2,1,0:T(8,128)(2,1)} %copy-done.5) | copy-start | bytes 3538948
  116.9 28.2 %all-to-all-start.2 = ((bf16[8,5,16,768]{3,2,1,0:T(8,128)(2,1)}), bf16[8,5,16,768]{3,2,1,0:T(8,128)(2,1)S(1)}, u32[]{:S(2)}, u32[]{:S(2)}) async-start(bf16[8,5,16,768]{3,2,1,0:T(8,128)(2,1)} %bitcast.174), calls=%async_computation.2 | async-start | bytes 1966080 | tf_op jit(solution)/shard_map/all_to_all | solution.py:37
  127.7 0.8 copy-start.17
  128.5 8.3 %copy-start.4 = (bf16[2,4,2,96,384]{4,3,2,1,0:T(8,128)(2,1)S(1)}, bf16[2,4,2,96,384]{4,3,2,1,0:T(8,128)(2,1)}, u32[]{:S(2)}) copy-start(bf16[2,4,2,96,384]{4,3,2,1,0:T(8,128)(2,1)} %copy-done.3) | copy-start | bytes 3538948
  139.4 8.8 %collective-permute-start.7 = (bf16[400,384]{1,0:T(8,128)(2,1)}, bf16[400,384]{1,0:T(8,128)(2,1)S(1)}, u32[]{:S(2)}, u32[]{:S(2)}) collective-permute-start(bf16[400,384]{1,0:T(8,128)(2,1)} %get-tuple-element.31), channel_id=1, source_target_pairs={{0,4},{4,0},{8,12},{12,8},{16,20},{20,16},{24,28},{28,24},{1,5},{5... | collective-permute-start | bytes 921608 | tf_op jit(solution)/shard_map/ppermute | solution.py:98
  146.1 8.3 %collective-permute-start.2 = (bf16[400,384]{1,0:T(8,128)(2,1)}, bf16[400,384]{1,0:T(8,128)(2,1)S(1)}, u32[]{:S(2)}, u32[]{:S(2)}) collective-permute-start(bf16[400,384]{1,0:T(8,128)(2,1)} %get-tuple-element.32), channel_id=1, source_target_pairs={{0,2},{1,3},{2,0},{3,1},{4,6},{5,7},{6,4},{7,5},{8,10},{9,11},{10,... | collective-permute-start | bytes 921608 | tf_op jit(solution)/shard_map/ppermute | solution.py:98
  148.2 0.7 copy-start.21
  150.8 13.0 %all-to-all-start.4 = ((bf16[4,112,384]{2,1,0:T(8,128)(2,1)}), bf16[4,112,384]{2,1,0:T(8,128)(2,1)S(1)}, u32[]{:S(2)}, u32[]{:S(2)}) async-start(bf16[4,112,384]{2,1,0:T(8,128)(2,1)} %pad_maximum_fusion.7), calls=%async_computation.4 | async-start | bytes 688128 | tf_op jit(solution)/shard_map/all_to_all | solution.py:122
  163.8 12.3 %all-to-all-start.3 = ((bf16[4,112,384]{2,1,0:T(8,128)(2,1)}), bf16[4,112,384]{2,1,0:T(8,128)(2,1)S(1)}, u32[]{:S(2)}, u32[]{:S(2)}) async-start(bf16[4,112,384]{2,1,0:T(8,128)(2,1)} %pad_maximum_fusion.6), calls=%async_computation.3 | async-start | bytes 688128 | tf_op jit(solution)/shard_map/all_to_all | solution.py:122
  167.4 11.8 %collective-permute-start.8 = (bf16[96,384]{1,0:T(8,128)(2,1)S(1)}, bf16[96,384]{1,0:T(8,128)(2,1)S(1)}, u32[]{:S(2)}, u32[]{:S(2)}) collective-permute-start(bf16[96,384]{1,0:T(8,128)(2,1)S(1)} %slice_reduce_fusion), channel_id=1, source_target_pairs={{0,2},{1,3},{2,0},{3,1},{4,6},{5,7},{6,4},{7,5},{8,10},{9,11},{10,... | collective-permute-start | bytes 221192 | tf_op jit(solution)/shard_map/ppermute | solution.py:125
  176.3 4.6 %collective-permute-start.3 = (bf16[96,384]{1,0:T(8,128)(2,1)S(1)}, bf16[96,384]{1,0:T(8,128)(2,1)S(1)}, u32[]{:S(2)}, u32[]{:S(2)}) collective-permute-start(bf16[96,384]{1,0:T(8,128)(2,1)S(1)} %slice_reduce_fusion.1), channel_id=1, source_target_pairs={{0,2},{1,3},{2,0},{3,1},{4,6},{5,7},{6,4},{7,5},{8,10},{9,11},{10,... | collective-permute-start | bytes 221192 | tf_op jit(solution)/shard_map/ppermute | solution.py:125
  179.1 1.9 %collective-permute-start.9 = (bf16[2,96,384]{2,1,0:T(8,128)(2,1)S(1)}, bf16[2,96,384]{2,1,0:T(8,128)(2,1)S(1)}, u32[]{:S(2)}, u32[]{:S(2)}) collective-permute-start(bf16[2,96,384]{2,1,0:T(8,128)(2,1)S(1)} %maximum_select_fusion.5), channel_id=1, source_target_pairs={{0,1},{1,0},{2,3},{3,2},{4,5},{5,4},{6,7},{7,6},{8,9},{9,8},{10,11... | collective-permute-start | bytes 442376 | tf_op jit(solution)/shard_map/ppermute | solution.py:127
  180.9 1.7 collective-permute-start.4

commit v2 on v1

v2 whole, which is shorter than its diff:
```python
import functools
import math

import jax
import jax.numpy as jnp
from jax import lax
from jax.experimental import pallas as pl
from jax.experimental.pallas import tpu as pltpu
from jax.sharding import PartitionSpec as P

DILATION_FIRST = 4096
DILATION_SECOND = 2048
NORM_ROWS = 16
VMEM_BYTES = 56 * 2**20
LATER_VMEM_BYTES = 24 * 2**20

IN_VMEM = pl.BlockSpec(memory_space=pltpu.VMEM)
ANYWHERE = pl.BlockSpec(memory_space=pl.ANY)


def smooth_value(normed):
    return normed * jax.nn.sigmoid(1.702 * normed)


def smooth_slope(normed):
    sigmoid_part = jax.nn.sigmoid(1.702 * normed)
    return sigmoid_part * (1.0 + 1.702 * normed * (1.0 - sigmoid_part))


def dot(left, right):
    return jnp.dot(left, right, preferred_element_type=jnp.float32)


def across(left, right):
    return lax.dot_general(left, right, (((1,), (1,)), ((), ())), preferred_element_type=jnp.float32)


def over_rows(left, right):
    return lax.dot_general(left, right, (((0,), (0,)), ((), ())), preferred_element_type=jnp.float32)


def pick(values, index):
    chosen = jnp.int32(int(values[0]))
    for at, value in enumerate(values[1:], 1):
        chosen = jnp.where(index == at, jnp.int32(int(value)), chosen)
    return chosen


class Routes:
    def __init__(self, rows, count):
        self.unit = math.gcd(rows, DILATION_SECOND // count)
        self.units = rows // self.unit
        same = math.gcd(self.units, count)
        permutes = []
        for j in range(self.units):
            permute = {}
            for i in range(count):
                slot = j // same * same + (j + i // (count // same)) % same
                whole = self.units * i + slot
                permute[i] = slot, whole % count, whole // count
            permutes.append(permute)
        stay, moved = self.without_stays(permutes, count)
        self.stay = stay
        self.permutes = permutes if stay is None else moved
        for permute in self.permutes:
            assert len({target for _, target, _ in permute.values()}) == count

    @staticmethod
    def without_stays(permutes, count):
        stay, moved = {}, []
        for permute in permutes:
            rest = {}
            for i, (slot, target, place) in permute.items():
                if target == i and i not in stay:
                    stay[i] = slot, place
                else:
                    rest[i] = slot, target, place
            for other in moved:
                targets = {target for _, target, _ in other.values()}
                if not (other.keys() & rest.keys()) and not any(t in targets for _, t, _ in rest.values()):
                    other.update(rest)
                    break
            else:
                moved.append(rest)
        if len(stay) != count or any(len(permute) != count for permute in moved):
            return None, None
        return stay, moved

    def slots(self):
        count = len(self.permutes[0])
        found = [[permute[i][0] for i in range(count)] for permute in self.permutes]
        return found if self.stay is None else found + [[self.stay[i][0] for i in range(count)]]

    def places(self):
        count = len(self.permutes[0])
        found = []
        for permute in self.permutes:
            by_target = {target: place for _, target, place in permute.values()}
            found.append([by_target[k] for k in range(count)])
        return found if self.stay is None else found + [[self.stay[k][1] for k in range(count)]]

    def out(self, field):
        mine = lax.axis_index("seq")
        came = []
        for permute in self.permutes:
            slots = [permute[i][0] for i in range(len(permute))]
            if len(set(slots)) == 1:
                part = field[slots[0] * self.unit : (slots[0] + 1) * self.unit]
            else:
                part = lax.dynamic_slice_in_dim(field, jnp.asarray(slots)[mine] * self.unit, self.unit, 0)
            came.append(lax.ppermute(part, "seq", [(i, t) for i, (_, t, _) in permute.items()]))
        return came

    def back(self, parts):
        return [
            lax.ppermute(part, "seq", [(t, i) for i, (_, t, _) in permute.items()])
            for part, permute in zip(parts, self.permutes)
        ]


def fetch(source, target, sem):
    copy = pltpu.make_async_copy(source, target, sem)
    copy.start()
    return copy


def unit_at(ref, place, unit):
    return ref.at[pl.ds(pl.multiple_of(place * unit, unit), unit), :]


def fetch_units(routes, field, came, target, sems, first):
    mine = lax.axis_index("seq")
    places, slots, unit = routes.places(), routes.slots(), routes.unit
    copies = []
    for j, place in enumerate(places):
        source = came[j] if j < len(came) else unit_at(field, pick(slots[j], mine), unit)
        copies.append(fetch(source, unit_at(target, pick(place, mine), unit), sems.at[first + j]))
    return copies


def wait_all(copies):
    for copy in copies:
        copy.wait()


def padded(share):
    return -(-share // 16) * 16


def row_parts(rows):
    step = math.gcd(rows, 128)
    return rows // step, step


def ahead_kernel(routes, shifts, *refs):
    steps, units = len(routes.permutes), routes.units
    field, slots, refs = refs[0], refs[1 : 1 + steps], refs[1 + steps :]
    taps_hbm, point_hbm, taps_b_hbm = refs[:3]
    scale_a, offset_a, scale_b, offset_b = refs[3:7]
    outs, refs = refs[7:12], refs[12:]
    inputs, taps, point, taps_b, pre_a, act_a, second, pre_b, act_b, sems = refs
    rows, width = pre_a.shape
    load_taps = fetch(taps_hbm, taps, sems.at[units])
    came = fetch_units(routes, field, slots, inputs, sems, 0)
    load_point = fetch(point_hbm, point, sems.at[units + 1])
    load_taps_b = fetch(taps_b_hbm, taps_b, sems.at[units + 2])

    def block(field, taps, scale_ref, offset_ref, pre, act, shift):
        pre[...] = dot(field[...], taps[1])
        pre[shift:, :] += dot(field[:-shift, :], taps[0])
        pre[:-shift, :] += dot(field[shift:, :], taps[2])
        scale, offset = scale_ref[...][None, :], offset_ref[...][None, :]
        steps, step = row_parts(rows)

        @pl.loop(0, steps)
        def _(at):
            part = pl.ds(pl.multiple_of(at * step, step), step)
            act[part, :] = smooth_value(scale * pre[part, :] + offset).astype(jnp.bfloat16)

    def leave(index, source):
        return fetch(source, outs[index], sems.at[units + 3 + index])

    wait_all(came)
    load_taps.wait()
    block(inputs, taps, scale_a, offset_a, pre_a, act_a, shifts[0])
    left = [leave(0, pre_a), leave(1, act_a)]
    load_point.wait()
    second[...] = (inputs[...].astype(jnp.float32) + dot(act_a[...], point[...])).astype(jnp.bfloat16)
    left += [leave(2, second)]
    load_taps_b.wait()
    block(second, taps_b, scale_b, offset_b, pre_b, act_b, shifts[1])
    wait_all(left + [leave(3, pre_b), leave(4, act_b)])


def ahead(routes, field, slots, first, second, shifts, rows):
    (taps, scale_a, offset_a, point), (taps_b, scale_b, offset_b, _) = first, second
    channels, width = taps.shape[1:]
    units = routes.units
    shape = jax.ShapeDtypeStruct
    thin, wide = (rows, width), (rows, channels)
    return pl.pallas_call(
        functools.partial(ahead_kernel, routes, shifts),
        out_shape=(
            shape(thin, jnp.float32),
            shape(thin, jnp.bfloat16),
            shape(wide, jnp.bfloat16),
            shape(thin, jnp.float32),
            shape(thin, jnp.bfloat16),
        ),
        in_specs=[ANYWHERE] * (1 + len(slots) + 3) + [IN_VMEM] * 4,
        out_specs=[ANYWHERE] * 5,
        scratch_shapes=[
            pltpu.VMEM(wide, jnp.bfloat16),
            pltpu.VMEM(taps.shape, jnp.bfloat16),
            pltpu.VMEM(point.shape, jnp.bfloat16),
            pltpu.VMEM(taps.shape, jnp.bfloat16),
            pltpu.VMEM(thin, jnp.float32),
            pltpu.VMEM(thin, jnp.bfloat16),
            pltpu.VMEM(wide, jnp.bfloat16),
            pltpu.VMEM(thin, jnp.float32),
            pltpu.VMEM(thin, jnp.bfloat16),
            pltpu.SemaphoreType.DMA((units + 8,)),
        ],
        compiler_params=pltpu.CompilerParams(vmem_limit_bytes=VMEM_BYTES),
        cost_estimate=pl.CostEstimate(
            flops=2 * width * channels * 5 * rows,
            bytes_accessed=10 * 2**20,
            transcendentals=2 * rows * width,
        ),
    )(field, *slots, taps, point, taps_b, scale_a, offset_a, scale_b, offset_b)


def split_norms(norms):
    high = norms.astype(jnp.bfloat16)
    low = (norms - high.astype(jnp.float32)).astype(jnp.bfloat16)
    blank = jnp.zeros((NORM_ROWS - 2 * norms.shape[0], norms.shape[1]), jnp.bfloat16)
    return jnp.concatenate([high, low, blank], 0)


def join_norms(rows, count):
    rows = rows.astype(jnp.float32)
    return rows[:count] + rows[count : 2 * count]


def reverse_kernel(routes, count, shifts, *refs):
    steps, units, unit = len(routes.permutes), routes.units, routes.unit
    u_field, u_slots, refs = refs[0], refs[1 : 1 + steps], refs[1 + steps :]
    g_field, g_slots, refs = refs[0], refs[1 : 1 + steps], refs[1 + steps :]
    second_hbm, pre_b_hbm, act_b_hbm, pre_a_hbm, act_a_hbm = refs[:5]
    taps_b_hbm, point_b_hbm, taps_a_hbm, point_a_hbm = refs[5:9]
    scale_a, offset_a, scale_b, offset_b = refs[9:13]
    places = routes.places()
    grad_slots, refs = refs[13 : 13 + len(places)], refs[13 + len(places) :]
    kept_b, sent_b, kept_a, sent_a, norms_ref = refs[:5]
    u_a, g_a, u_b, g_b, pre_a, pre_b, act_a, act_b, taps_a, taps_b, point_a, point_b = refs[5:17]
    grad_act, grad_pre, product, staged, wide, sums, norm_rows, sems, out_sems = refs[17:]
    rows, width = pre_a.shape
    channels = u_a.shape[1]
    share = channels // count
    pad = padded(share)
    half = count // 2 * pad
    seq, chrom = lax.axis_index("seq"), lax.axis_index("chrom")
    core, side, odd, rest = chrom % 2, chrom // 2, seq % 2, seq // 2

    def load(at, source, target):
        return fetch(source, target, sems.at[2 * units + at])

    came_g = fetch_units(routes, g_field, g_slots, g_b, sems, 0)
    loads_b = [load(0, point_b_hbm, point_b), load(1, pre_b_hbm, pre_b)]
    came_second = [load(2, second_hbm, u_b)]
    loads_b += [load(3, act_b_hbm, act_b), load(4, taps_b_hbm, taps_b)]
    loads_a = [load(5, point_a_hbm, point_a), load(6, pre_a_hbm, pre_a)]
    came_u = fetch_units(routes, u_field, u_slots, u_a, sems, units)
    loads_a += [load(7, act_a_hbm, act_a), load(8, taps_a_hbm, taps_a)]

    def block(index, u, g, pre, act, taps, point, loads, came, scale_ref, offset_ref, shift, kept, sent):
        scale, offset = scale_ref[...][None, :], offset_ref[...][None, :]
        loads[0].wait()
        grad_act[...] = across(g[...], point[...])
        sums[...] = jnp.zeros_like(sums)
        steps, step = row_parts(rows)
        loads[1].wait()

        @pl.loop(0, steps)
        def _(at):
            part = pl.ds(pl.multiple_of(at * step, step), step)
            value = pre[part, :]
            normed = scale * value + offset
            grad_norm = grad_act[part, :] * smooth_slope(normed)
            grad_pre[part, :] = (grad_norm * scale).astype(jnp.bfloat16)
            sums[0] += jnp.sum((grad_norm * value).reshape(step // 8, 8, width), 0)
            sums[1] += jnp.sum(grad_norm.reshape(step // 8, 8, width), 0)

        norms = jnp.sum(sums[...], 1)
        norms_ref[2 * index : 2 * index + 2, :] = norms
        norm_rows[index] = split_norms(norms)
        tail = fetch(norm_rows.at[index], sent.at[pl.ds(4 * half, NORM_ROWS)], out_sems.at[index, 8])

        def copies(kind, target):
            source = staged.at[4 * index + kind]
            slot = (kind % 2) ^ side
            for part in range(2):
                place = (slot * 2 + part if index == 1 else part * 2 + slot) * half
                yield pltpu.make_async_copy(
                    source.at[pl.ds(part * half, half)],
                    target.at[pl.ds(pl.multiple_of(place, half), half)],
                    out_sems.at[index, 2 * kind + part],
                )

        def both(kind, act_on):
            @pl.when(core == kind // 2)
            def _():
                for copy in copies(kind, kept):
                    act_on(copy)

            @pl.when(core != kind // 2)
            def _():
                for copy in copies(kind, sent):
                    act_on(copy)

        def settle_one(kind, value):
            product[:channels, :] = value
            for at in range(count):
                place = ((at % 2) ^ odd) * half + ((at // 2) ^ rest) * pad
                staged[4 * index + kind, pl.ds(pl.multiple_of(place, pad), pad), :] = product[
                    at * share : at * share + pad, :
                ].astype(jnp.bfloat16)
            both(kind, lambda copy: copy.start())

        wait_all(came)
        settle_one(0, over_rows(u[:-shift, :], grad_pre[shift:, :]))
        settle_one(1, over_rows(u[...], grad_pre[...]))
        settle_one(2, over_rows(u[shift:, :], grad_pre[:-shift, :]))
        loads[2].wait()
        settle_one(3, over_rows(g[...], act[...]))
        loads[3].wait()
        wide[...] = across(grad_pre[...], taps[1])
        wide[:-shift, :] += across(grad_pre[shift:, :], taps[0])
        wide[shift:, :] += across(grad_pre[:-shift, :], taps[2])
        g_a[...] = (wide[...] + g[...].astype(jnp.float32)).astype(jnp.bfloat16)

        def finish():
            tail.wait()
            for kind in range(4):
                both(kind, lambda copy: copy.wait())

        return finish

    wait_all(came_g)
    finish_b = block(
        1, u_b, g_b, pre_b, act_b, taps_b, point_b, loads_b, came_second, scale_b, offset_b, shifts[1], kept_b, sent_b
    )
    finish_a = block(
        0, u_a, g_a, pre_a, act_a, taps_a, point_a, loads_a, came_u, scale_a, offset_a, shifts[0], kept_a, sent_a
    )
    grads = [
        fetch(unit_at(g_a, pick(places[j], seq), unit), slot, sems.at[j])
        for j, slot in enumerate(grad_slots)
    ]
    finish_b()
    finish_a()
    wait_all(grads)


def reverse(routes, u_field, u_slots, g_field, g_slots, saved, first, second, shifts, rows):
    (taps_a, scale_a, offset_a, point_a), (taps_b, scale_b, offset_b, point_b) = first, second
    pre_a, act_a, second_inputs, pre_b, act_b = saved
    channels, width = taps_a.shape[1:]
    units, count = routes.units, lax.axis_size("seq")
    went = len(routes.places())
    shape = jax.ShapeDtypeStruct
    thin, wide = (rows, width), (rows, channels)
    pad = padded(channels // count)
    kept = shape((2 * count * pad, width), jnp.bfloat16)
    sent = shape((2 * count * pad + NORM_ROWS, width), jnp.bfloat16)
    vmem = pltpu.VMEM
    outs = pl.pallas_call(
        functools.partial(reverse_kernel, routes, count, shifts),
        out_shape=(
            *[shape((routes.unit, channels), jnp.bfloat16)] * went,
            kept,
            sent,
            kept,
            sent,
            shape((4, width), jnp.float32),
        ),
        in_specs=[ANYWHERE] * (2 + len(u_slots) + len(g_slots) + 9) + [IN_VMEM] * 4,
        out_specs=[ANYWHERE] * (went + 4) + [IN_VMEM],
        scratch_shapes=[
            *[vmem(wide, jnp.bfloat16)] * 4,
            *[vmem(thin, jnp.float32)] * 2,
            *[vmem(thin, jnp.bfloat16)] * 2,
            *[vmem(taps_a.shape, jnp.bfloat16)] * 2,
            *[vmem(point_a.shape, jnp.bfloat16)] * 2,
            vmem(thin, jnp.float32),
            vmem(thin, jnp.bfloat16),
            vmem((channels + pad - channels // count, width), jnp.float32),
            vmem((8, count * pad, width), jnp.bfloat16),
            vmem(wide, jnp.float32),
            vmem((2, 8, width), jnp.float32),
            vmem((2, NORM_ROWS, width), jnp.bfloat16),
            pltpu.SemaphoreType.DMA((2 * units + 9,)),
            pltpu.SemaphoreType.DMA((2, 9)),
        ],
        compiler_params=pltpu.CompilerParams(vmem_limit_bytes=VMEM_BYTES),
        cost_estimate=pl.CostEstimate(
            flops=2 * width * channels * 11 * rows,
            bytes_accessed=18 * 2**20,
            transcendentals=2 * rows * width,
        ),
    )(
        u_field, *u_slots, g_field, *g_slots, second_inputs, pre_b, act_b, pre_a, act_a,
        taps_b, point_b, taps_a, point_a,
        scale_a, offset_a, scale_b, offset_b,
    )
    return outs[:went], outs[went : went + 4], outs[went + 4]


def gather_kernel(routes, *refs):
    parts, out = refs[:-1], refs[-1]
    mine, unit = lax.axis_index("seq"), routes.unit
    for slots, part in zip(routes.slots(), parts):
        out[pl.ds(pl.multiple_of(pick(slots, mine) * unit, unit), unit), :] = part[...]


def gather_units(routes, parts):
    unit, channels = parts[0].shape
    return pl.pallas_call(
        functools.partial(gather_kernel, routes),
        out_shape=jax.ShapeDtypeStruct((routes.units * unit, channels), jnp.bfloat16),
        in_specs=[IN_VMEM] * len(parts),
        out_specs=IN_VMEM,
        cost_estimate=pl.CostEstimate(flops=0, bytes_accessed=2**21, transcendentals=0),
    )(*parts)


def trade(value, axis, bits):
    return lax.ppermute(value, axis, [(i, i ^ bits) for i in range(lax.axis_size(axis))])


def rows_at(block, index, width):
    return pl.BlockSpec((block, width), lambda step: (index, 0))


def summed(parts):
    total = parts[0][...].astype(jnp.float32)
    for part in parts[1:]:
        total = total + part[...].astype(jnp.float32)
    return total


def combine_kernel(number, norms_in, *refs):
    outs = refs[2 * number + 2 : 2 * number + 4]
    norms_out = refs[2 * number + 4]
    for block in range(2):
        parts = refs[block * (number + 1) : (block + 1) * (number + 1)]
        size = parts[0].shape[0]
        norms = norms_in[2 * block : 2 * block + 2, :] + join_norms(parts[number][...], 2)
        norms_out[2 * block : 2 * block + 2, :] = norms
        outs[block][:size, :] = summed(parts[:number]).astype(jnp.bfloat16)
        outs[block][size:, :] = split_norms(norms)


def combine(norms, parts_a, parts_b, waited, vmem_bytes):
    number, width = len(parts_a), norms.shape[1]
    size = (parts_a[-1].shape[0] - NORM_ROWS) // 2
    specs = [rows_at(size, 1, width)] * number + [rows_at(NORM_ROWS, 2 * size // NORM_ROWS, width)]
    shape = jax.ShapeDtypeStruct
    payload = shape((size + NORM_ROWS, width), jnp.bfloat16)
    whole = pl.BlockSpec(payload.shape, lambda step: (0, 0))
    small = pl.BlockSpec(norms.shape, lambda step: (0, 0))

    def kernel(*refs):
        combine_kernel(number, refs[0], *refs[1 : 2 * number + 3], *refs[2 * number + 3 + len(waited) :])

    return pl.pallas_call(
        kernel,
        grid=(1,),
        out_shape=(payload, payload, shape(norms.shape, jnp.float32)),
        in_specs=[small] + specs * 2 + [ANYWHERE] * len(waited),
        out_specs=(whole, whole, small),
        compiler_params=pltpu.CompilerParams(vmem_limit_bytes=vmem_bytes),
        cost_estimate=pl.CostEstimate(flops=0, bytes_accessed=8 * size * width * number, transcendentals=0),
    )(norms, *parts_a, parts_a[-1], *parts_b, parts_b[-1], *waited)


def pieces_kernel(number, norms_in, *refs):
    parts, refs = refs[: 2 * number + 2], refs[2 * number + 2 :]
    mine, norms_out, payloads, total = refs[0], refs[1], refs[2:-1], refs[-1]
    pad = mine.shape[0] // 2
    norms = []
    for block in range(2):
        own = parts[block * (number + 1) : (block + 1) * (number + 1)]
        norms.append(norms_in[2 * block : 2 * block + 2, :] + join_norms(own[number][...], 2))
        total[...] = summed(own[:number])
        mine[block * pad : (block + 1) * pad, :] = total[:pad, :]
        for at, payload in enumerate(payloads, 1):
            payload[block * pad : (block + 1) * pad, :] = total[
                at * pad : (at + 1) * pad, :
            ].astype(jnp.bfloat16)
    norms = jnp.concatenate(norms, 0)
    norms_out[...] = norms
    for payload in payloads:
        payload[2 * pad :, :] = split_norms(norms)


def cut_pieces(norms, parts_a, parts_b, share):
    number, width = len(parts_a), norms.shape[1]
    size = parts_a[-1].shape[0] - NORM_ROWS
    pad = padded(share)
    shape = jax.ShapeDtypeStruct
    specs = [rows_at(size, 0, width)] * number + [rows_at(NORM_ROWS, size // NORM_ROWS, width)]
    outs = (
        shape((2 * pad, width), jnp.float32),
        shape(norms.shape, jnp.float32),
        *[shape((2 * pad + NORM_ROWS, width), jnp.bfloat16)] * (size // pad - 1),
    )
    return pl.pallas_call(
        functools.partial(pieces_kernel, number),
        grid=(1,),
        out_shape=outs,
        in_specs=[pl.BlockSpec(norms.shape, lambda step: (0, 0))] + specs * 2,
        out_specs=[pl.BlockSpec(out.shape, lambda step: (0, 0)) for out in outs],
        scratch_shapes=[pltpu.VMEM((size, width), jnp.float32)],
        compiler_params=pltpu.CompilerParams(vmem_limit_bytes=LATER_VMEM_BYTES),
        cost_estimate=pl.CostEstimate(flops=0, bytes_accessed=8 * size * width * number, transcendentals=0),
    )(norms, *parts_a, parts_a[-1], *parts_b, parts_b[-1])


def total_kernel(norms_in, mine, *refs):
    came, out, norms_out = refs[:-2], refs[-2], refs[-1]
    rows = mine.shape[0]
    total, norms = mine[...], norms_in[...]
    for payload in came:
        total = total + payload[:rows, :].astype(jnp.float32)
        norms = norms + join_norms(payload[rows:, :], norms.shape[0])
    out[...] = total.astype(jnp.bfloat16)
    norms_out[...] = norms


def add_pieces(norms, mine, came):
    return pl.pallas_call(
        total_kernel,
        out_shape=(
            jax.ShapeDtypeStruct(mine.shape, jnp.bfloat16),
            jax.ShapeDtypeStruct(norms.shape, jnp.float32),
        ),
        in_specs=[IN_VMEM] * (2 + len(came)),
        out_specs=[IN_VMEM] * 2,
        compiler_params=pltpu.CompilerParams(vmem_limit_bytes=LATER_VMEM_BYTES),
        cost_estimate=pl.CostEstimate(flops=0, bytes_accessed=2**20, transcendentals=0),
    )(norms, mine, *came)


def finish_kernel(factor, share, norms_in, *refs):
    pieces, outs, norms_out = refs[:4], refs[4:8], refs[8:]
    chrom = lax.axis_index("chrom")
    mine = chrom % 2 * 2 + chrom // 2
    for row, out in enumerate(norms_out):
        out[...] = norms_in[row, :] * factor
    pad = pieces[0].shape[0] // 2
    for block in range(2):
        taps, point = outs[2 * block : 2 * block + 2]
        for bits in range(4):
            kind = mine ^ bits
            value = pieces[bits][block * pad : block * pad + share, :].astype(jnp.float32) * factor

            @pl.when(kind < 3)
            def _():
                taps[jnp.minimum(kind, 2)] = value

            @pl.when(kind == 3)
            def _():
                point[...] = value


def finish(norms, pieces, share, factor):
    width = norms.shape[1]
    shape = jax.ShapeDtypeStruct
    pair = [shape((3, share, width), jnp.float32), shape((share, width), jnp.float32)]
    return pl.pallas_call(
        functools.partial(finish_kernel, factor, share),
        out_shape=(*pair, *pair, *[shape((width,), jnp.float32)] * 4),
        in_specs=[IN_VMEM] * 5,
        out_specs=[IN_VMEM] * 8,
        cost_estimate=pl.CostEstimate(flops=0, bytes_accessed=2 * 2**20, transcendentals=0),
    )(norms, *pieces)


def settle(halves, norms, waited, share, factor):
    kept_b, sent_b, kept_a, sent_a = halves
    parts_b, parts_a = [kept_b, trade(sent_b, "chrom", 1)], [kept_a, trade(sent_a, "chrom", 1)]
    sent_a, sent_b, norms = combine(norms, parts_a, parts_b, waited[3:], VMEM_BYTES)
    parts_b.append(trade(sent_b, "chrom", 2))
    parts_a.append(trade(sent_a, "seq", 1))
    sent_a, sent_b, norms = combine(norms, parts_a, parts_b, waited[:3], LATER_VMEM_BYTES)
    parts_b.append(trade(sent_b, "seq", 1))
    parts_a.append(trade(sent_a, "chrom", 2))
    mine, norms, *payloads = cut_pieces(norms, parts_a, parts_b, share)
    came = [trade(payload, "seq", 2 * b) for b, payload in enumerate(payloads, 1)]
    mine, norms = add_pieces(norms, mine, came)
    pieces = [mine] + [trade(mine, "chrom", bits) for bits in (2, 1, 3)]
    return finish(norms, pieces, share, factor)


def body(
    features,
    first_dilated_taps,
    first_norm_scale,
    first_norm_offset,
    first_pointwise_weight,
    second_dilated_taps,
    second_norm_scale,
    second_norm_offset,
    second_pointwise_weight,
    cotangent,
):
    count = lax.axis_size("seq")
    rows = features.shape[1]
    factor = 1.0 / math.sqrt(rows * count * lax.axis_size("chrom"))
    shifts = DILATION_FIRST // count, DILATION_SECOND // count
    routes = Routes(rows, count)
    first = first_dilated_taps, first_norm_scale, first_norm_offset, first_pointwise_weight
    second = second_dilated_taps, second_norm_scale, second_norm_offset, second_pointwise_weight
    u_slots = routes.out(features[0])
    g_slots = routes.out(cotangent[0])
    saved = ahead(routes, features[0], u_slots, first, second, shifts, rows)
    grads, halves, norms = reverse(
        routes, features[0], u_slots, cotangent[0], g_slots, saved, first, second, shifts, rows
    )
    came = routes.back(grads)
    share = features.shape[2] // count
    conv_a, point_a, conv_b, point_b, *norms = settle(halves, norms, came, share, factor)
    grad_input = gather_units(routes, came + list(grads[len(came) :]))[None]
    return (
        grad_input,
        conv_a, point_a.T, norms[0], norms[1],
        conv_b, point_b.T, norms[2], norms[3],
    )


def solution(mesh):
    in_specs = (
        P("chrom", "seq", None),
        P(),
        P(),
        P(),
        P(),
        P(),
        P(),
        P(),
        P(),
        P("chrom", "seq", None),
    )
    out_specs = (
        P("chrom", "seq", None),
        P(None, "seq", None),
        P(None, "seq"),
        P(),
        P(),
        P(None, "seq", None),
        P(None, "seq"),
        P(),
        P(),
    )
    return jax.shard_map(body, mesh=mesh, in_specs=in_specs, out_specs=out_specs, check_vma=False)
```

time: 186 us -> 138 us (0.74)
  Pallas kernels: 0 us -> 30.1 us
  local copies, waits for them, and re-layouts: 38.6 us -> 10.1 us
  matrix products: 25.2 us -> 0 us
  waiting for transfers between devices: 74.2 us -> 56.1 us
  other arithmetic: 11.7 us -> 0 us
  starting transfers between devices: 33.1 us -> 39.7 us
    all_to_all x5 -> x0, waiting for transfers between devices: 55.5 us -> none  [the longest x2 37.7 us: to_classes(): return lax.all_to_all(pieces, 'seq', 0, 0).reshape(rows, width)]
    ppermute x10 -> x24, waiting for transfers between devices: 18.7 us -> 56.1 us  [the longest x12 22.5 us: trade(): lax.ppermute(value, axis, [(i, i ^ bits) for i in range(lax.axis_size(axi...]
    pallas_call x0 -> x8, Pallas kernels: none -> 30.1 us  [the longest x1 14.5 us: reverse(): pl.pallas_call(functools.partial(reverse_kernel, routes, count, shifts),...]
    ppermute x10 -> x24, starting transfers between devices: 11.6 us -> 39.7 us  [the longest x8 16.2 us: out(): lax.ppermute(part, 'seq', [(i, t) for i, (_, t, _) in permute.items()])]
    dot_general x23 -> x0, matrix products: 25.2 us -> none  [dot(): return jnp.dot(left, right, preferred_element_type=jnp.float32)]
    all_to_all x5 -> x0, starting transfers between devices: 21.4 us -> none  [the longest x2 10.8 us: to_classes(): return lax.all_to_all(pieces, 'seq', 0, 0).reshape(rows, width)]
    concatenate x2 -> x0, local copies, waits for them, and re-layouts: 15.5 us -> none  [halve(): packed = jnp.concatenate([sent.reshape(-1, width), split_norms(norms)], 0)]
    slice x10 -> x2, local copies, waits for them, and re-layouts: 8.2 us -> 1.33 us  [out(): part = field[slots[0] * self.unit:(slots[0] + 1) * self.unit]]
  transfers between devices with their start and end apart: 15 -> 24, of which waited for: 11 -> 14; matrix products, arithmetic and copies ran while one was open for 17% -> 0% of each run, Pallas kernels for 0% -> 7%
where the time goes in v2:
time: 138 us; the launch traced here: 137 us
  waiting for transfers between devices  56.1 us (41%)
  starting transfers between devices  39.7 us (29%)
  Pallas kernels  30.1 us (22%)
  local copies, waits for them, and re-layouts  10.1 us (7%)
  between operations  1.56 us (1%)
    ppermute x12, waiting for transfers between devices, trade(): lax.ppermute(value, axis, [(i, i ^ bits) for i in range(lax.axis_size(axi...  22.5 us
    ppermute x4, waiting for transfers between devices, back(): lax.ppermute(part, 'seq', [(t, i) for i, (_, t, _) in permute.items()])  17.5 us
    ppermute x8, starting transfers between devices, out(): lax.ppermute(part, 'seq', [(i, t) for i, (_, t, _) in permute.items()])  16.2 us
    ppermute x8, waiting for transfers between devices, out(): lax.ppermute(part, 'seq', [(i, t) for i, (_, t, _) in permute.items()])  16.2 us
    ppermute x12, starting transfers between devices, trade(): lax.ppermute(value, axis, [(i, i ^ bits) for i in range(lax.axis_size(axi...  14.9 us
    pallas_call x1, Pallas kernels, reverse(): pl.pallas_call(functools.partial(reverse_kernel, routes, count, shifts),...  14.5 us
    ppermute x4, starting transfers between devices, back(): lax.ppermute(part, 'seq', [(t, i) for i, (_, t, _) in permute.items()])  8.55 us
    unnamed x60, local copies, waits for them, and re-layouts  7.43 us
  transfers between devices with their start and end apart: 24, of which 14 were waited for; matrix products, arithmetic and copies ran while one was open for 0% of the time, Pallas kernels for 7%

profile of v2, /device:TPU:0, one launch (start us, length us, event | category | flops | bytes accessed | tf_op | source)
XLA Modules:
  0.0 137.5 jit_solution(14989881153045074042)
XLA Ops:
  0.6 0.0 copy-start.15
  0.7 1.3 dynamic_slice.16
  2.6 1.3 slice_bitcast_fusion.3
  3.9 4.0 %collective-permute-start.3 = (bf16[128,768]{1,0:T(8,128)(2,1)S(1)}, bf16[128,768]{1,0:T(8,128)(2,1)S(1)}, u32[]{:S(2)}, u32[]{:S(2)}) collective-permute-start(bf16[128,768]{1,0:T(8,128)(2,1)S(1)} %get-tuple-element.85), channel_id=1, source_target_pairs={{0,12},{4,0},{8,20},{12,8},{16,28},{20,16},{24,4},{28,24},{1,13},{... | collective-permute-start | bytes 589832 | tf_op jit(solution)/shard_map/ppermute | solution.py:111
  8.0 0.0 collective-permute-start.1
  8.0 2.6 %collective-permute-start = (bf16[128,768]{1,0:T(8,128)(2,1)S(1)}, bf16[128,768]{1,0:T(8,128)(2,1)S(1)}, u32[]{:S(2)}, u32[]{:S(2)}) collective-permute-start(bf16[128,768]{1,0:T(8,128)(2,1)S(1)} %get-tuple-element.87), channel_id=1, source_target_pairs={{4,20},{12,28},{20,4},{28,12},{0,16},{8,24},{16,0},{24,8},{5,21},{... | collective-permute-start | bytes 589832 | tf_op jit(solution)/shard_map/ppermute | solution.py:111
  10.5 1.1 collective-permute-start.2
  11.6 0.1 slice_bitcast_fusion
  11.7 2.4 %collective-permute-start.7 = (bf16[128,768]{1,0:T(8,128)(2,1)S(1)}, bf16[128,768]{1,0:T(8,128)(2,1)S(1)}, u32[]{:S(2)}, u32[]{:S(2)}) collective-permute-start(bf16[128,768]{1,0:T(8,128)(2,1)S(1)} %get-tuple-element.81), channel_id=1, source_target_pairs={{0,12},{4,0},{8,20},{12,8},{16,28},{20,16},{24,4},{28,24},{1,13},{... | collective-permute-start | bytes 589832 | tf_op jit(solution)/shard_map/ppermute | solution.py:111
  14.0 2.2 %collective-permute-done.3.refs_4_ = bf16[128,768]{1,0:T(8,128)(2,1)S(1)} collective-permute-done((bf16[128,768]{1,0:T(8,128)(2,1)S(1)}, bf16[128,768]{1,0:T(8,128)(2,1)S(1)}, u32[]{:S(2)}, u32[]{:S(2)}) %collective-permute-start.3) | collective-permute-done | bytes 196640 | tf_op jit(solution)/shard_map/ppermute | solution.py:111
  16.2 1.3 collective-permute-start.5
  17.5 0.1 collective-permute-done.1.refs_2_
  17.6 4.9 %collective-permute-start.4 = (bf16[128,768]{1,0:T(8,128)(2,1)S(1)}, bf16[128,768]{1,0:T(8,128)(2,1)S(1)}, u32[]{:S(2)}, u32[]{:S(2)}) collective-permute-start(bf16[128,768]{1,0:T(8,128)(2,1)S(1)} %get-tuple-element.83), channel_id=1, source_target_pairs={{4,20},{12,28},{20,4},{28,12},{0,16},{8,24},{16,0},{24,8},{5,21},{... | collective-permute-start | bytes 589832 | tf_op jit(solution)/shard_map/ppermute | solution.py:111
  22.5 13.5 %collective-permute-done.refs_1_ = bf16[128,768]{1,0:T(8,128)(2,1)S(1)} collective-permute-done((bf16[128,768]{1,0:T(8,128)(2,1)S(1)}, bf16[128,768]{1,0:T(8,128)(2,1)S(1)}, u32[]{:S(2)}, u32[]{:S(2)}) %collective-permute-start) | collective-permute-done | bytes 196640 | tf_op jit(solution)/shard_map/ppermute | solution.py:111
  36.0 0.0 collective-permute-start.6
  36.0 0.6 copy-done.21
  36.7 0.1 copy-done.22
  36.7 7.3 %shard_map.187 = (f32[640,384]{1,0:T(8,128)}, bf16[640,384]{1,0:T(8,128)(2,1)}, bf16[640,768]{1,0:T(8,128)(2,1)}, f32[640,384]{1,0:T(8,128)}, bf16[640,384]{1,0:T(8,128)(2,1)}) custom-call(bf16[640,768]{1,0:T(8,128)(2,1)} %bitcast.23, bf16[128,768]{1,0:T(8,128)(2,1)} %copy-done.21, bf16[128,768]{1,0:T(8,128)(2,1)} %copy-done.20, ...), custom_call_target="tpu_custom_call" | custom-call | flops 1887436800 | bytes 10485760 | tf_op jit(solution)/shard_map/pallas_call | solution.py:201
  44.0 0.0 collective-permute-done.7.refs_9_
  44.1 0.0 collective-permute-done.4.refs_6_
  44.1 0.4 collective-permute-done.6.refs_8_
  44.5 0.2 copy-done.26
  44.8 0.1 copy-done.27
  44.8 0.1 copy-done.28
  44.9 0.3 copy-done.29
  45.2 14.5 %shard_map.188 = (bf16[128,768]{1,0:T(8,128)(2,1)}, bf16[128,768]{1,0:T(8,128)(2,1)}, bf16[128,768]{1,0:T(8,128)(2,1)}, bf16[128,768]{1,0:T(8,128)(2,1)}, bf16[1...) custom-call(bf16[640,768]{1,0:T(8,128)(2,1)} %bitcast.24, ...), custom_call_target="tpu_custom_call" | custom-call | flops 4152360960 | bytes 18874368 | tf_op jit(solution)/shard_map/pallas_call | solution.py:377
  59.7 0.1 collective-permute-start.12
  59.7 0.5 collective-permute-start.13
  60.2 4.7 %collective-permute-start.11 = (bf16[128,768]{1,0:T(8,128)(2,1)}, bf16[128,768]{1,0:T(8,128)(2,1)S(1)}, u32[]{:S(2)}, u32[]{:S(2)}) collective-permute-start(bf16[128,768]{1,0:T(8,128)(2,1)} %get-tuple-element.53), channel_id=1, source_target_pairs={{12,0},{0,4},{20,8},{8,12},{28,16},{16,20},{4,24},{24,28},{13,1},{... | collective-permute-start | bytes 589832 | tf_op jit(solution)/shard_map/ppermute | solution.py:116
  65.0 4.7 %collective-permute-done.11.refs_3_.refs_7_ = bf16[128,768]{1,0:T(8,128)(2,1)S(1)} collective-permute-done((bf16[128,768]{1,0:T(8,128)(2,1)}, bf16[128,768]{1,0:T(8,128)(2,1)S(1)}, u32[]{:S(2)}, u32[]{:S(2)}) %collective-permute-start.11) | collective-permute-done | bytes 196640 | tf_op jit(solution)/shard_map/ppermute | solution.py:116
  69.7 0.7 copy-done.14
  70.4 0.4 copy-done
  70.7 0.4 copy-done.3
  71.2 3.0 %shard_map.190 = (bf16[784,384]{1,0:T(8,128)(2,1)}, bf16[784,384]{1,0:T(8,128)(2,1)}, f32[4,384]{1,0:T(4,128)}) custom-call(f32[4,384]{1,0:T(4,128)} %get-tuple-element.55.refs_0_, bf16[1536,384]{1,0:T(8,128)(2,1)} %get-tuple-element.56.refs_1_.refs_0_, bf16[1552,384]{1,0:T(8,128)(2,1)} %copy-done, bf16[1552,384]{1,0:T(8,128)(2,1)} %copy-done, ...), custom_call_target="tpu_custom_call" | custom-call | bytes 4718592 | tf_op jit(solution)/shard_map/pallas_call | solution.py:476
  74.1 2.4 %collective-permute-start.14 = (bf16[784,384]{1,0:T(8,128)(2,1)}, bf16[784,384]{1,0:T(8,128)(2,1)S(1)}, u32[]{:S(2)}, u32[]{:S(2)}) collective-permute-start(bf16[784,384]{1,0:T(8,128)(2,1)} %get-tuple-element.61), channel_id=1, source_target_pairs={{0,4},{4,0},{8,12},{12,8},{16,20},{20,16},{24,28},{28,24},{1,5},{5... | collective-permute-start | bytes 1806344 | tf_op jit(solution)/shard_map/ppermute | solution.py:438
  76.5 1.5 %collective-permute-start.15 = (bf16[784,384]{1,0:T(8,128)(2,1)}, bf16[784,384]{1,0:T(8,128)(2,1)S(1)}, u32[]{:S(2)}, u32[]{:S(2)}) collective-permute-start(bf16[784,384]{1,0:T(8,128)(2,1)} %get-tuple-element.62), channel_id=1, source_target_pairs={{0,2},{1,3},{2,0},{3,1},{4,6},{5,7},{6,4},{7,5},{8,10},{9,11},{10,... | collective-permute-start | bytes 1806344 | tf_op jit(solution)/shard_map/ppermute | solution.py:438
  78.0 3.5 %collective-permute-start.9 = (bf16[128,768]{1,0:T(8,128)(2,1)S(1)}, bf16[128,768]{1,0:T(8,128)(2,1)S(1)}, u32[]{:S(2)}, u32[]{:S(2)}) collective-permute-start(bf16[128,768]{1,0:T(8,128)(2,1)S(1)} %copy-done.24), channel_id=1, source_target_pairs={{4,0},{24,4},{12,8},{0,12},{20,16},{8,20},{28,24},{16,28},{5,1},{2... | collective-permute-start | bytes 589832 | tf_op jit(solution)/shard_map/ppermute | solution.py:116
  81.6 0.3 collective-permute-start.10
  81.9 10.3 %collective-permute-done.8.refs_0_.refs_9_ = bf16[128,768]{1,0:T(8,128)(2,1)S(1)} collective-permute-done((bf16[128,768]{1,0:T(8,128)(2,1)S(1)}, bf16[128,768]{1,0:T(8,128)(2,1)S(1)}, u32[]{:S(2)}, u32[]{:S(2)}) %collective-permute-start.8) | collective-permute-done | bytes 196640 | tf_op jit(solution)/shard_map/ppermute | solution.py:116
  92.1 1.8 %collective-permute-done.9.refs_1_.refs_10_ = bf16[128,768]{1,0:T(8,128)(2,1)S(1)} collective-permute-done((bf16[128,768]{1,0:T(8,128)(2,1)S(1)}, bf16[128,768]{1,0:T(8,128)(2,1)S(1)}, u32[]{:S(2)}, u32[]{:S(2)}) %collective-permute-start.9) | collective-permute-done | bytes 196640 | tf_op jit(solution)/shard_map/ppermute | solution.py:116
  93.9 0.7 collective-permute-done.10.refs_2_.refs_11_
  94.7 1.3 copy-done.1
  96.0 1.3 copy-done.4
  97.3 0.7 copy-done.12
  98.0 0.2 shard_map.191
  98.2 0.9 collective-permute-start.16
  99.2 1.6 %collective-permute-start.17 = (bf16[400,384]{1,0:T(8,128)(2,1)S(1)}, bf16[400,384]{1,0:T(8,128)(2,1)S(1)}, u32[]{:S(2)}, u32[]{:S(2)}) collective-permute-start(bf16[400,384]{1,0:T(8,128)(2,1)S(1)} %get-tuple-element.65), channel_id=1, source_target_pairs={{0,4},{4,0},{8,12},{12,8},{16,20},{20,16},{24,28},{28,24},{1,5},{5... | collective-permute-start | bytes 921608 | tf_op jit(solution)/shard_map/ppermute | solution.py:438
  100.8 5.3 %collective-permute-done.16.refs_3_.refs_4_ = bf16[400,384]{1,0:T(8,128)(2,1)S(1)} collective-permute-done((bf16[400,384]{1,0:T(8,128)(2,1)S(1)}, bf16[400,384]{1,0:T(8,128)(2,1)S(1)}, u32[]{:S(2)}, u32[]{:S(2)}) %collective-permute-start.16) | collective-permute-done | bytes 307232 | tf_op jit(solution)/shard_map/ppermute | solution.py:438
  106.1 0.6 collective-permute-done.17.refs_8_.refs_9_
  106.7 0.3 shard_map.192
  107.0 3.3 %collective-permute-start.18 = (bf16[208,384]{1,0:T(8,128)(2,1)S(1)}, bf16[208,384]{1,0:T(8,128)(2,1)S(1)}, u32[]{:S(2)}, u32[]{:S(2)}) collective-permute-start(bf16[208,384]{1,0:T(8,128)(2,1)S(1)} %get-tuple-element.68), channel_id=1, source_target_pairs={{0,8},{4,12},{8,0},{12,4},{16,24},{20,28},{24,16},{28,20},{1,9},{5... | collective-permute-start | bytes 479240 | tf_op jit(solution)/shard_map/ppermute | solution.py:438
  110.3 0.4 collective-permute-start.19
  110.8 2.0 %collective-permute-start.20 = (bf16[208,384]{1,0:T(8,128)(2,1)S(1)}, bf16[208,384]{1,0:T(8,128)(2,1)S(1)}, u32[]{:S(2)}, u32[]{:S(2)}) collective-permute-start(bf16[208,384]{1,0:T(8,128)(2,1)S(1)} %get-tuple-element.70), channel_id=1, source_target_pairs={{0,24},{4,28},{8,16},{12,20},{16,8},{20,12},{24,0},{28,4},{1,25},{... | collective-permute-start | bytes 479240 | tf_op jit(solution)/shard_map/ppermute | solution.py:438
  112.8 2.6 %collective-permute-done.18.refs_0_ = bf16[208,384]{1,0:T(8,128)(2,1)S(1)} collective-permute-done((bf16[208,384]{1,0:T(8,128)(2,1)S(1)}, bf16[208,384]{1,0:T(8,128)(2,1)S(1)}, u32[]{:S(2)}, u32[]{:S(2)}) %collective-permute-start.18) | collective-permute-done | bytes 159776 | tf_op jit(solution)/shard_map/ppermute | solution.py:438
  115.4 9.0 %collective-permute-done.19.refs_1_ = bf16[208,384]{1,0:T(8,128)(2,1)S(1)} collective-permute-done((bf16[208,384]{1,0:T(8,128)(2,1)S(1)}, bf16[208,384]{1,0:T(8,128)(2,1)S(1)}, u32[]{:S(2)}, u32[]{:S(2)}) %collective-permute-start.19) | collective-permute-done | bytes 159776 | tf_op jit(solution)/shard_map/ppermute | solution.py:438
  124.5 0.1 shard_map.193
  124.6 0.6 copy-done.13
  125.1 1.6 %collective-permute-start.22 = (bf16[192,384]{1,0:T(8,128)(2,1)S(1)}, bf16[192,384]{1,0:T(8,128)(2,1)S(1)}, u32[]{:S(2)}, u32[]{:S(2)}) collective-permute-start(bf16[192,384]{1,0:T(8,128)(2,1)S(1)} %get-tuple-element.72.refs_0_), channel_id=1, source_target_pairs={{0,1},{1,0},{2,3},{3,2},{4,5},{5,4},{6,7},{7,6},{8,9},{9,8},{10,11... | collective-permute-start | bytes 442376 | tf_op jit(solution)/shard_map/ppermute | solution.py:438
  126.7 0.6 collective-permute-start.21
  127.3 2.3 %shard_map.189 = bf16[640,768]{1,0:T(8,128)(2,1)} custom-call(bf16[128,768]{1,0:T(8,128)(2,1)} %copy-done.8, bf16[128,768]{1,0:T(8,128)(2,1)} %copy-done.9, bf16[128,768]{1,0:T(8,128)(2,1)} %copy-done.10, bf16[128,768]{1,0:T(8,128)(2,1)} %copy-done.14, bf16[128,768]{1,0:T(8,128)(2,1)} %get-tuple-element.54.refs_4_), custom_call_target="tpu_custom_call" | custom-call | bytes 2097152 | tf_op jit(solution)/shard_map/pallas_call | solution.py:428
  129.6 1.7 %collective-permute-done.23.refs_3_ = bf16[192,384]{1,0:T(8,128)(2,1)S(1)} collective-permute-done((bf16[192,384]{1,0:T(8,128)(2,1)S(1)}, bf16[192,384]{1,0:T(8,128)(2,1)S(1)}, u32[]{:S(2)}, u32[]{:S(2)}) %collective-permute-start.23) | collective-permute-done | bytes 147488 | tf_op jit(solution)/shard_map/ppermute | solution.py:438
  131.3 3.2 %collective-permute-done.21.refs_1_ = bf16[192,384]{1,0:T(8,128)(2,1)S(1)} collective-permute-done((bf16[192,384]{1,0:T(8,128)(2,1)S(1)}, bf16[192,384]{1,0:T(8,128)(2,1)S(1)}, u32[]{:S(2)}, u32[]{:S(2)}) %collective-permute-start.21) | collective-permute-done | bytes 147488 | tf_op jit(solution)/shard_map/ppermute | solution.py:438
  134.5 0.6 copy-done.18
  135.1 2.4 %shard_map.194 = (f32[3,96,384]{2,1,0:T(8,128)}, f32[96,384]{1,0:T(8,128)}, f32[3,96,384]{2,1,0:T(8,128)}, f32[96,384]{1,0:T(8,128)}, f32[384]{0:T(512)}, /*index=5*/f32[384]{0:T(512)}, f32[384]{0:T(512)}, f32[384]{0:T(512)}) custom-call(f32[4,384]{1,0:T(4,128)} %copy-done.13, bf16[192,384]{1,0:T(8,128)(2,1)} %copy-done.11, bf16[192,384]{1,0:T(8,128)(2,1)} %copy-done.18, ...), custom_call_target="tpu_custom_call" | custom-call | bytes 2097152 | tf_op jit(solution)/shard_map/pallas_call | solution.py:581
  (55 shorter events, 0.1 us)
Async XLA Ops:
  0.6 11.0 %copy-start.15 = (bf16[1,640,768]{2,1,0:T(8,128)(2,1)S(1)}, bf16[1,640,768]{2,1,0:T(8,128)(2,1)}, u32[]{:S(2)}) copy-start(bf16[1,640,768]{2,1,0:T(8,128)(2,1)} %param.21) | copy-start | bytes 2949124
  3.9 12.3 %collective-permute-start.3 = (bf16[128,768]{1,0:T(8,128)(2,1)S(1)}, bf16[128,768]{1,0:T(8,128)(2,1)S(1)}, u32[]{:S(2)}, u32[]{:S(2)}) collective-permute-start(bf16[128,768]{1,0:T(8,128)(2,1)S(1)} %get-tuple-element.85), channel_id=1, source_target_pairs={{0,12},{4,0},{8,20},{12,8},{16,28},{20,16},{24,4},{28,24},{1,13},{... | collective-permute-start | bytes 589832 | tf_op jit(solution)/shard_map/ppermute | solution.py:111
  8.0 9.7 %collective-permute-start.1 = (bf16[128,768]{1,0:T(8,128)(2,1)S(1)}, bf16[128,768]{1,0:T(8,128)(2,1)S(1)}, u32[]{:S(2)}, u32[]{:S(2)}) collective-permute-start(bf16[128,768]{1,0:T(8,128)(2,1)S(1)} %get-tuple-element.86), channel_id=1, source_target_pairs={{0,4},{4,24},{8,12},{12,0},{16,20},{20,8},{24,28},{28,16},{1,5},{5... | collective-permute-start | bytes 589832 | tf_op jit(solution)/shard_map/ppermute | solution.py:111
  8.0 28.0 %collective-permute-start = (bf16[128,768]{1,0:T(8,128)(2,1)S(1)}, bf16[128,768]{1,0:T(8,128)(2,1)S(1)}, u32[]{:S(2)}, u32[]{:S(2)}) collective-permute-start(bf16[128,768]{1,0:T(8,128)(2,1)S(1)} %get-tuple-element.87), channel_id=1, source_target_pairs={{4,20},{12,28},{20,4},{28,12},{0,16},{8,24},{16,0},{24,8},{5,21},{... | collective-permute-start | bytes 589832 | tf_op jit(solution)/shard_map/ppermute | solution.py:111
  10.5 25.4 %collective-permute-start.2 = (bf16[128,768]{1,0:T(8,128)(2,1)S(1)}, bf16[128,768]{1,0:T(8,128)(2,1)S(1)}, u32[]{:S(2)}, u32[]{:S(2)}) collective-permute-start(bf16[128,768]{1,0:T(8,128)(2,1)S(1)} %get-tuple-element.88), channel_id=1, source_target_pairs={{0,8},{4,28},{8,16},{12,4},{16,24},{20,12},{24,0},{28,20},{1,9},{5... | collective-permute-start | bytes 589832 | tf_op jit(solution)/shard_map/ppermute | solution.py:111
  11.7 32.4 %collective-permute-start.7 = (bf16[128,768]{1,0:T(8,128)(2,1)S(1)}, bf16[128,768]{1,0:T(8,128)(2,1)S(1)}, u32[]{:S(2)}, u32[]{:S(2)}) collective-permute-start(bf16[128,768]{1,0:T(8,128)(2,1)S(1)} %get-tuple-element.81), channel_id=1, source_target_pairs={{0,12},{4,0},{8,20},{12,8},{16,28},{20,16},{24,4},{28,24},{1,13},{... | collective-permute-start | bytes 589832 | tf_op jit(solution)/shard_map/ppermute | solution.py:111
  16.2 19.8 %copy-start.19 = (bf16[128,768]{1,0:T(8,128)(2,1)}, bf16[128,768]{1,0:T(8,128)(2,1)S(1)}, u32[]{:S(2)}) copy-start(bf16[128,768]{1,0:T(8,128)(2,1)S(1)} %collective-permute-done.3.refs_4_) | copy-start | bytes 589828
  16.2 27.9 %collective-permute-start.5 = (bf16[128,768]{1,0:T(8,128)(2,1)S(1)}, bf16[128,768]{1,0:T(8,128)(2,1)S(1)}, u32[]{:S(2)}, u32[]{:S(2)}) collective-permute-start(bf16[128,768]{1,0:T(8,128)(2,1)S(1)} %get-tuple-element.82), channel_id=1, source_target_pairs={{0,4},{4,24},{8,12},{12,0},{16,20},{20,8},{24,28},{28,16},{1,5},{5... | collective-permute-start | bytes 589832 | tf_op jit(solution)/shard_map/ppermute | solution.py:111
  17.6 18.4 %copy-start.20 = (bf16[128,768]{1,0:T(8,128)(2,1)}, bf16[128,768]{1,0:T(8,128)(2,1)S(1)}, u32[]{:S(2)}) copy-start(bf16[128,768]{1,0:T(8,128)(2,1)S(1)} %collective-permute-done.1.refs_2_) | copy-start | bytes 589828
  17.6 26.5 %collective-permute-start.4 = (bf16[128,768]{1,0:T(8,128)(2,1)S(1)}, bf16[128,768]{1,0:T(8,128)(2,1)S(1)}, u32[]{:S(2)}, u32[]{:S(2)}) collective-permute-start(bf16[128,768]{1,0:T(8,128)(2,1)S(1)} %get-tuple-element.83), channel_id=1, source_target_pairs={{4,20},{12,28},{20,4},{28,12},{0,16},{8,24},{16,0},{24,8},{5,21},{... | collective-permute-start | bytes 589832 | tf_op jit(solution)/shard_map/ppermute | solution.py:111
  36.0 0.7 copy-start.21
  36.0 8.5 %collective-permute-start.6 = (bf16[128,768]{1,0:T(8,128)(2,1)S(1)}, bf16[128,768]{1,0:T(8,128)(2,1)S(1)}, u32[]{:S(2)}, u32[]{:S(2)}) collective-permute-start(bf16[128,768]{1,0:T(8,128)(2,1)S(1)} %get-tuple-element.84), channel_id=1, source_target_pairs={{0,8},{4,28},{8,16},{12,4},{16,24},{20,12},{24,0},{28,20},{1,9},{5... | collective-permute-start | bytes 589832 | tf_op jit(solution)/shard_map/ppermute | solution.py:111
  36.0 0.7 copy-start.22
  44.1 0.7 copy-start.26
  44.1 0.7 copy-start.27
  44.1 0.8 copy-start.28
  44.5 0.7 copy-start.29
  59.7 10.0 %collective-permute-start.12 = (bf16[1552,384]{1,0:T(8,128)(2,1)}, bf16[1552,384]{1,0:T(8,128)(2,1)S(1)}, u32[]{:S(2)}, u32[]{:S(2)}) collective-permute-start(bf16[1552,384]{1,0:T(8,128)(2,1)} %get-tuple-element.57), channel_id=1, source_target_pairs={{0,1},{1,0},{2,3},{3,2},{4,5},{5,4},{6,7},{7,6},{8,9},{9,8},{10,11... | collective-permute-start | bytes 3575816 | tf_op jit(solution)/shard_map/ppermute | solution.py:438
  59.7 9.9 %collective-permute-start.13 = (bf16[1552,384]{1,0:T(8,128)(2,1)}, bf16[1552,384]{1,0:T(8,128)(2,1)S(1)}, u32[]{:S(2)}, u32[]{:S(2)}) collective-permute-start(bf16[1552,384]{1,0:T(8,128)(2,1)} %get-tuple-element.59), channel_id=1, source_target_pairs={{0,1},{1,0},{2,3},{3,2},{4,5},{5,4},{6,7},{7,6},{8,9},{9,8},{10,11... | collective-permute-start | bytes 3575816 | tf_op jit(solution)/shard_map/ppermute | solution.py:438
  60.2 9.4 %collective-permute-start.11 = (bf16[128,768]{1,0:T(8,128)(2,1)}, bf16[128,768]{1,0:T(8,128)(2,1)S(1)}, u32[]{:S(2)}, u32[]{:S(2)}) collective-permute-start(bf16[128,768]{1,0:T(8,128)(2,1)} %get-tuple-element.53), channel_id=1, source_target_pairs={{12,0},{0,4},{20,8},{8,12},{28,16},{16,20},{4,24},{24,28},{13,1},{... | collective-permute-start | bytes 589832 | tf_op jit(solution)/shard_map/ppermute | solution.py:116
  69.7 0.7 copy-start.14
  69.7 1.1 copy-start
  69.7 1.5 %copy-start.3 = (bf16[1552,384]{1,0:T(8,128)(2,1)}, bf16[1552,384]{1,0:T(8,128)(2,1)S(1)}, u32[]{:S(2)}) copy-start(bf16[1552,384]{1,0:T(8,128)(2,1)S(1)} %collective-permute-done.13.refs_5_.refs_6_) | copy-start | bytes 3575812
  71.2 6.8 %copy-start.25 = (bf16[128,768]{1,0:T(8,128)(2,1)S(1)}, bf16[128,768]{1,0:T(8,128)(2,1)}, u32[]{:S(2)}) copy-start(bf16[128,768]{1,0:T(8,128)(2,1)} %get-tuple-element.50) | copy-start | bytes 589828
  71.2 6.9 %copy-start.24 = (bf16[128,768]{1,0:T(8,128)(2,1)S(1)}, bf16[128,768]{1,0:T(8,128)(2,1)}, u32[]{:S(2)}) copy-start(bf16[128,768]{1,0:T(8,128)(2,1)} %get-tuple-element.51) | copy-start | bytes 589828
  71.2 10.4 %copy-start.23 = (bf16[128,768]{1,0:T(8,128)(2,1)S(1)}, bf16[128,768]{1,0:T(8,128)(2,1)}, u32[]{:S(2)}) copy-start(bf16[128,768]{1,0:T(8,128)(2,1)} %get-tuple-element.52) | copy-start | bytes 589828
  71.2 23.5 %copy-start.6 = (bf16[1536,384]{1,0:T(8,128)(2,1)S(1)}, bf16[1536,384]{1,0:T(8,128)(2,1)}, u32[]{:S(2)}) copy-start(bf16[1536,384]{1,0:T(8,128)(2,1)} %get-tuple-element.58.refs_4_.refs_5_) | copy-start | bytes 3538948
  71.2 23.5 %copy-start.7 = (bf16[1536,384]{1,0:T(8,128)(2,1)S(1)}, bf16[1536,384]{1,0:T(8,128)(2,1)}, u32[]{:S(2)}) copy-start(bf16[1536,384]{1,0:T(8,128)(2,1)} %get-tuple-element.56.refs_1_.refs_0_) | copy-start | bytes 3538948
  74.1 20.5 %collective-permute-start.14 = (bf16[784,384]{1,0:T(8,128)(2,1)}, bf16[784,384]{1,0:T(8,128)(2,1)S(1)}, u32[]{:S(2)}, u32[]{:S(2)}) collective-permute-start(bf16[784,384]{1,0:T(8,128)(2,1)} %get-tuple-element.61), channel_id=1, source_target_pairs={{0,4},{4,0},{8,12},{12,8},{16,20},{20,16},{24,28},{28,24},{1,5},{5... | collective-permute-start | bytes 1806344 | tf_op jit(solution)/shard_map/ppermute | solution.py:438
  76.5 18.1 %collective-permute-start.15 = (bf16[784,384]{1,0:T(8,128)(2,1)}, bf16[784,384]{1,0:T(8,128)(2,1)S(1)}, u32[]{:S(2)}, u32[]{:S(2)}) collective-permute-start(bf16[784,384]{1,0:T(8,128)(2,1)} %get-tuple-element.62), channel_id=1, source_target_pairs={{0,2},{1,3},{2,0},{3,1},{4,6},{5,7},{6,4},{7,5},{8,10},{9,11},{10,... | collective-permute-start | bytes 1806344 | tf_op jit(solution)/shard_map/ppermute | solution.py:438
  78.0 14.1 %collective-permute-start.8 = (bf16[128,768]{1,0:T(8,128)(2,1)S(1)}, bf16[128,768]{1,0:T(8,128)(2,1)S(1)}, u32[]{:S(2)}, u32[]{:S(2)}) collective-permute-start(bf16[128,768]{1,0:T(8,128)(2,1)S(1)} %copy-done.25), channel_id=1, source_target_pairs={{20,4},{28,12},{4,20},{12,28},{16,0},{24,8},{0,16},{8,24},{21,5},{... | collective-permute-start | bytes 589832 | tf_op jit(solution)/shard_map/ppermute | solution.py:116
  78.0 15.9 %collective-permute-start.9 = (bf16[128,768]{1,0:T(8,128)(2,1)S(1)}, bf16[128,768]{1,0:T(8,128)(2,1)S(1)}, u32[]{:S(2)}, u32[]{:S(2)}) collective-permute-start(bf16[128,768]{1,0:T(8,128)(2,1)S(1)} %copy-done.24), channel_id=1, source_target_pairs={{4,0},{24,4},{12,8},{0,12},{20,16},{8,20},{28,24},{16,28},{5,1},{2... | collective-permute-start | bytes 589832 | tf_op jit(solution)/shard_map/ppermute | solution.py:116
  81.6 13.1 %collective-permute-start.10 = (bf16[128,768]{1,0:T(8,128)(2,1)S(1)}, bf16[128,768]{1,0:T(8,128)(2,1)S(1)}, u32[]{:S(2)}, u32[]{:S(2)}) collective-permute-start(bf16[128,768]{1,0:T(8,128)(2,1)S(1)} %copy-done.23), channel_id=1, source_target_pairs={{8,0},{28,4},{16,8},{4,12},{24,16},{12,20},{0,24},{20,28},{9,1},{2... | collective-permute-start | bytes 589832 | tf_op jit(solution)/shard_map/ppermute | solution.py:116
  92.1 6.1 %copy-start.8 = (bf16[128,768]{1,0:T(8,128)(2,1)}, bf16[128,768]{1,0:T(8,128)(2,1)S(1)}, u32[]{:S(2)}) copy-start(bf16[128,768]{1,0:T(8,128)(2,1)S(1)} %collective-permute-done.8.refs_0_.refs_9_) | copy-start | bytes 589828
  93.9 4.3 %copy-start.9 = (bf16[128,768]{1,0:T(8,128)(2,1)}, bf16[128,768]{1,0:T(8,128)(2,1)S(1)}, u32[]{:S(2)}) copy-start(bf16[128,768]{1,0:T(8,128)(2,1)S(1)} %collective-permute-done.9.refs_1_.refs_10_) | copy-start | bytes 589828
  94.6 3.6 %copy-start.10 = (bf16[128,768]{1,0:T(8,128)(2,1)}, bf16[128,768]{1,0:T(8,128)(2,1)S(1)}, u32[]{:S(2)}) copy-start(bf16[128,768]{1,0:T(8,128)(2,1)S(1)} %collective-permute-done.10.refs_2_.refs_11_) | copy-start | bytes 589828
  94.7 1.3 copy-start.1
  96.0 1.3 copy-start.4
  97.3 0.7 copy-start.12
  98.0 8.7 %copy-start.2 = (bf16[1552,384]{1,0:T(8,128)(2,1)S(1)}, bf16[1552,384]{1,0:T(8,128)(2,1)}, u32[]{:S(2)}) copy-start(bf16[1552,384]{1,0:T(8,128)(2,1)} %copy-done) | copy-start | bytes 3575812
  98.0 8.7 %copy-start.5 = (bf16[1552,384]{1,0:T(8,128)(2,1)S(1)}, bf16[1552,384]{1,0:T(8,128)(2,1)}, u32[]{:S(2)}) copy-start(bf16[1552,384]{1,0:T(8,128)(2,1)} %copy-done.3) | copy-start | bytes 3575812
  98.2 7.9 %collective-permute-start.16 = (bf16[400,384]{1,0:T(8,128)(2,1)S(1)}, bf16[400,384]{1,0:T(8,128)(2,1)S(1)}, u32[]{:S(2)}, u32[]{:S(2)}) collective-permute-start(bf16[400,384]{1,0:T(8,128)(2,1)S(1)} %get-tuple-element.64), channel_id=1, source_target_pairs={{0,2},{1,3},{2,0},{3,1},{4,6},{5,7},{6,4},{7,5},{8,10},{9,11},{10,... | collective-permute-start | bytes 921608 | tf_op jit(solution)/shard_map/ppermute | solution.py:438
  99.2 7.5 %collective-permute-start.17 = (bf16[400,384]{1,0:T(8,128)(2,1)S(1)}, bf16[400,384]{1,0:T(8,128)(2,1)S(1)}, u32[]{:S(2)}, u32[]{:S(2)}) collective-permute-start(bf16[400,384]{1,0:T(8,128)(2,1)S(1)} %get-tuple-element.65), channel_id=1, source_target_pairs={{0,4},{4,0},{8,12},{12,8},{16,20},{20,16},{24,28},{28,24},{1,5},{5... | collective-permute-start | bytes 921608 | tf_op jit(solution)/shard_map/ppermute | solution.py:438
  107.0 8.4 %collective-permute-start.18 = (bf16[208,384]{1,0:T(8,128)(2,1)S(1)}, bf16[208,384]{1,0:T(8,128)(2,1)S(1)}, u32[]{:S(2)}, u32[]{:S(2)}) collective-permute-start(bf16[208,384]{1,0:T(8,128)(2,1)S(1)} %get-tuple-element.68), channel_id=1, source_target_pairs={{0,8},{4,12},{8,0},{12,4},{16,24},{20,28},{24,16},{28,20},{1,9},{5... | collective-permute-start | bytes 479240 | tf_op jit(solution)/shard_map/ppermute | solution.py:438
  110.3 14.1 %collective-permute-start.19 = (bf16[208,384]{1,0:T(8,128)(2,1)S(1)}, bf16[208,384]{1,0:T(8,128)(2,1)S(1)}, u32[]{:S(2)}, u32[]{:S(2)}) collective-permute-start(bf16[208,384]{1,0:T(8,128)(2,1)S(1)} %get-tuple-element.69), channel_id=1, source_target_pairs={{0,16},{4,20},{8,24},{12,28},{16,0},{20,4},{24,8},{28,12},{1,17},{... | collective-permute-start | bytes 479240 | tf_op jit(solution)/shard_map/ppermute | solution.py:438
  110.8 13.7 %collective-permute-start.20 = (bf16[208,384]{1,0:T(8,128)(2,1)S(1)}, bf16[208,384]{1,0:T(8,128)(2,1)S(1)}, u32[]{:S(2)}, u32[]{:S(2)}) collective-permute-start(bf16[208,384]{1,0:T(8,128)(2,1)S(1)} %get-tuple-element.70), channel_id=1, source_target_pairs={{0,24},{4,28},{8,16},{12,20},{16,8},{20,12},{24,0},{28,4},{1,25},{... | collective-permute-start | bytes 479240 | tf_op jit(solution)/shard_map/ppermute | solution.py:438
  124.5 0.6 copy-start.13
  125.1 9.3 %copy-start.11 = (bf16[192,384]{1,0:T(8,128)(2,1)}, bf16[192,384]{1,0:T(8,128)(2,1)S(1)}, u32[]{:S(2)}) copy-start(bf16[192,384]{1,0:T(8,128)(2,1)S(1)} %get-tuple-element.72.refs_0_) | copy-start | bytes 442372
  125.1 6.1 %collective-permute-start.23 = (bf16[192,384]{1,0:T(8,128)(2,1)S(1)}, bf16[192,384]{1,0:T(8,128)(2,1)S(1)}, u32[]{:S(2)}, u32[]{:S(2)}) collective-permute-start(bf16[192,384]{1,0:T(8,128)(2,1)S(1)} %get-tuple-element.72.refs_0_), channel_id=1, source_target_pairs={{0,3},{1,2},{2,1},{3,0},{4,7},{5,6},{6,5},{7,4},{8,11},{9,10},{10,... | collective-permute-start | bytes 442376 | tf_op jit(solution)/shard_map/ppermute | solution.py:438
  125.1 6.1 %collective-permute-start.22 = (bf16[192,384]{1,0:T(8,128)(2,1)S(1)}, bf16[192,384]{1,0:T(8,128)(2,1)S(1)}, u32[]{:S(2)}, u32[]{:S(2)}) collective-permute-start(bf16[192,384]{1,0:T(8,128)(2,1)S(1)} %get-tuple-element.72.refs_0_), channel_id=1, source_target_pairs={{0,1},{1,0},{2,3},{3,2},{4,5},{5,4},{6,7},{7,6},{8,9},{9,8},{10,11... | collective-permute-start | bytes 442376 | tf_op jit(solution)/shard_map/ppermute | solution.py:438
  126.7 7.7 %collective-permute-start.21 = (bf16[192,384]{1,0:T(8,128)(2,1)S(1)}, bf16[192,384]{1,0:T(8,128)(2,1)S(1)}, u32[]{:S(2)}, u32[]{:S(2)}) collective-permute-start(bf16[192,384]{1,0:T(8,128)(2,1)S(1)} %get-tuple-element.72.refs_0_), channel_id=1, source_target_pairs={{0,2},{1,3},{2,0},{3,1},{4,6},{5,7},{6,4},{7,5},{8,10},{9,11},{10,... | collective-permute-start | bytes 442376 | tf_op jit(solution)/shard_map/ppermute | solution.py:438
  131.3 3.2 %copy-start.16 = (bf16[192,384]{1,0:T(8,128)(2,1)}, bf16[192,384]{1,0:T(8,128)(2,1)S(1)}, u32[]{:S(2)}) copy-start(bf16[192,384]{1,0:T(8,128)(2,1)S(1)} %collective-permute-done.23.refs_3_) | copy-start | bytes 442372
  131.3 3.2 %copy-start.17 = (bf16[192,384]{1,0:T(8,128)(2,1)}, bf16[192,384]{1,0:T(8,128)(2,1)S(1)}, u32[]{:S(2)}) copy-start(bf16[192,384]{1,0:T(8,128)(2,1)S(1)} %collective-permute-done.22.refs_2_) | copy-start | bytes 442372
  134.4 0.6 copy-start.18

commit v3 on v2

--- a/solution.py
+++ b/solution.py
@@ -104,10 +104,11 @@
         came = []
         for permute in self.permutes:
             slots = [permute[i][0] for i in range(len(permute))]
-            if len(set(slots)) == 1:
-                part = field[slots[0] * self.unit : (slots[0] + 1) * self.unit]
-            else:
-                part = lax.dynamic_slice_in_dim(field, jnp.asarray(slots)[mine] * self.unit, self.unit, 0)
+            kinds = sorted(set(slots))
+            part = field[kinds[0] * self.unit : (kinds[0] + 1) * self.unit]
+            for kind in kinds[1:]:
+                other = field[kind * self.unit : (kind + 1) * self.unit]
+                part = jnp.where(pick([slot == kind for slot in slots], mine) == 1, other, part)
             came.append(lax.ppermute(part, "seq", [(i, t) for i, (_, t, _) in permute.items()]))
         return came
 
@@ -148,7 +149,7 @@
 
 
 def row_parts(rows):
-    step = math.gcd(rows, 128)
+    step = math.gcd(rows, 32)
     return rows // step, step
 
 
@@ -172,7 +173,7 @@
         scale, offset = scale_ref[...][None, :], offset_ref[...][None, :]
         steps, step = row_parts(rows)
 
-        @pl.loop(0, steps)
+        @pl.loop(0, steps, unroll=2 if steps % 2 == 0 else 1)
         def _(at):
             part = pl.ds(pl.multiple_of(at * step, step), step)
             act[part, :] = smooth_value(scale * pre[part, :] + offset).astype(jnp.bfloat16)
@@ -253,7 +254,7 @@
     grad_slots, refs = refs[13 : 13 + len(places)], refs[13 + len(places) :]
     kept_b, sent_b, kept_a, sent_a, norms_ref = refs[:5]
     u_a, g_a, u_b, g_b, pre_a, pre_b, act_a, act_b, taps_a, taps_b, point_a, point_b = refs[5:17]
-    grad_act, grad_pre, product, staged, wide, sums, norm_rows, sems, out_sems = refs[17:]
+    grad_act, grad_pre, turned, product, staged, wide, sums, norm_rows, sems, out_sems = refs[17:]
     rows, width = pre_a.shape
     channels = u_a.shape[1]
     share = channels // count
@@ -281,7 +282,7 @@
         steps, step = row_parts(rows)
         loads[1].wait()
 
-        @pl.loop(0, steps)
+        @pl.loop(0, steps, unroll=2 if steps % 2 == 0 else 1)
         def _(at):
             part = pl.ds(pl.multiple_of(at * step, step), step)
             value = pre[part, :]
@@ -319,18 +320,27 @@
                     act_on(copy)
 
         def settle_one(kind, value):
-            product[:channels, :] = value
+            if pad != share:
+                product[:channels, :] = value
             for at in range(count):
+                piece = (value if pad == share else product)[at * share : at * share + pad, :]
                 place = ((at % 2) ^ odd) * half + ((at // 2) ^ rest) * pad
-                staged[4 * index + kind, pl.ds(pl.multiple_of(place, pad), pad), :] = product[
-                    at * share : at * share + pad, :
-                ].astype(jnp.bfloat16)
+                staged[4 * index + kind, pl.ds(pl.multiple_of(place, pad), pad), :] = piece.astype(
+                    jnp.bfloat16
+                )
             both(kind, lambda copy: copy.start())
 
         wait_all(came)
-        settle_one(0, over_rows(u[:-shift, :], grad_pre[shift:, :]))
-        settle_one(1, over_rows(u[...], grad_pre[...]))
-        settle_one(2, over_rows(u[shift:, :], grad_pre[:-shift, :]))
+        if shift % 128 == 0 and rows % 128 == 0:
+            for first in range(0, rows, 128):
+                turned[:, first : first + 128] = u[first : first + 128, :].T
+            settle_one(0, dot(turned[:, : rows - shift], grad_pre[shift:, :]))
+            settle_one(1, dot(turned[...], grad_pre[...]))
+            settle_one(2, dot(turned[:, shift:], grad_pre[:-shift, :]))
+        else:
+            settle_one(0, over_rows(u[:-shift, :], grad_pre[shift:, :]))
+            settle_one(1, over_rows(u[...], grad_pre[...]))
+            settle_one(2, over_rows(u[shift:, :], grad_pre[:-shift, :]))
         loads[2].wait()
         settle_one(3, over_rows(g[...], act[...]))
         loads[3].wait()
@@ -394,7 +404,8 @@
             *[vmem(point_a.shape, jnp.bfloat16)] * 2,
             vmem(thin, jnp.float32),
             vmem(thin, jnp.bfloat16),
-            vmem((channels + pad - channels // count, width), jnp.float32),
+            vmem((channels, rows), jnp.bfloat16),
+            vmem((8 if pad == channels // count else channels + pad, width), jnp.float32),
             vmem((8, count * pad, width), jnp.bfloat16),
             vmem(wide, jnp.float32),
             vmem((2, 8, width), jnp.float32),
@@ -482,6 +493,26 @@
         compiler_params=pltpu.CompilerParams(vmem_limit_bytes=vmem_bytes),
         cost_estimate=pl.CostEstimate(flops=0, bytes_accessed=8 * size * width * number, transcendentals=0),
     )(norms, *parts_a, parts_a[-1], *parts_b, parts_b[-1], *waited)
+
+
+def fold_kernel(kept_a, came_a, kept_b, came_b, out_a, out_b):
+    out_a[...] = summed([kept_a, came_a]).astype(jnp.bfloat16)
+    out_b[...] = summed([kept_b, came_b]).astype(jnp.bfloat16)
+
+
+def fold(parts_a, parts_b):
+    rows, width = parts_a[0].shape
+    half = jax.ShapeDtypeStruct((rows // 2, width), jnp.bfloat16)
+    spec = rows_at(rows // 2, 0, width)
+    return pl.pallas_call(
+        fold_kernel,
+        grid=(1,),
+        out_shape=(half, half),
+        in_specs=[spec] * 4,
+        out_specs=(spec, spec),
+        compiler_params=pltpu.CompilerParams(vmem_limit_bytes=LATER_VMEM_BYTES),
+        cost_estimate=pl.CostEstimate(flops=0, bytes_accessed=6 * rows * width, transcendentals=0),
+    )(*parts_a, *parts_b)
 
 
 def pieces_kernel(number, norms_in, *refs):
@@ -591,15 +622,17 @@
     kept_b, sent_b, kept_a, sent_a = halves
     parts_b, parts_a = [kept_b, trade(sent_b, "chrom", 1)], [kept_a, trade(sent_a, "chrom", 1)]
     sent_a, sent_b, norms = combine(norms, parts_a, parts_b, waited[3:], VMEM_BYTES)
-    parts_b.append(trade(sent_b, "chrom", 2))
-    parts_a.append(trade(sent_a, "seq", 1))
+    came_b, came_a = trade(sent_b, "chrom", 2), trade(sent_a, "seq", 1)
+    rest_a, rest_b = fold(parts_a, parts_b)
+    parts_a, parts_b = [rest_a, came_a], [rest_b, came_b]
     sent_a, sent_b, norms = combine(norms, parts_a, parts_b, waited[:3], LATER_VMEM_BYTES)
     parts_b.append(trade(sent_b, "seq", 1))
     parts_a.append(trade(sent_a, "chrom", 2))
     mine, norms, *payloads = cut_pieces(norms, parts_a, parts_b, share)
     came = [trade(payload, "seq", 2 * b) for b, payload in enumerate(payloads, 1)]
     mine, norms = add_pieces(norms, mine, came)
-    pieces = [mine] + [trade(mine, "chrom", bits) for bits in (2, 1, 3)]
+    side = trade(mine, "chrom", 2)
+    pieces = [mine, side, trade(mine, "chrom", 1), trade(side, "chrom", 1)]
     return finish(norms, pieces, share, factor)
 
 

time: 138 us -> 131 us (0.949)
  starting transfers between devices: 39.7 us -> 35.3 us
  local copies, waits for them, and re-layouts: 10.1 us -> 7.35 us
  other arithmetic: 0 us -> 1.47 us
    ppermute x4, waiting for transfers between devices: 17.5 us -> 13.3 us  [back(): lax.ppermute(part, 'seq', [(t, i) for i, (_, t, _) in permute.items()])]
    ppermute x8, waiting for transfers between devices: 16.2 us -> 19.7 us  [out(): lax.ppermute(part, 'seq', [(i, t) for i, (_, t, _) in permute.items()])]
    ppermute x8, starting transfers between devices: 16.2 us -> 12.9 us  [out(): lax.ppermute(part, 'seq', [(i, t) for i, (_, t, _) in permute.items()])]
    ppermute x12, starting transfers between devices: 14.9 us -> 12.9 us  [trade(): lax.ppermute(value, axis, [(i, i ^ bits) for i in range(lax.axis_size(axi...]
    slice x0 -> x2, other arithmetic: none -> 1.47 us  [out(): part = field[kinds[0] * self.unit:(kinds[0] + 1) * self.unit]]
    unnamed x60 -> x56, local copies, waits for them, and re-layouts: 7.43 us -> 7.35 us
  transfers between devices with their start and end apart: 24 -> 24, of which waited for: 14 -> 10; matrix products, arithmetic and copies ran while one was open for 0% -> 0% of each run, Pallas kernels for 7% -> 8%
where the time goes in v3:
time: 131 us
  waiting for transfers between devices  55.1 us (42%)
  starting transfers between devices  35.3 us (27%)
  Pallas kernels  30.5 us (23%)
  local copies, waits for them, and re-layouts  7.35 us (6%)
  other arithmetic  1.47 us (1%)
    ppermute x12, waiting for transfers between devices, trade(): lax.ppermute(value, axis, [(i, i ^ bits) for i in range(lax.axis_size(axi...  22.1 us
    ppermute x8, waiting for transfers between devices, out(): lax.ppermute(part, 'seq', [(i, t) for i, (_, t, _) in permute.items()])  19.7 us
    pallas_call x1, Pallas kernels, reverse(): pl.pallas_call(functools.partial(reverse_kernel, routes, count, shifts),...  14.6 us
    ppermute x4, waiting for transfers between devices, back(): lax.ppermute(part, 'seq', [(t, i) for i, (_, t, _) in permute.items()])  13.3 us
    ppermute x12, starting transfers between devices, trade(): lax.ppermute(value, axis, [(i, i ^ bits) for i in range(lax.axis_size(axi...  12.9 us
    ppermute x8, starting transfers between devices, out(): lax.ppermute(part, 'seq', [(i, t) for i, (_, t, _) in permute.items()])  12.9 us
    ppermute x4, starting transfers between devices, back(): lax.ppermute(part, 'seq', [(t, i) for i, (_, t, _) in permute.items()])  9.57 us
    pallas_call x1, Pallas kernels, ahead(): pl.pallas_call(functools.partial(ahead_kernel, routes, shifts), out_shape...  7.45 us
  transfers between devices with their start and end apart: 24, of which 10 were waited for; matrix products, arithmetic and copies ran while one was open for 0% of the time, Pallas kernels for 8%

profile of v3, /device:TPU:0, one launch (start us, length us, event | category | flops | bytes accessed | tf_op | source)
XLA Modules:
  0.0 130.7 jit_solution(4686717381346243061)
XLA Ops:
  0.6 0.0 copy-start.12
  0.7 1.4 %slice_bitcast_fusion.3 = (bf16[128,768]{1,0:T(8,128)(2,1)S(1)}, bf16[128,768]{1,0:T(8,128)(2,1)S(1)}, bf16[128,768]{1,0:T(8,128)(2,1)S(1)}, bf16[128,768]{1,0:T(8,128)(2,1)S(1)}) fusion(bf16[1,640,768]{2,1,0:T(8,128)(2,1)} %param.10, pred[]{:T(512)S(6)} %eq.39), kind=kLoop, calls=%fused_computation.4 | loop fusion | flops 98304 | bytes 1769473 | tf_op jit(solution)/shard_map/slice | solution.py:108
  2.1 4.0 %collective-permute-start.3 = (bf16[128,768]{1,0:T(8,128)(2,1)S(1)}, bf16[128,768]{1,0:T(8,128)(2,1)S(1)}, u32[]{:S(2)}, u32[]{:S(2)}) collective-permute-start(bf16[128,768]{1,0:T(8,128)(2,1)S(1)} %get-tuple-element.89), channel_id=1, source_target_pairs={{0,12},{4,0},{8,20},{12,8},{16,28},{20,16},{24,4},{28,24},{1,13},{... | collective-permute-start | bytes 589832 | tf_op jit(solution)/shard_map/ppermute | solution.py:112
  6.1 2.6 %collective-permute-start = (bf16[128,768]{1,0:T(8,128)(2,1)S(1)}, bf16[128,768]{1,0:T(8,128)(2,1)S(1)}, u32[]{:S(2)}, u32[]{:S(2)}) collective-permute-start(bf16[128,768]{1,0:T(8,128)(2,1)S(1)} %get-tuple-element.90), channel_id=1, source_target_pairs={{4,20},{12,28},{20,4},{28,12},{0,16},{8,24},{16,0},{24,8},{5,21},{... | collective-permute-start | bytes 589832 | tf_op jit(solution)/shard_map/ppermute | solution.py:112
  8.7 1.1 collective-permute-start.2
  9.8 0.1 slice_bitcast_fusion
  9.9 3.3 %collective-permute-start.7 = (bf16[128,768]{1,0:T(8,128)(2,1)S(1)}, bf16[128,768]{1,0:T(8,128)(2,1)S(1)}, u32[]{:S(2)}, u32[]{:S(2)}) collective-permute-start(bf16[128,768]{1,0:T(8,128)(2,1)S(1)} %get-tuple-element.85), channel_id=1, source_target_pairs={{0,12},{4,0},{8,20},{12,8},{16,28},{20,16},{24,4},{28,24},{1,13},{... | collective-permute-start | bytes 589832 | tf_op jit(solution)/shard_map/ppermute | solution.py:112
  13.1 1.4 %collective-permute-start.4 = (bf16[128,768]{1,0:T(8,128)(2,1)S(1)}, bf16[128,768]{1,0:T(8,128)(2,1)S(1)}, u32[]{:S(2)}, u32[]{:S(2)}) collective-permute-start(bf16[128,768]{1,0:T(8,128)(2,1)S(1)} %get-tuple-element.86), channel_id=1, source_target_pairs={{4,20},{12,28},{20,4},{28,12},{0,16},{8,24},{16,0},{24,8},{5,21},{... | collective-permute-start | bytes 589832 | tf_op jit(solution)/shard_map/ppermute | solution.py:112
  14.5 19.7 %collective-permute-done.refs_1_ = bf16[128,768]{1,0:T(8,128)(2,1)S(1)} collective-permute-done((bf16[128,768]{1,0:T(8,128)(2,1)S(1)}, bf16[128,768]{1,0:T(8,128)(2,1)S(1)}, u32[]{:S(2)}, u32[]{:S(2)}) %collective-permute-start) | collective-permute-done | bytes 196640 | tf_op jit(solution)/shard_map/ppermute | solution.py:112
  34.2 0.0 collective-permute-start.5
  34.2 0.0 copy-start.19
  34.2 0.5 collective-permute-start.6
  34.7 0.0 collective-permute-done.2.refs_3_
  34.7 0.1 copy-done.18
  34.8 0.1 copy-done.19
  34.9 0.5 copy-done.21
  35.4 7.5 %shard_map.169 = (f32[640,384]{1,0:T(8,128)}, bf16[640,384]{1,0:T(8,128)(2,1)}, bf16[640,768]{1,0:T(8,128)(2,1)}, f32[640,384]{1,0:T(8,128)}, bf16[640,384]{1,0:T(8,128)(2,1)}) custom-call(bf16[640,768]{1,0:T(8,128)(2,1)} %bitcast.21, bf16[128,768]{1,0:T(8,128)(2,1)} %copy-done.18, bf16[128,768]{1,0:T(8,128)(2,1)} %copy-done.19, ...), custom_call_target="tpu_custom_call" | custom-call | flops 1887436800 | bytes 10485760 | tf_op jit(solution)/shard_map/pallas_call | solution.py:202
  42.9 0.0 collective-permute-done.7.refs_9_
  42.9 0.0 collective-permute-done.4.refs_6_
  42.9 0.0 collective-permute-done.6.refs_8_
  42.9 0.6 copy-done.24
  43.6 0.1 copy-done.25
  43.6 0.1 copy-done.26
  43.7 0.1 copy-done.27
  43.8 14.6 %shard_map.170 = (bf16[128,768]{1,0:T(8,128)(2,1)}, bf16[128,768]{1,0:T(8,128)(2,1)}, bf16[128,768]{1,0:T(8,128)(2,1)}, bf16[128,768]{1,0:T(8,128)(2,1)}, bf16[1...) custom-call(bf16[640,768]{1,0:T(8,128)(2,1)} %bitcast.22, ...), custom_call_target="tpu_custom_call" | custom-call | flops 4152360960 | bytes 18874368 | tf_op jit(solution)/shard_map/pallas_call | solution.py:387
  58.4 0.1 collective-permute-start.12
  58.5 0.5 collective-permute-start.13
  59.0 3.5 %collective-permute-start.11 = (bf16[128,768]{1,0:T(8,128)(2,1)}, bf16[128,768]{1,0:T(8,128)(2,1)S(1)}, u32[]{:S(2)}, u32[]{:S(2)}) collective-permute-start(bf16[128,768]{1,0:T(8,128)(2,1)} %get-tuple-element.55), channel_id=1, source_target_pairs={{12,0},{0,4},{20,8},{8,12},{28,16},{16,20},{4,24},{24,28},{13,1},{... | collective-permute-start | bytes 589832 | tf_op jit(solution)/shard_map/ppermute | solution.py:117
  62.5 4.7 %collective-permute-done.11.refs_3_.refs_7_ = bf16[128,768]{1,0:T(8,128)(2,1)S(1)} collective-permute-done((bf16[128,768]{1,0:T(8,128)(2,1)}, bf16[128,768]{1,0:T(8,128)(2,1)S(1)}, u32[]{:S(2)}, u32[]{:S(2)}) %collective-permute-start.11) | collective-permute-done | bytes 196640 | tf_op jit(solution)/shard_map/ppermute | solution.py:117
  67.2 0.7 copy-done.13
  67.9 0.4 copy-done
  68.3 0.4 copy-done.2
  68.7 3.0 %shard_map.172 = (bf16[784,384]{1,0:T(8,128)(2,1)}, bf16[784,384]{1,0:T(8,128)(2,1)}, f32[4,384]{1,0:T(4,128)}) custom-call(f32[4,384]{1,0:T(4,128)} %get-tuple-element.57.refs_0_, bf16[1536,384]{1,0:T(8,128)(2,1)} %get-tuple-element.58.refs_1_.kept_a, bf16[1552,384]{1,0:T(8,128)(2,1)} %copy-done, bf16[1552,384]{1,0:T(8,128)(2,1)} %copy-done, ...), custom_call_target="tpu_custom_call" | custom-call | bytes 4718592 | tf_op jit(solution)/shard_map/pallas_call | solution.py:487
  71.7 2.4 %collective-permute-start.14 = (bf16[784,384]{1,0:T(8,128)(2,1)}, bf16[784,384]{1,0:T(8,128)(2,1)S(1)}, u32[]{:S(2)}, u32[]{:S(2)}) collective-permute-start(bf16[784,384]{1,0:T(8,128)(2,1)} %get-tuple-element.64), channel_id=1, source_target_pairs={{0,4},{4,0},{8,12},{12,8},{16,20},{20,16},{24,28},{28,24},{1,5},{5... | collective-permute-start | bytes 1806344 | tf_op jit(solution)/shard_map/ppermute | solution.py:449
  74.0 1.5 %collective-permute-start.15 = (bf16[784,384]{1,0:T(8,128)(2,1)}, bf16[784,384]{1,0:T(8,128)(2,1)S(1)}, u32[]{:S(2)}, u32[]{:S(2)}) collective-permute-start(bf16[784,384]{1,0:T(8,128)(2,1)} %get-tuple-element.66), channel_id=1, source_target_pairs={{0,2},{1,3},{2,0},{3,1},{4,6},{5,7},{6,4},{7,5},{8,10},{9,11},{10,... | collective-permute-start | bytes 1806344 | tf_op jit(solution)/shard_map/ppermute | solution.py:449
  75.5 0.9 collective-permute-start.8
  76.4 3.7 %collective-permute-start.9 = (bf16[128,768]{1,0:T(8,128)(2,1)S(1)}, bf16[128,768]{1,0:T(8,128)(2,1)S(1)}, u32[]{:S(2)}, u32[]{:S(2)}) collective-permute-start(bf16[128,768]{1,0:T(8,128)(2,1)S(1)} %copy-done.22), channel_id=1, source_target_pairs={{4,0},{24,4},{12,8},{0,12},{20,16},{8,20},{28,24},{16,28},{5,1},{2... | collective-permute-start | bytes 589832 | tf_op jit(solution)/shard_map/ppermute | solution.py:117
  80.1 1.5 %collective-permute-start.10 = (bf16[128,768]{1,0:T(8,128)(2,1)S(1)}, bf16[128,768]{1,0:T(8,128)(2,1)S(1)}, u32[]{:S(2)}, u32[]{:S(2)}) collective-permute-start(bf16[128,768]{1,0:T(8,128)(2,1)S(1)} %copy-done.20), channel_id=1, source_target_pairs={{8,0},{28,4},{16,8},{4,12},{24,16},{12,20},{0,24},{20,28},{9,1},{2... | collective-permute-start | bytes 589832 | tf_op jit(solution)/shard_map/ppermute | solution.py:117
  81.6 1.3 copy-done.1
  82.9 1.3 copy-done.3
  84.2 0.3 shard_map.173
  84.5 6.2 %collective-permute-done.8.refs_0_.refs_7_ = bf16[128,768]{1,0:T(8,128)(2,1)S(1)} collective-permute-done((bf16[128,768]{1,0:T(8,128)(2,1)S(1)}, bf16[128,768]{1,0:T(8,128)(2,1)S(1)}, u32[]{:S(2)}, u32[]{:S(2)}) %collective-permute-start.8) | collective-permute-done | bytes 196640 | tf_op jit(solution)/shard_map/ppermute | solution.py:117
  90.7 0.8 collective-permute-done.9.refs_1_.refs_8_
  91.5 1.6 %collective-permute-done.10.refs_2_.refs_9_ = bf16[128,768]{1,0:T(8,128)(2,1)S(1)} collective-permute-done((bf16[128,768]{1,0:T(8,128)(2,1)S(1)}, bf16[128,768]{1,0:T(8,128)(2,1)S(1)}, u32[]{:S(2)}, u32[]{:S(2)}) %collective-permute-start.10) | collective-permute-done | bytes 196640 | tf_op jit(solution)/shard_map/ppermute | solution.py:117
  93.1 0.2 shard_map.174
  93.3 0.5 copy-done.8
  93.8 0.5 collective-permute-start.16
  94.3 0.7 collective-permute-start.17
  95.0 6.6 %collective-permute-done.16.refs_2_.refs_3_ = bf16[400,384]{1,0:T(8,128)(2,1)S(1)} collective-permute-done((bf16[400,384]{1,0:T(8,128)(2,1)S(1)}, bf16[400,384]{1,0:T(8,128)(2,1)S(1)}, u32[]{:S(2)}, u32[]{:S(2)}) %collective-permute-start.16) | collective-permute-done | bytes 307232 | tf_op jit(solution)/shard_map/ppermute | solution.py:449
  101.6 0.2 collective-permute-done.17.refs_6_.refs_7_
  101.8 0.2 shard_map.175
  102.1 3.4 %collective-permute-start.18 = (bf16[208,384]{1,0:T(8,128)(2,1)S(1)}, bf16[208,384]{1,0:T(8,128)(2,1)S(1)}, u32[]{:S(2)}, u32[]{:S(2)}) collective-permute-start(bf16[208,384]{1,0:T(8,128)(2,1)S(1)} %get-tuple-element.72), channel_id=1, source_target_pairs={{0,8},{4,12},{8,0},{12,4},{16,24},{20,28},{24,16},{28,20},{1,9},{5... | collective-permute-start | bytes 479240 | tf_op jit(solution)/shard_map/ppermute | solution.py:449
  105.4 0.6 collective-permute-start.19
  106.1 1.8 %collective-permute-start.20 = (bf16[208,384]{1,0:T(8,128)(2,1)S(1)}, bf16[208,384]{1,0:T(8,128)(2,1)S(1)}, u32[]{:S(2)}, u32[]{:S(2)}) collective-permute-start(bf16[208,384]{1,0:T(8,128)(2,1)S(1)} %get-tuple-element.74), channel_id=1, source_target_pairs={{0,24},{4,28},{8,16},{12,20},{16,8},{20,12},{24,0},{28,4},{1,25},{... | collective-permute-start | bytes 479240 | tf_op jit(solution)/shard_map/ppermute | solution.py:449
  107.9 2.7 %collective-permute-done.18.refs_0_ = bf16[208,384]{1,0:T(8,128)(2,1)S(1)} collective-permute-done((bf16[208,384]{1,0:T(8,128)(2,1)S(1)}, bf16[208,384]{1,0:T(8,128)(2,1)S(1)}, u32[]{:S(2)}, u32[]{:S(2)}) %collective-permute-start.18) | collective-permute-done | bytes 159776 | tf_op jit(solution)/shard_map/ppermute | solution.py:449
  110.5 8.9 %collective-permute-done.19.refs_1_ = bf16[208,384]{1,0:T(8,128)(2,1)S(1)} collective-permute-done((bf16[208,384]{1,0:T(8,128)(2,1)S(1)}, bf16[208,384]{1,0:T(8,128)(2,1)S(1)}, u32[]{:S(2)}, u32[]{:S(2)}) %collective-permute-start.19) | collective-permute-done | bytes 159776 | tf_op jit(solution)/shard_map/ppermute | solution.py:449
  119.4 0.1 shard_map.176
  119.5 0.6 copy-done.11
  120.1 1.4 %collective-permute-start.21 = (bf16[192,384]{1,0:T(8,128)(2,1)S(1)}, bf16[192,384]{1,0:T(8,128)(2,1)S(1)}, u32[]{:S(2)}, u32[]{:S(2)}) collective-permute-start(bf16[192,384]{1,0:T(8,128)(2,1)S(1)} %get-tuple-element.76.refs_0_), channel_id=1, source_target_pairs={{0,2},{1,3},{2,0},{3,1},{4,6},{5,7},{6,4},{7,5},{8,10},{9,11},{10,... | collective-permute-start | bytes 442376 | tf_op jit(solution)/shard_map/ppermute | solution.py:449
  121.5 3.7 %collective-permute-done.21.refs_1_ = bf16[192,384]{1,0:T(8,128)(2,1)S(1)} collective-permute-done((bf16[192,384]{1,0:T(8,128)(2,1)S(1)}, bf16[192,384]{1,0:T(8,128)(2,1)S(1)}, u32[]{:S(2)}, u32[]{:S(2)}) %collective-permute-start.21) | collective-permute-done | bytes 147488 | tf_op jit(solution)/shard_map/ppermute | solution.py:449
  125.2 2.3 %shard_map.171 = bf16[640,768]{1,0:T(8,128)(2,1)} custom-call(bf16[128,768]{1,0:T(8,128)(2,1)} %copy-done.6, bf16[128,768]{1,0:T(8,128)(2,1)} %copy-done.7, bf16[128,768]{1,0:T(8,128)(2,1)} %copy-done.8, bf16[128,768]{1,0:T(8,128)(2,1)} %copy-done.13, bf16[128,768]{1,0:T(8,128)(2,1)} %get-tuple-element.56.refs_4_), custom_call_target="tpu_custom_call" | custom-call | bytes 2097152 | tf_op jit(solution)/shard_map/pallas_call | solution.py:439
  127.6 0.6 copy-done.15
  128.2 0.1 copy-done.16
  128.3 2.4 %shard_map.177 = (f32[3,96,384]{2,1,0:T(8,128)}, f32[96,384]{1,0:T(8,128)}, f32[3,96,384]{2,1,0:T(8,128)}, f32[96,384]{1,0:T(8,128)}, f32[384]{0:T(512)}, /*index=5*/f32[384]{0:T(512)}, f32[384]{0:T(512)}, f32[384]{0:T(512)}) custom-call(f32[4,384]{1,0:T(4,128)} %copy-done.11, bf16[192,384]{1,0:T(8,128)(2,1)} %copy-done.9, bf16[192,384]{1,0:T(8,128)(2,1)} %copy-done.14, ...), custom_call_target="tpu_custom_call" | custom-call | bytes 2097152 | tf_op jit(solution)/shard_map/pallas_call | solution.py:612
  (51 shorter events, 0.1 us)
Async XLA Ops:
  0.6 9.2 %copy-start.12 = (bf16[1,640,768]{2,1,0:T(8,128)(2,1)S(1)}, bf16[1,640,768]{2,1,0:T(8,128)(2,1)}, u32[]{:S(2)}) copy-start(bf16[1,640,768]{2,1,0:T(8,128)(2,1)} %param.19) | copy-start | bytes 2949124
  2.1 11.0 %collective-permute-start.3 = (bf16[128,768]{1,0:T(8,128)(2,1)S(1)}, bf16[128,768]{1,0:T(8,128)(2,1)S(1)}, u32[]{:S(2)}, u32[]{:S(2)}) collective-permute-start(bf16[128,768]{1,0:T(8,128)(2,1)S(1)} %get-tuple-element.89), channel_id=1, source_target_pairs={{0,12},{4,0},{8,20},{12,8},{16,28},{20,16},{24,4},{28,24},{1,13},{... | collective-permute-start | bytes 589832 | tf_op jit(solution)/shard_map/ppermute | solution.py:112
  6.1 28.0 %collective-permute-start = (bf16[128,768]{1,0:T(8,128)(2,1)S(1)}, bf16[128,768]{1,0:T(8,128)(2,1)S(1)}, u32[]{:S(2)}, u32[]{:S(2)}) collective-permute-start(bf16[128,768]{1,0:T(8,128)(2,1)S(1)} %get-tuple-element.90), channel_id=1, source_target_pairs={{4,20},{12,28},{20,4},{28,12},{0,16},{8,24},{16,0},{24,8},{5,21},{... | collective-permute-start | bytes 589832 | tf_op jit(solution)/shard_map/ppermute | solution.py:112
  8.7 25.4 %collective-permute-start.1 = (bf16[128,768]{1,0:T(8,128)(2,1)S(1)}, bf16[128,768]{1,0:T(8,128)(2,1)S(1)}, u32[]{:S(2)}, u32[]{:S(2)}) collective-permute-start(bf16[128,768]{1,0:T(8,128)(2,1)S(1)} %get-tuple-element.91), channel_id=1, source_target_pairs={{0,4},{4,24},{8,12},{12,0},{16,20},{20,8},{24,28},{28,16},{1,5},{5... | collective-permute-start | bytes 589832 | tf_op jit(solution)/shard_map/ppermute | solution.py:112
  8.7 26.0 %collective-permute-start.2 = (bf16[128,768]{1,0:T(8,128)(2,1)S(1)}, bf16[128,768]{1,0:T(8,128)(2,1)S(1)}, u32[]{:S(2)}, u32[]{:S(2)}) collective-permute-start(bf16[128,768]{1,0:T(8,128)(2,1)S(1)} %get-tuple-element.92), channel_id=1, source_target_pairs={{0,8},{4,28},{8,16},{12,4},{16,24},{20,12},{24,0},{28,20},{1,9},{5... | collective-permute-start | bytes 589832 | tf_op jit(solution)/shard_map/ppermute | solution.py:112
  9.9 33.0 %collective-permute-start.7 = (bf16[128,768]{1,0:T(8,128)(2,1)S(1)}, bf16[128,768]{1,0:T(8,128)(2,1)S(1)}, u32[]{:S(2)}, u32[]{:S(2)}) collective-permute-start(bf16[128,768]{1,0:T(8,128)(2,1)S(1)} %get-tuple-element.85), channel_id=1, source_target_pairs={{0,12},{4,0},{8,20},{12,8},{16,28},{20,16},{24,4},{28,24},{1,13},{... | collective-permute-start | bytes 589832 | tf_op jit(solution)/shard_map/ppermute | solution.py:112
  13.1 21.6 %copy-start.17 = (bf16[128,768]{1,0:T(8,128)(2,1)}, bf16[128,768]{1,0:T(8,128)(2,1)S(1)}, u32[]{:S(2)}) copy-start(bf16[128,768]{1,0:T(8,128)(2,1)S(1)} %collective-permute-done.3.refs_4_) | copy-start | bytes 589828
  13.1 29.8 %collective-permute-start.4 = (bf16[128,768]{1,0:T(8,128)(2,1)S(1)}, bf16[128,768]{1,0:T(8,128)(2,1)S(1)}, u32[]{:S(2)}, u32[]{:S(2)}) collective-permute-start(bf16[128,768]{1,0:T(8,128)(2,1)S(1)} %get-tuple-element.86), channel_id=1, source_target_pairs={{4,20},{12,28},{20,4},{28,12},{0,16},{8,24},{16,0},{24,8},{5,21},{... | collective-permute-start | bytes 589832 | tf_op jit(solution)/shard_map/ppermute | solution.py:112
  34.2 0.7 copy-start.18
  34.2 8.7 %collective-permute-start.5 = (bf16[128,768]{1,0:T(8,128)(2,1)S(1)}, bf16[128,768]{1,0:T(8,128)(2,1)S(1)}, u32[]{:S(2)}, u32[]{:S(2)}) collective-permute-start(bf16[128,768]{1,0:T(8,128)(2,1)S(1)} %get-tuple-element.87), channel_id=1, source_target_pairs={{0,4},{4,24},{8,12},{12,0},{16,20},{20,8},{24,28},{28,16},{1,5},{5... | collective-permute-start | bytes 589832 | tf_op jit(solution)/shard_map/ppermute | solution.py:112
  34.2 0.7 copy-start.19
  34.2 8.7 %collective-permute-start.6 = (bf16[128,768]{1,0:T(8,128)(2,1)S(1)}, bf16[128,768]{1,0:T(8,128)(2,1)S(1)}, u32[]{:S(2)}, u32[]{:S(2)}) collective-permute-start(bf16[128,768]{1,0:T(8,128)(2,1)S(1)} %get-tuple-element.88), channel_id=1, source_target_pairs={{0,8},{4,28},{8,16},{12,4},{16,24},{20,12},{24,0},{28,20},{1,9},{5... | collective-permute-start | bytes 589832 | tf_op jit(solution)/shard_map/ppermute | solution.py:112
  34.7 0.7 copy-start.21
  42.9 0.7 copy-start.24
  42.9 0.7 copy-start.25
  42.9 0.8 copy-start.26
  42.9 0.8 copy-start.27
  58.4 8.8 %collective-permute-start.12 = (bf16[1552,384]{1,0:T(8,128)(2,1)}, bf16[1552,384]{1,0:T(8,128)(2,1)S(1)}, u32[]{:S(2)}, u32[]{:S(2)}) collective-permute-start(bf16[1552,384]{1,0:T(8,128)(2,1)} %get-tuple-element.59), channel_id=1, source_target_pairs={{0,1},{1,0},{2,3},{3,2},{4,5},{5,4},{6,7},{7,6},{8,9},{9,8},{10,11... | collective-permute-start | bytes 3575816 | tf_op jit(solution)/shard_map/ppermute | solution.py:449
  58.5 8.7 %collective-permute-start.13 = (bf16[1552,384]{1,0:T(8,128)(2,1)}, bf16[1552,384]{1,0:T(8,128)(2,1)S(1)}, u32[]{:S(2)}, u32[]{:S(2)}) collective-permute-start(bf16[1552,384]{1,0:T(8,128)(2,1)} %get-tuple-element.61), channel_id=1, source_target_pairs={{0,1},{1,0},{2,3},{3,2},{4,5},{5,4},{6,7},{7,6},{8,9},{9,8},{10,11... | collective-permute-start | bytes 3575816 | tf_op jit(solution)/shard_map/ppermute | solution.py:449
  59.0 8.2 %collective-permute-start.11 = (bf16[128,768]{1,0:T(8,128)(2,1)}, bf16[128,768]{1,0:T(8,128)(2,1)S(1)}, u32[]{:S(2)}, u32[]{:S(2)}) collective-permute-start(bf16[128,768]{1,0:T(8,128)(2,1)} %get-tuple-element.55), channel_id=1, source_target_pairs={{12,0},{0,4},{20,8},{8,12},{28,16},{16,20},{4,24},{24,28},{13,1},{... | collective-permute-start | bytes 589832 | tf_op jit(solution)/shard_map/ppermute | solution.py:117
  67.2 0.7 copy-start.13
  67.2 1.1 copy-start
  67.2 1.5 %copy-start.2 = (bf16[1552,384]{1,0:T(8,128)(2,1)}, bf16[1552,384]{1,0:T(8,128)(2,1)S(1)}, u32[]{:S(2)}) copy-start(bf16[1552,384]{1,0:T(8,128)(2,1)S(1)} %collective-permute-done.13.refs_5_.refs_6_.came_b) | copy-start | bytes 3575812
  68.7 6.8 %copy-start.23 = (bf16[128,768]{1,0:T(8,128)(2,1)S(1)}, bf16[128,768]{1,0:T(8,128)(2,1)}, u32[]{:S(2)}) copy-start(bf16[128,768]{1,0:T(8,128)(2,1)} %get-tuple-element.52) | copy-start | bytes 589828
  68.7 7.7 %copy-start.22 = (bf16[128,768]{1,0:T(8,128)(2,1)S(1)}, bf16[128,768]{1,0:T(8,128)(2,1)}, u32[]{:S(2)}) copy-start(bf16[128,768]{1,0:T(8,128)(2,1)} %get-tuple-element.53) | copy-start | bytes 589828
  68.7 11.4 %copy-start.20 = (bf16[128,768]{1,0:T(8,128)(2,1)S(1)}, bf16[128,768]{1,0:T(8,128)(2,1)}, u32[]{:S(2)}) copy-start(bf16[128,768]{1,0:T(8,128)(2,1)} %get-tuple-element.54) | copy-start | bytes 589828
  68.7 12.9 %copy-start.4 = (bf16[1536,384]{1,0:T(8,128)(2,1)S(1)}, bf16[1536,384]{1,0:T(8,128)(2,1)}, u32[]{:S(2)}) copy-start(bf16[1536,384]{1,0:T(8,128)(2,1)} %get-tuple-element.60.refs_4_.kept_b) | copy-start | bytes 3538948
  68.7 12.9 %copy-start.5 = (bf16[1536,384]{1,0:T(8,128)(2,1)S(1)}, bf16[1536,384]{1,0:T(8,128)(2,1)}, u32[]{:S(2)}) copy-start(bf16[1536,384]{1,0:T(8,128)(2,1)} %get-tuple-element.58.refs_1_.kept_a) | copy-start | bytes 3538948
  71.7 21.4 %collective-permute-start.14 = (bf16[784,384]{1,0:T(8,128)(2,1)}, bf16[784,384]{1,0:T(8,128)(2,1)S(1)}, u32[]{:S(2)}, u32[]{:S(2)}) collective-permute-start(bf16[784,384]{1,0:T(8,128)(2,1)} %get-tuple-element.64), channel_id=1, source_target_pairs={{0,4},{4,0},{8,12},{12,8},{16,20},{20,16},{24,28},{28,24},{1,5},{5... | collective-permute-start | bytes 1806344 | tf_op jit(solution)/shard_map/ppermute | solution.py:449
  74.0 19.1 %collective-permute-start.15 = (bf16[784,384]{1,0:T(8,128)(2,1)}, bf16[784,384]{1,0:T(8,128)(2,1)S(1)}, u32[]{:S(2)}, u32[]{:S(2)}) collective-permute-start(bf16[784,384]{1,0:T(8,128)(2,1)} %get-tuple-element.66), channel_id=1, source_target_pairs={{0,2},{1,3},{2,0},{3,1},{4,6},{5,7},{6,4},{7,5},{8,10},{9,11},{10,... | collective-permute-start | bytes 1806344 | tf_op jit(solution)/shard_map/ppermute | solution.py:449
  75.5 15.1 %collective-permute-start.8 = (bf16[128,768]{1,0:T(8,128)(2,1)S(1)}, bf16[128,768]{1,0:T(8,128)(2,1)S(1)}, u32[]{:S(2)}, u32[]{:S(2)}) collective-permute-start(bf16[128,768]{1,0:T(8,128)(2,1)S(1)} %copy-done.23), channel_id=1, source_target_pairs={{20,4},{28,12},{4,20},{12,28},{16,0},{24,8},{0,16},{8,24},{21,5},{... | collective-permute-start | bytes 589832 | tf_op jit(solution)/shard_map/ppermute | solution.py:117
  76.4 15.0 %collective-permute-start.9 = (bf16[128,768]{1,0:T(8,128)(2,1)S(1)}, bf16[128,768]{1,0:T(8,128)(2,1)S(1)}, u32[]{:S(2)}, u32[]{:S(2)}) collective-permute-start(bf16[128,768]{1,0:T(8,128)(2,1)S(1)} %copy-done.22), channel_id=1, source_target_pairs={{4,0},{24,4},{12,8},{0,12},{20,16},{8,20},{28,24},{16,28},{5,1},{2... | collective-permute-start | bytes 589832 | tf_op jit(solution)/shard_map/ppermute | solution.py:117
  80.1 13.0 %collective-permute-start.10 = (bf16[128,768]{1,0:T(8,128)(2,1)S(1)}, bf16[128,768]{1,0:T(8,128)(2,1)S(1)}, u32[]{:S(2)}, u32[]{:S(2)}) collective-permute-start(bf16[128,768]{1,0:T(8,128)(2,1)S(1)} %copy-done.20), channel_id=1, source_target_pairs={{8,0},{28,4},{16,8},{4,12},{24,16},{12,20},{0,24},{20,28},{9,1},{2... | collective-permute-start | bytes 589832 | tf_op jit(solution)/shard_map/ppermute | solution.py:117
  81.6 1.3 copy-start.1
  82.9 1.3 copy-start.3
  84.2 8.9 %copy-start.10 = (f32[4,384]{1,0:T(4,128)S(1)}, f32[4,384]{1,0:T(4,128)}, u32[]{:S(2)}) copy-start(f32[4,384]{1,0:T(4,128)} %get-tuple-element.62.refs_0_) | copy-start | bytes 18436
  90.7 2.6 %copy-start.6 = (bf16[128,768]{1,0:T(8,128)(2,1)}, bf16[128,768]{1,0:T(8,128)(2,1)S(1)}, u32[]{:S(2)}) copy-start(bf16[128,768]{1,0:T(8,128)(2,1)S(1)} %collective-permute-done.8.refs_0_.refs_7_) | copy-start | bytes 589828
  91.5 1.8 %copy-start.7 = (bf16[128,768]{1,0:T(8,128)(2,1)}, bf16[128,768]{1,0:T(8,128)(2,1)S(1)}, u32[]{:S(2)}) copy-start(bf16[128,768]{1,0:T(8,128)(2,1)S(1)} %collective-permute-done.9.refs_1_.refs_8_) | copy-start | bytes 589828
  93.1 0.7 copy-start.8
  93.8 7.8 %collective-permute-start.16 = (bf16[400,384]{1,0:T(8,128)(2,1)S(1)}, bf16[400,384]{1,0:T(8,128)(2,1)S(1)}, u32[]{:S(2)}, u32[]{:S(2)}) collective-permute-start(bf16[400,384]{1,0:T(8,128)(2,1)S(1)} %get-tuple-element.68), channel_id=1, source_target_pairs={{0,2},{1,3},{2,0},{3,1},{4,6},{5,7},{6,4},{7,5},{8,10},{9,11},{10,... | collective-permute-start | bytes 921608 | tf_op jit(solution)/shard_map/ppermute | solution.py:449
  94.3 7.5 %collective-permute-start.17 = (bf16[400,384]{1,0:T(8,128)(2,1)S(1)}, bf16[400,384]{1,0:T(8,128)(2,1)S(1)}, u32[]{:S(2)}, u32[]{:S(2)}) collective-permute-start(bf16[400,384]{1,0:T(8,128)(2,1)S(1)} %get-tuple-element.69), channel_id=1, source_target_pairs={{0,4},{4,0},{8,12},{12,8},{16,20},{20,16},{24,28},{28,24},{1,5},{5... | collective-permute-start | bytes 921608 | tf_op jit(solution)/shard_map/ppermute | solution.py:449
  102.1 8.5 %collective-permute-start.18 = (bf16[208,384]{1,0:T(8,128)(2,1)S(1)}, bf16[208,384]{1,0:T(8,128)(2,1)S(1)}, u32[]{:S(2)}, u32[]{:S(2)}) collective-permute-start(bf16[208,384]{1,0:T(8,128)(2,1)S(1)} %get-tuple-element.72), channel_id=1, source_target_pairs={{0,8},{4,12},{8,0},{12,4},{16,24},{20,28},{24,16},{28,20},{1,9},{5... | collective-permute-start | bytes 479240 | tf_op jit(solution)/shard_map/ppermute | solution.py:449
  105.4 14.0 %collective-permute-start.19 = (bf16[208,384]{1,0:T(8,128)(2,1)S(1)}, bf16[208,384]{1,0:T(8,128)(2,1)S(1)}, u32[]{:S(2)}, u32[]{:S(2)}) collective-permute-start(bf16[208,384]{1,0:T(8,128)(2,1)S(1)} %get-tuple-element.73), channel_id=1, source_target_pairs={{0,16},{4,20},{8,24},{12,28},{16,0},{20,4},{24,8},{28,12},{1,17},{... | collective-permute-start | bytes 479240 | tf_op jit(solution)/shard_map/ppermute | solution.py:449
  106.1 13.3 %collective-permute-start.20 = (bf16[208,384]{1,0:T(8,128)(2,1)S(1)}, bf16[208,384]{1,0:T(8,128)(2,1)S(1)}, u32[]{:S(2)}, u32[]{:S(2)}) collective-permute-start(bf16[208,384]{1,0:T(8,128)(2,1)S(1)} %get-tuple-element.74), channel_id=1, source_target_pairs={{0,24},{4,28},{8,16},{12,20},{16,8},{20,12},{24,0},{28,4},{1,25},{... | collective-permute-start | bytes 479240 | tf_op jit(solution)/shard_map/ppermute | solution.py:449
  119.5 0.6 copy-start.11
  120.1 7.5 %copy-start.9 = (bf16[192,384]{1,0:T(8,128)(2,1)}, bf16[192,384]{1,0:T(8,128)(2,1)S(1)}, u32[]{:S(2)}) copy-start(bf16[192,384]{1,0:T(8,128)(2,1)S(1)} %get-tuple-element.76.refs_0_) | copy-start | bytes 442372
  120.1 5.1 %collective-permute-start.21 = (bf16[192,384]{1,0:T(8,128)(2,1)S(1)}, bf16[192,384]{1,0:T(8,128)(2,1)S(1)}, u32[]{:S(2)}, u32[]{:S(2)}) collective-permute-start(bf16[192,384]{1,0:T(8,128)(2,1)S(1)} %get-tuple-element.76.refs_0_), channel_id=1, source_target_pairs={{0,2},{1,3},{2,0},{3,1},{4,6},{5,7},{6,4},{7,5},{8,10},{9,11},{10,... | collective-permute-start | bytes 442376 | tf_op jit(solution)/shard_map/ppermute | solution.py:449
  121.5 6.1 %collective-permute-start.22 = (bf16[192,384]{1,0:T(8,128)(2,1)S(1)}, bf16[192,384]{1,0:T(8,128)(2,1)S(1)}, u32[]{:S(2)}, u32[]{:S(2)}) collective-permute-start(bf16[192,384]{1,0:T(8,128)(2,1)S(1)} %get-tuple-element.76.refs_0_), channel_id=1, source_target_pairs={{0,1},{1,0},{2,3},{3,2},{4,5},{5,4},{6,7},{7,6},{8,9},{9,8},{10,11... | collective-permute-start | bytes 442376 | tf_op jit(solution)/shard_map/ppermute | solution.py:449
  125.2 2.4 %copy-start.14 = (bf16[192,384]{1,0:T(8,128)(2,1)}, bf16[192,384]{1,0:T(8,128)(2,1)S(1)}, u32[]{:S(2)}) copy-start(bf16[192,384]{1,0:T(8,128)(2,1)S(1)} %collective-permute-done.21.refs_1_) | copy-start | bytes 442372
  125.2 2.4 %collective-permute-start.23 = (bf16[192,384]{1,0:T(8,128)(2,1)S(1)}, bf16[192,384]{1,0:T(8,128)(2,1)S(1)}, u32[]{:S(2)}, u32[]{:S(2)}) collective-permute-start(bf16[192,384]{1,0:T(8,128)(2,1)S(1)} %collective-permute-done.21.refs_1_), channel_id=1, source_target_pairs={{0,1},{1,0},{2,3},{3,2},{4,5},{5,4},{6,7},{7,6},{8,9},{9,8},{10,11... | collective-permute-start | bytes 442376 | tf_op jit(solution)/shard_map/ppermute | solution.py:449
  127.6 0.7 copy-start.15
  127.6 0.7 copy-start.16

commit v4 on v3

--- a/solution.py
+++ b/solution.py
@@ -163,8 +163,6 @@
     rows, width = pre_a.shape
     load_taps = fetch(taps_hbm, taps, sems.at[units])
     came = fetch_units(routes, field, slots, inputs, sems, 0)
-    load_point = fetch(point_hbm, point, sems.at[units + 1])
-    load_taps_b = fetch(taps_b_hbm, taps_b, sems.at[units + 2])
 
     def block(field, taps, scale_ref, offset_ref, pre, act, shift):
         pre[...] = dot(field[...], taps[1])
@@ -183,6 +181,8 @@
 
     wait_all(came)
     load_taps.wait()
+    load_point = fetch(point_hbm, point, sems.at[units + 1])
+    load_taps_b = fetch(taps_b_hbm, taps_b, sems.at[units + 2])
     block(inputs, taps, scale_a, offset_a, pre_a, act_a, shifts[0])
     left = [leave(0, pre_a), leave(1, act_a)]
     load_point.wait()
@@ -268,15 +268,22 @@
 
     came_g = fetch_units(routes, g_field, g_slots, g_b, sems, 0)
     loads_b = [load(0, point_b_hbm, point_b), load(1, pre_b_hbm, pre_b)]
-    came_second = [load(2, second_hbm, u_b)]
-    loads_b += [load(3, act_b_hbm, act_b), load(4, taps_b_hbm, taps_b)]
-    loads_a = [load(5, point_a_hbm, point_a), load(6, pre_a_hbm, pre_a)]
-    came_u = fetch_units(routes, u_field, u_slots, u_a, sems, units)
-    loads_a += [load(7, act_a_hbm, act_a), load(8, taps_a_hbm, taps_a)]
+    came_second, loads_a, came_u = [], [], []
+
+    def load_rest_b():
+        came_second.append(load(2, second_hbm, u_b))
+        loads_b.extend([load(3, act_b_hbm, act_b), load(4, taps_b_hbm, taps_b)])
+
+    def load_a():
+        loads_a.extend([load(5, point_a_hbm, point_a), load(6, pre_a_hbm, pre_a)])
+        came_u.extend(fetch_units(routes, u_field, u_slots, u_a, sems, units))
+        loads_a.extend([load(7, act_a_hbm, act_a), load(8, taps_a_hbm, taps_a)])
 
     def block(index, u, g, pre, act, taps, point, loads, came, scale_ref, offset_ref, shift, kept, sent):
         scale, offset = scale_ref[...][None, :], offset_ref[...][None, :]
         loads[0].wait()
+        if index == 1:
+            load_rest_b()
         grad_act[...] = across(g[...], point[...])
         sums[...] = jnp.zeros_like(sums)
         steps, step = row_parts(rows)
@@ -292,6 +299,8 @@
             sums[0] += jnp.sum((grad_norm * value).reshape(step // 8, 8, width), 0)
             sums[1] += jnp.sum(grad_norm.reshape(step // 8, 8, width), 0)
 
+        if index == 1:
+            load_a()
         norms = jnp.sum(sums[...], 1)
         norms_ref[2 * index : 2 * index + 2, :] = norms
         norm_rows[index] = split_norms(norms)

time: 131 us -> 131 us (level)
  no operation moved by 1% of the time
where the time goes in v4:
time: 131 us
  waiting for transfers between devices  55.1 us (42%)
  starting transfers between devices  35.3 us (27%)
  Pallas kernels  30.5 us (23%)
  local copies, waits for them, and re-layouts  7.35 us (6%)
  other arithmetic  1.47 us (1%)
    ppermute x12, waiting for transfers between devices, trade(): lax.ppermute(value, axis, [(i, i ^ bits) for i in range(lax.axis_size(axi...  22.1 us
    ppermute x8, waiting for transfers between devices, out(): lax.ppermute(part, 'seq', [(i, t) for i, (_, t, _) in permute.items()])  19.7 us
    pallas_call x1, Pallas kernels, reverse(): pl.pallas_call(functools.partial(reverse_kernel, routes, count, shifts),...  14.6 us
    ppermute x4, waiting for transfers between devices, back(): lax.ppermute(part, 'seq', [(t, i) for i, (_, t, _) in permute.items()])  13.3 us
    ppermute x12, starting transfers between devices, trade(): lax.ppermute(value, axis, [(i, i ^ bits) for i in range(lax.axis_size(axi...  12.9 us
    ppermute x8, starting transfers between devices, out(): lax.ppermute(part, 'seq', [(i, t) for i, (_, t, _) in permute.items()])  12.9 us
    ppermute x4, starting transfers between devices, back(): lax.ppermute(part, 'seq', [(t, i) for i, (_, t, _) in permute.items()])  9.57 us
    pallas_call x1, Pallas kernels, ahead(): pl.pallas_call(functools.partial(ahead_kernel, routes, shifts), out_shape...  7.45 us
  transfers between devices with their start and end apart: 24, of which 10 were waited for; matrix products, arithmetic and copies ran while one was open for 0% of the time, Pallas kernels for 8%

profile of v4, /device:TPU:0, one launch (start us, length us, event | category | flops | bytes accessed | tf_op | source)
XLA Modules:
  0.0 130.7 jit_solution(9137436609501818345)
XLA Ops:
  0.6 0.0 copy-start.12
  0.7 1.4 %slice_bitcast_fusion.3 = (bf16[128,768]{1,0:T(8,128)(2,1)S(1)}, bf16[128,768]{1,0:T(8,128)(2,1)S(1)}, bf16[128,768]{1,0:T(8,128)(2,1)S(1)}, bf16[128,768]{1,0:T(8,128)(2,1)S(1)}) fusion(bf16[1,640,768]{2,1,0:T(8,128)(2,1)} %param.10, pred[]{:T(512)S(6)} %eq.39), kind=kLoop, calls=%fused_computation.4 | loop fusion | flops 98304 | bytes 1769473 | tf_op jit(solution)/shard_map/slice | solution.py:108
  2.1 4.0 %collective-permute-start.3 = (bf16[128,768]{1,0:T(8,128)(2,1)S(1)}, bf16[128,768]{1,0:T(8,128)(2,1)S(1)}, u32[]{:S(2)}, u32[]{:S(2)}) collective-permute-start(bf16[128,768]{1,0:T(8,128)(2,1)S(1)} %get-tuple-element.89), channel_id=1, source_target_pairs={{0,12},{4,0},{8,20},{12,8},{16,28},{20,16},{24,4},{28,24},{1,13},{... | collective-permute-start | bytes 589832 | tf_op jit(solution)/shard_map/ppermute | solution.py:112
  6.1 2.6 %collective-permute-start = (bf16[128,768]{1,0:T(8,128)(2,1)S(1)}, bf16[128,768]{1,0:T(8,128)(2,1)S(1)}, u32[]{:S(2)}, u32[]{:S(2)}) collective-permute-start(bf16[128,768]{1,0:T(8,128)(2,1)S(1)} %get-tuple-element.90), channel_id=1, source_target_pairs={{4,20},{12,28},{20,4},{28,12},{0,16},{8,24},{16,0},{24,8},{5,21},{... | collective-permute-start | bytes 589832 | tf_op jit(solution)/shard_map/ppermute | solution.py:112
  8.7 0.0 collective-permute-start.1
  8.7 1.1 collective-permute-start.2
  9.8 0.1 slice_bitcast_fusion
  9.9 3.3 %collective-permute-start.7 = (bf16[128,768]{1,0:T(8,128)(2,1)S(1)}, bf16[128,768]{1,0:T(8,128)(2,1)S(1)}, u32[]{:S(2)}, u32[]{:S(2)}) collective-permute-start(bf16[128,768]{1,0:T(8,128)(2,1)S(1)} %get-tuple-element.85), channel_id=1, source_target_pairs={{0,12},{4,0},{8,20},{12,8},{16,28},{20,16},{24,4},{28,24},{1,13},{... | collective-permute-start | bytes 589832 | tf_op jit(solution)/shard_map/ppermute | solution.py:112
  13.1 0.0 collective-permute-done.3.refs_4_
  13.1 1.4 %collective-permute-start.4 = (bf16[128,768]{1,0:T(8,128)(2,1)S(1)}, bf16[128,768]{1,0:T(8,128)(2,1)S(1)}, u32[]{:S(2)}, u32[]{:S(2)}) collective-permute-start(bf16[128,768]{1,0:T(8,128)(2,1)S(1)} %get-tuple-element.86), channel_id=1, source_target_pairs={{4,20},{12,28},{20,4},{28,12},{0,16},{8,24},{16,0},{24,8},{5,21},{... | collective-permute-start | bytes 589832 | tf_op jit(solution)/shard_map/ppermute | solution.py:112
  14.5 19.7 %collective-permute-done.refs_1_ = bf16[128,768]{1,0:T(8,128)(2,1)S(1)} collective-permute-done((bf16[128,768]{1,0:T(8,128)(2,1)S(1)}, bf16[128,768]{1,0:T(8,128)(2,1)S(1)}, u32[]{:S(2)}, u32[]{:S(2)}) %collective-permute-start) | collective-permute-done | bytes 196640 | tf_op jit(solution)/shard_map/ppermute | solution.py:112
  34.2 0.0 collective-permute-done.1.refs_2_
  34.2 0.0 copy-start.19
  34.2 0.5 collective-permute-start.6
  34.7 0.1 copy-done.18
  34.8 0.1 copy-done.19
  34.9 0.5 copy-done.21
  35.4 7.5 %shard_map.169 = (f32[640,384]{1,0:T(8,128)}, bf16[640,384]{1,0:T(8,128)(2,1)}, bf16[640,768]{1,0:T(8,128)(2,1)}, f32[640,384]{1,0:T(8,128)}, bf16[640,384]{1,0:T(8,128)(2,1)}) custom-call(bf16[640,768]{1,0:T(8,128)(2,1)} %bitcast.21, bf16[128,768]{1,0:T(8,128)(2,1)} %copy-done.18, bf16[128,768]{1,0:T(8,128)(2,1)} %copy-done.19, ...), custom_call_target="tpu_custom_call" | custom-call | flops 1887436800 | bytes 10485760 | tf_op jit(solution)/shard_map/pallas_call | solution.py:202
  42.9 0.0 collective-permute-done.4.refs_6_
  42.9 0.0 collective-permute-done.5.refs_7_
  42.9 0.6 copy-done.24
  43.6 0.1 copy-done.25
  43.6 0.1 copy-done.26
  43.7 0.1 copy-done.27
  43.8 14.6 %shard_map.170 = (bf16[128,768]{1,0:T(8,128)(2,1)}, bf16[128,768]{1,0:T(8,128)(2,1)}, bf16[128,768]{1,0:T(8,128)(2,1)}, bf16[128,768]{1,0:T(8,128)(2,1)}, bf16[1...) custom-call(bf16[640,768]{1,0:T(8,128)(2,1)} %bitcast.22, ...), custom_call_target="tpu_custom_call" | custom-call | flops 4152360960 | bytes 18874368 | tf_op jit(solution)/shard_map/pallas_call | solution.py:396
  58.4 0.1 collective-permute-start.12
  58.5 0.5 collective-permute-start.13
  59.0 3.5 %collective-permute-start.11 = (bf16[128,768]{1,0:T(8,128)(2,1)}, bf16[128,768]{1,0:T(8,128)(2,1)S(1)}, u32[]{:S(2)}, u32[]{:S(2)}) collective-permute-start(bf16[128,768]{1,0:T(8,128)(2,1)} %get-tuple-element.55), channel_id=1, source_target_pairs={{12,0},{0,4},{20,8},{8,12},{28,16},{16,20},{4,24},{24,28},{13,1},{... | collective-permute-start | bytes 589832 | tf_op jit(solution)/shard_map/ppermute | solution.py:117
  62.5 4.7 %collective-permute-done.11.refs_3_.refs_7_ = bf16[128,768]{1,0:T(8,128)(2,1)S(1)} collective-permute-done((bf16[128,768]{1,0:T(8,128)(2,1)}, bf16[128,768]{1,0:T(8,128)(2,1)S(1)}, u32[]{:S(2)}, u32[]{:S(2)}) %collective-permute-start.11) | collective-permute-done | bytes 196640 | tf_op jit(solution)/shard_map/ppermute | solution.py:117
  67.2 0.7 copy-done.13
  67.9 0.4 copy-done
  68.3 0.4 copy-done.2
  68.7 3.0 %shard_map.172 = (bf16[784,384]{1,0:T(8,128)(2,1)}, bf16[784,384]{1,0:T(8,128)(2,1)}, f32[4,384]{1,0:T(4,128)}) custom-call(f32[4,384]{1,0:T(4,128)} %get-tuple-element.57.refs_0_, bf16[1536,384]{1,0:T(8,128)(2,1)} %get-tuple-element.58.refs_1_.kept_a, bf16[1552,384]{1,0:T(8,128)(2,1)} %copy-done, bf16[1552,384]{1,0:T(8,128)(2,1)} %copy-done, ...), custom_call_target="tpu_custom_call" | custom-call | bytes 4718592 | tf_op jit(solution)/shard_map/pallas_call | solution.py:496
  71.7 2.4 %collective-permute-start.14 = (bf16[784,384]{1,0:T(8,128)(2,1)}, bf16[784,384]{1,0:T(8,128)(2,1)S(1)}, u32[]{:S(2)}, u32[]{:S(2)}) collective-permute-start(bf16[784,384]{1,0:T(8,128)(2,1)} %get-tuple-element.64), channel_id=1, source_target_pairs={{0,4},{4,0},{8,12},{12,8},{16,20},{20,16},{24,28},{28,24},{1,5},{5... | collective-permute-start | bytes 1806344 | tf_op jit(solution)/shard_map/ppermute | solution.py:458
  74.0 1.5 %collective-permute-start.15 = (bf16[784,384]{1,0:T(8,128)(2,1)}, bf16[784,384]{1,0:T(8,128)(2,1)S(1)}, u32[]{:S(2)}, u32[]{:S(2)}) collective-permute-start(bf16[784,384]{1,0:T(8,128)(2,1)} %get-tuple-element.66), channel_id=1, source_target_pairs={{0,2},{1,3},{2,0},{3,1},{4,6},{5,7},{6,4},{7,5},{8,10},{9,11},{10,... | collective-permute-start | bytes 1806344 | tf_op jit(solution)/shard_map/ppermute | solution.py:458
  75.5 0.9 collective-permute-start.8
  76.4 3.7 %collective-permute-start.9 = (bf16[128,768]{1,0:T(8,128)(2,1)S(1)}, bf16[128,768]{1,0:T(8,128)(2,1)S(1)}, u32[]{:S(2)}, u32[]{:S(2)}) collective-permute-start(bf16[128,768]{1,0:T(8,128)(2,1)S(1)} %copy-done.22), channel_id=1, source_target_pairs={{4,0},{24,4},{12,8},{0,12},{20,16},{8,20},{28,24},{16,28},{5,1},{2... | collective-permute-start | bytes 589832 | tf_op jit(solution)/shard_map/ppermute | solution.py:117
  80.1 1.5 %collective-permute-start.10 = (bf16[128,768]{1,0:T(8,128)(2,1)S(1)}, bf16[128,768]{1,0:T(8,128)(2,1)S(1)}, u32[]{:S(2)}, u32[]{:S(2)}) collective-permute-start(bf16[128,768]{1,0:T(8,128)(2,1)S(1)} %copy-done.20), channel_id=1, source_target_pairs={{8,0},{28,4},{16,8},{4,12},{24,16},{12,20},{0,24},{20,28},{9,1},{2... | collective-permute-start | bytes 589832 | tf_op jit(solution)/shard_map/ppermute | solution.py:117
  81.6 1.3 copy-done.1
  82.9 1.3 copy-done.3
  84.2 0.3 shard_map.173
  84.5 6.2 %collective-permute-done.8.refs_0_.refs_7_ = bf16[128,768]{1,0:T(8,128)(2,1)S(1)} collective-permute-done((bf16[128,768]{1,0:T(8,128)(2,1)S(1)}, bf16[128,768]{1,0:T(8,128)(2,1)S(1)}, u32[]{:S(2)}, u32[]{:S(2)}) %collective-permute-start.8) | collective-permute-done | bytes 196640 | tf_op jit(solution)/shard_map/ppermute | solution.py:117
  90.7 0.8 collective-permute-done.9.refs_1_.refs_8_
  91.5 1.6 %collective-permute-done.10.refs_2_.refs_9_ = bf16[128,768]{1,0:T(8,128)(2,1)S(1)} collective-permute-done((bf16[128,768]{1,0:T(8,128)(2,1)S(1)}, bf16[128,768]{1,0:T(8,128)(2,1)S(1)}, u32[]{:S(2)}, u32[]{:S(2)}) %collective-permute-start.10) | collective-permute-done | bytes 196640 | tf_op jit(solution)/shard_map/ppermute | solution.py:117
  93.1 0.2 shard_map.174
  93.3 0.5 copy-done.8
  93.8 0.5 collective-permute-start.16
  94.3 0.7 collective-permute-start.17
  95.0 6.6 %collective-permute-done.16.refs_2_.refs_3_ = bf16[400,384]{1,0:T(8,128)(2,1)S(1)} collective-permute-done((bf16[400,384]{1,0:T(8,128)(2,1)S(1)}, bf16[400,384]{1,0:T(8,128)(2,1)S(1)}, u32[]{:S(2)}, u32[]{:S(2)}) %collective-permute-start.16) | collective-permute-done | bytes 307232 | tf_op jit(solution)/shard_map/ppermute | solution.py:458
  101.6 0.3 collective-permute-done.17.refs_6_.refs_7_
  101.8 0.2 shard_map.175
  102.1 3.4 %collective-permute-start.18 = (bf16[208,384]{1,0:T(8,128)(2,1)S(1)}, bf16[208,384]{1,0:T(8,128)(2,1)S(1)}, u32[]{:S(2)}, u32[]{:S(2)}) collective-permute-start(bf16[208,384]{1,0:T(8,128)(2,1)S(1)} %get-tuple-element.72), channel_id=1, source_target_pairs={{0,8},{4,12},{8,0},{12,4},{16,24},{20,28},{24,16},{28,20},{1,9},{5... | collective-permute-start | bytes 479240 | tf_op jit(solution)/shard_map/ppermute | solution.py:458
  105.4 0.6 collective-permute-start.19
  106.1 1.8 %collective-permute-start.20 = (bf16[208,384]{1,0:T(8,128)(2,1)S(1)}, bf16[208,384]{1,0:T(8,128)(2,1)S(1)}, u32[]{:S(2)}, u32[]{:S(2)}) collective-permute-start(bf16[208,384]{1,0:T(8,128)(2,1)S(1)} %get-tuple-element.74), channel_id=1, source_target_pairs={{0,24},{4,28},{8,16},{12,20},{16,8},{20,12},{24,0},{28,4},{1,25},{... | collective-permute-start | bytes 479240 | tf_op jit(solution)/shard_map/ppermute | solution.py:458
  107.9 2.6 %collective-permute-done.18.refs_0_ = bf16[208,384]{1,0:T(8,128)(2,1)S(1)} collective-permute-done((bf16[208,384]{1,0:T(8,128)(2,1)S(1)}, bf16[208,384]{1,0:T(8,128)(2,1)S(1)}, u32[]{:S(2)}, u32[]{:S(2)}) %collective-permute-start.18) | collective-permute-done | bytes 159776 | tf_op jit(solution)/shard_map/ppermute | solution.py:458
  110.5 8.9 %collective-permute-done.19.refs_1_ = bf16[208,384]{1,0:T(8,128)(2,1)S(1)} collective-permute-done((bf16[208,384]{1,0:T(8,128)(2,1)S(1)}, bf16[208,384]{1,0:T(8,128)(2,1)S(1)}, u32[]{:S(2)}, u32[]{:S(2)}) %collective-permute-start.19) | collective-permute-done | bytes 159776 | tf_op jit(solution)/shard_map/ppermute | solution.py:458
  119.4 0.1 shard_map.176
  119.5 0.6 copy-done.11
  120.1 1.4 %collective-permute-start.21 = (bf16[192,384]{1,0:T(8,128)(2,1)S(1)}, bf16[192,384]{1,0:T(8,128)(2,1)S(1)}, u32[]{:S(2)}, u32[]{:S(2)}) collective-permute-start(bf16[192,384]{1,0:T(8,128)(2,1)S(1)} %get-tuple-element.76.refs_0_), channel_id=1, source_target_pairs={{0,2},{1,3},{2,0},{3,1},{4,6},{5,7},{6,4},{7,5},{8,10},{9,11},{10,... | collective-permute-start | bytes 442376 | tf_op jit(solution)/shard_map/ppermute | solution.py:458
  121.5 3.7 %collective-permute-done.21.refs_1_ = bf16[192,384]{1,0:T(8,128)(2,1)S(1)} collective-permute-done((bf16[192,384]{1,0:T(8,128)(2,1)S(1)}, bf16[192,384]{1,0:T(8,128)(2,1)S(1)}, u32[]{:S(2)}, u32[]{:S(2)}) %collective-permute-start.21) | collective-permute-done | bytes 147488 | tf_op jit(solution)/shard_map/ppermute | solution.py:458
  125.2 2.3 %shard_map.171 = bf16[640,768]{1,0:T(8,128)(2,1)} custom-call(bf16[128,768]{1,0:T(8,128)(2,1)} %copy-done.6, bf16[128,768]{1,0:T(8,128)(2,1)} %copy-done.7, bf16[128,768]{1,0:T(8,128)(2,1)} %copy-done.8, bf16[128,768]{1,0:T(8,128)(2,1)} %copy-done.13, bf16[128,768]{1,0:T(8,128)(2,1)} %get-tuple-element.56.refs_4_), custom_call_target="tpu_custom_call" | custom-call | bytes 2097152 | tf_op jit(solution)/shard_map/pallas_call | solution.py:448
  127.6 0.6 copy-done.15
  128.2 0.1 copy-done.16
  128.3 2.4 %shard_map.177 = (f32[3,96,384]{2,1,0:T(8,128)}, f32[96,384]{1,0:T(8,128)}, f32[3,96,384]{2,1,0:T(8,128)}, f32[96,384]{1,0:T(8,128)}, f32[384]{0:T(512)}, /*index=5*/f32[384]{0:T(512)}, f32[384]{0:T(512)}, f32[384]{0:T(512)}) custom-call(f32[4,384]{1,0:T(4,128)} %copy-done.11, bf16[192,384]{1,0:T(8,128)(2,1)} %copy-done.9, bf16[192,384]{1,0:T(8,128)(2,1)} %copy-done.14, ...), custom_call_target="tpu_custom_call" | custom-call | bytes 2097152 | tf_op jit(solution)/shard_map/pallas_call | solution.py:621
  (51 shorter events, 0.1 us)
Async XLA Ops:
  0.6 9.2 %copy-start.12 = (bf16[1,640,768]{2,1,0:T(8,128)(2,1)S(1)}, bf16[1,640,768]{2,1,0:T(8,128)(2,1)}, u32[]{:S(2)}) copy-start(bf16[1,640,768]{2,1,0:T(8,128)(2,1)} %param.19) | copy-start | bytes 2949124
  2.1 11.0 %collective-permute-start.3 = (bf16[128,768]{1,0:T(8,128)(2,1)S(1)}, bf16[128,768]{1,0:T(8,128)(2,1)S(1)}, u32[]{:S(2)}, u32[]{:S(2)}) collective-permute-start(bf16[128,768]{1,0:T(8,128)(2,1)S(1)} %get-tuple-element.89), channel_id=1, source_target_pairs={{0,12},{4,0},{8,20},{12,8},{16,28},{20,16},{24,4},{28,24},{1,13},{... | collective-permute-start | bytes 589832 | tf_op jit(solution)/shard_map/ppermute | solution.py:112
  6.1 28.0 %collective-permute-start = (bf16[128,768]{1,0:T(8,128)(2,1)S(1)}, bf16[128,768]{1,0:T(8,128)(2,1)S(1)}, u32[]{:S(2)}, u32[]{:S(2)}) collective-permute-start(bf16[128,768]{1,0:T(8,128)(2,1)S(1)} %get-tuple-element.90), channel_id=1, source_target_pairs={{4,20},{12,28},{20,4},{28,12},{0,16},{8,24},{16,0},{24,8},{5,21},{... | collective-permute-start | bytes 589832 | tf_op jit(solution)/shard_map/ppermute | solution.py:112
  8.7 25.4 %collective-permute-start.1 = (bf16[128,768]{1,0:T(8,128)(2,1)S(1)}, bf16[128,768]{1,0:T(8,128)(2,1)S(1)}, u32[]{:S(2)}, u32[]{:S(2)}) collective-permute-start(bf16[128,768]{1,0:T(8,128)(2,1)S(1)} %get-tuple-element.91), channel_id=1, source_target_pairs={{0,4},{4,24},{8,12},{12,0},{16,20},{20,8},{24,28},{28,16},{1,5},{5... | collective-permute-start | bytes 589832 | tf_op jit(solution)/shard_map/ppermute | solution.py:112
  8.7 26.0 %collective-permute-start.2 = (bf16[128,768]{1,0:T(8,128)(2,1)S(1)}, bf16[128,768]{1,0:T(8,128)(2,1)S(1)}, u32[]{:S(2)}, u32[]{:S(2)}) collective-permute-start(bf16[128,768]{1,0:T(8,128)(2,1)S(1)} %get-tuple-element.92), channel_id=1, source_target_pairs={{0,8},{4,28},{8,16},{12,4},{16,24},{20,12},{24,0},{28,20},{1,9},{5... | collective-permute-start | bytes 589832 | tf_op jit(solution)/shard_map/ppermute | solution.py:112
  9.9 33.0 %collective-permute-start.7 = (bf16[128,768]{1,0:T(8,128)(2,1)S(1)}, bf16[128,768]{1,0:T(8,128)(2,1)S(1)}, u32[]{:S(2)}, u32[]{:S(2)}) collective-permute-start(bf16[128,768]{1,0:T(8,128)(2,1)S(1)} %get-tuple-element.85), channel_id=1, source_target_pairs={{0,12},{4,0},{8,20},{12,8},{16,28},{20,16},{24,4},{28,24},{1,13},{... | collective-permute-start | bytes 589832 | tf_op jit(solution)/shard_map/ppermute | solution.py:112
  13.1 21.6 %copy-start.17 = (bf16[128,768]{1,0:T(8,128)(2,1)}, bf16[128,768]{1,0:T(8,128)(2,1)S(1)}, u32[]{:S(2)}) copy-start(bf16[128,768]{1,0:T(8,128)(2,1)S(1)} %collective-permute-done.3.refs_4_) | copy-start | bytes 589828
  13.1 29.8 %collective-permute-start.4 = (bf16[128,768]{1,0:T(8,128)(2,1)S(1)}, bf16[128,768]{1,0:T(8,128)(2,1)S(1)}, u32[]{:S(2)}, u32[]{:S(2)}) collective-permute-start(bf16[128,768]{1,0:T(8,128)(2,1)S(1)} %get-tuple-element.86), channel_id=1, source_target_pairs={{4,20},{12,28},{20,4},{28,12},{0,16},{8,24},{16,0},{24,8},{5,21},{... | collective-permute-start | bytes 589832 | tf_op jit(solution)/shard_map/ppermute | solution.py:112
  34.2 0.7 copy-start.18
  34.2 8.7 %collective-permute-start.5 = (bf16[128,768]{1,0:T(8,128)(2,1)S(1)}, bf16[128,768]{1,0:T(8,128)(2,1)S(1)}, u32[]{:S(2)}, u32[]{:S(2)}) collective-permute-start(bf16[128,768]{1,0:T(8,128)(2,1)S(1)} %get-tuple-element.87), channel_id=1, source_target_pairs={{0,4},{4,24},{8,12},{12,0},{16,20},{20,8},{24,28},{28,16},{1,5},{5... | collective-permute-start | bytes 589832 | tf_op jit(solution)/shard_map/ppermute | solution.py:112
  34.2 0.7 copy-start.19
  34.2 8.7 %collective-permute-start.6 = (bf16[128,768]{1,0:T(8,128)(2,1)S(1)}, bf16[128,768]{1,0:T(8,128)(2,1)S(1)}, u32[]{:S(2)}, u32[]{:S(2)}) collective-permute-start(bf16[128,768]{1,0:T(8,128)(2,1)S(1)} %get-tuple-element.88), channel_id=1, source_target_pairs={{0,8},{4,28},{8,16},{12,4},{16,24},{20,12},{24,0},{28,20},{1,9},{5... | collective-permute-start | bytes 589832 | tf_op jit(solution)/shard_map/ppermute | solution.py:112
  34.7 0.7 copy-start.21
  42.9 0.7 copy-start.24
  42.9 0.7 copy-start.25
  42.9 0.8 copy-start.26
  42.9 0.8 copy-start.27
  58.4 8.8 %collective-permute-start.12 = (bf16[1552,384]{1,0:T(8,128)(2,1)}, bf16[1552,384]{1,0:T(8,128)(2,1)S(1)}, u32[]{:S(2)}, u32[]{:S(2)}) collective-permute-start(bf16[1552,384]{1,0:T(8,128)(2,1)} %get-tuple-element.59), channel_id=1, source_target_pairs={{0,1},{1,0},{2,3},{3,2},{4,5},{5,4},{6,7},{7,6},{8,9},{9,8},{10,11... | collective-permute-start | bytes 3575816 | tf_op jit(solution)/shard_map/ppermute | solution.py:458
  58.5 8.7 %collective-permute-start.13 = (bf16[1552,384]{1,0:T(8,128)(2,1)}, bf16[1552,384]{1,0:T(8,128)(2,1)S(1)}, u32[]{:S(2)}, u32[]{:S(2)}) collective-permute-start(bf16[1552,384]{1,0:T(8,128)(2,1)} %get-tuple-element.61), channel_id=1, source_target_pairs={{0,1},{1,0},{2,3},{3,2},{4,5},{5,4},{6,7},{7,6},{8,9},{9,8},{10,11... | collective-permute-start | bytes 3575816 | tf_op jit(solution)/shard_map/ppermute | solution.py:458
  59.0 8.2 %collective-permute-start.11 = (bf16[128,768]{1,0:T(8,128)(2,1)}, bf16[128,768]{1,0:T(8,128)(2,1)S(1)}, u32[]{:S(2)}, u32[]{:S(2)}) collective-permute-start(bf16[128,768]{1,0:T(8,128)(2,1)} %get-tuple-element.55), channel_id=1, source_target_pairs={{12,0},{0,4},{20,8},{8,12},{28,16},{16,20},{4,24},{24,28},{13,1},{... | collective-permute-start | bytes 589832 | tf_op jit(solution)/shard_map/ppermute | solution.py:117
  67.2 0.7 copy-start.13
  67.2 1.1 copy-start
  67.2 1.5 %copy-start.2 = (bf16[1552,384]{1,0:T(8,128)(2,1)}, bf16[1552,384]{1,0:T(8,128)(2,1)S(1)}, u32[]{:S(2)}) copy-start(bf16[1552,384]{1,0:T(8,128)(2,1)S(1)} %collective-permute-done.13.refs_5_.refs_6_.came_b) | copy-start | bytes 3575812
  68.7 6.8 %copy-start.23 = (bf16[128,768]{1,0:T(8,128)(2,1)S(1)}, bf16[128,768]{1,0:T(8,128)(2,1)}, u32[]{:S(2)}) copy-start(bf16[128,768]{1,0:T(8,128)(2,1)} %get-tuple-element.52) | copy-start | bytes 589828
  68.7 7.7 %copy-start.22 = (bf16[128,768]{1,0:T(8,128)(2,1)S(1)}, bf16[128,768]{1,0:T(8,128)(2,1)}, u32[]{:S(2)}) copy-start(bf16[128,768]{1,0:T(8,128)(2,1)} %get-tuple-element.53) | copy-start | bytes 589828
  68.7 11.4 %copy-start.20 = (bf16[128,768]{1,0:T(8,128)(2,1)S(1)}, bf16[128,768]{1,0:T(8,128)(2,1)}, u32[]{:S(2)}) copy-start(bf16[128,768]{1,0:T(8,128)(2,1)} %get-tuple-element.54) | copy-start | bytes 589828
  68.7 12.9 %copy-start.4 = (bf16[1536,384]{1,0:T(8,128)(2,1)S(1)}, bf16[1536,384]{1,0:T(8,128)(2,1)}, u32[]{:S(2)}) copy-start(bf16[1536,384]{1,0:T(8,128)(2,1)} %get-tuple-element.60.refs_4_.kept_b) | copy-start | bytes 3538948
  68.7 12.9 %copy-start.5 = (bf16[1536,384]{1,0:T(8,128)(2,1)S(1)}, bf16[1536,384]{1,0:T(8,128)(2,1)}, u32[]{:S(2)}) copy-start(bf16[1536,384]{1,0:T(8,128)(2,1)} %get-tuple-element.58.refs_1_.kept_a) | copy-start | bytes 3538948
  71.7 21.4 %collective-permute-start.14 = (bf16[784,384]{1,0:T(8,128)(2,1)}, bf16[784,384]{1,0:T(8,128)(2,1)S(1)}, u32[]{:S(2)}, u32[]{:S(2)}) collective-permute-start(bf16[784,384]{1,0:T(8,128)(2,1)} %get-tuple-element.64), channel_id=1, source_target_pairs={{0,4},{4,0},{8,12},{12,8},{16,20},{20,16},{24,28},{28,24},{1,5},{5... | collective-permute-start | bytes 1806344 | tf_op jit(solution)/shard_map/ppermute | solution.py:458
  74.0 19.0 %collective-permute-start.15 = (bf16[784,384]{1,0:T(8,128)(2,1)}, bf16[784,384]{1,0:T(8,128)(2,1)S(1)}, u32[]{:S(2)}, u32[]{:S(2)}) collective-permute-start(bf16[784,384]{1,0:T(8,128)(2,1)} %get-tuple-element.66), channel_id=1, source_target_pairs={{0,2},{1,3},{2,0},{3,1},{4,6},{5,7},{6,4},{7,5},{8,10},{9,11},{10,... | collective-permute-start | bytes 1806344 | tf_op jit(solution)/shard_map/ppermute | solution.py:458
  75.5 15.1 %collective-permute-start.8 = (bf16[128,768]{1,0:T(8,128)(2,1)S(1)}, bf16[128,768]{1,0:T(8,128)(2,1)S(1)}, u32[]{:S(2)}, u32[]{:S(2)}) collective-permute-start(bf16[128,768]{1,0:T(8,128)(2,1)S(1)} %copy-done.23), channel_id=1, source_target_pairs={{20,4},{28,12},{4,20},{12,28},{16,0},{24,8},{0,16},{8,24},{21,5},{... | collective-permute-start | bytes 589832 | tf_op jit(solution)/shard_map/ppermute | solution.py:117
  76.4 15.0 %collective-permute-start.9 = (bf16[128,768]{1,0:T(8,128)(2,1)S(1)}, bf16[128,768]{1,0:T(8,128)(2,1)S(1)}, u32[]{:S(2)}, u32[]{:S(2)}) collective-permute-start(bf16[128,768]{1,0:T(8,128)(2,1)S(1)} %copy-done.22), channel_id=1, source_target_pairs={{4,0},{24,4},{12,8},{0,12},{20,16},{8,20},{28,24},{16,28},{5,1},{2... | collective-permute-start | bytes 589832 | tf_op jit(solution)/shard_map/ppermute | solution.py:117
  80.1 13.0 %collective-permute-start.10 = (bf16[128,768]{1,0:T(8,128)(2,1)S(1)}, bf16[128,768]{1,0:T(8,128)(2,1)S(1)}, u32[]{:S(2)}, u32[]{:S(2)}) collective-permute-start(bf16[128,768]{1,0:T(8,128)(2,1)S(1)} %copy-done.20), channel_id=1, source_target_pairs={{8,0},{28,4},{16,8},{4,12},{24,16},{12,20},{0,24},{20,28},{9,1},{2... | collective-permute-start | bytes 589832 | tf_op jit(solution)/shard_map/ppermute | solution.py:117
  81.6 1.3 copy-start.1
  82.9 1.3 copy-start.3
  84.2 8.9 %copy-start.10 = (f32[4,384]{1,0:T(4,128)S(1)}, f32[4,384]{1,0:T(4,128)}, u32[]{:S(2)}) copy-start(f32[4,384]{1,0:T(4,128)} %get-tuple-element.62.refs_0_) | copy-start | bytes 18436
  90.7 2.6 %copy-start.6 = (bf16[128,768]{1,0:T(8,128)(2,1)}, bf16[128,768]{1,0:T(8,128)(2,1)S(1)}, u32[]{:S(2)}) copy-start(bf16[128,768]{1,0:T(8,128)(2,1)S(1)} %collective-permute-done.8.refs_0_.refs_7_) | copy-start | bytes 589828
  91.5 1.8 %copy-start.7 = (bf16[128,768]{1,0:T(8,128)(2,1)}, bf16[128,768]{1,0:T(8,128)(2,1)S(1)}, u32[]{:S(2)}) copy-start(bf16[128,768]{1,0:T(8,128)(2,1)S(1)} %collective-permute-done.9.refs_1_.refs_8_) | copy-start | bytes 589828
  93.1 0.7 copy-start.8
  93.8 7.8 %collective-permute-start.16 = (bf16[400,384]{1,0:T(8,128)(2,1)S(1)}, bf16[400,384]{1,0:T(8,128)(2,1)S(1)}, u32[]{:S(2)}, u32[]{:S(2)}) collective-permute-start(bf16[400,384]{1,0:T(8,128)(2,1)S(1)} %get-tuple-element.68), channel_id=1, source_target_pairs={{0,2},{1,3},{2,0},{3,1},{4,6},{5,7},{6,4},{7,5},{8,10},{9,11},{10,... | collective-permute-start | bytes 921608 | tf_op jit(solution)/shard_map/ppermute | solution.py:458
  94.3 7.5 %collective-permute-start.17 = (bf16[400,384]{1,0:T(8,128)(2,1)S(1)}, bf16[400,384]{1,0:T(8,128)(2,1)S(1)}, u32[]{:S(2)}, u32[]{:S(2)}) collective-permute-start(bf16[400,384]{1,0:T(8,128)(2,1)S(1)} %get-tuple-element.69), channel_id=1, source_target_pairs={{0,4},{4,0},{8,12},{12,8},{16,20},{20,16},{24,28},{28,24},{1,5},{5... | collective-permute-start | bytes 921608 | tf_op jit(solution)/shard_map/ppermute | solution.py:458
  102.1 8.5 %collective-permute-start.18 = (bf16[208,384]{1,0:T(8,128)(2,1)S(1)}, bf16[208,384]{1,0:T(8,128)(2,1)S(1)}, u32[]{:S(2)}, u32[]{:S(2)}) collective-permute-start(bf16[208,384]{1,0:T(8,128)(2,1)S(1)} %get-tuple-element.72), channel_id=1, source_target_pairs={{0,8},{4,12},{8,0},{12,4},{16,24},{20,28},{24,16},{28,20},{1,9},{5... | collective-permute-start | bytes 479240 | tf_op jit(solution)/shard_map/ppermute | solution.py:458
  105.4 13.9 %collective-permute-start.19 = (bf16[208,384]{1,0:T(8,128)(2,1)S(1)}, bf16[208,384]{1,0:T(8,128)(2,1)S(1)}, u32[]{:S(2)}, u32[]{:S(2)}) collective-permute-start(bf16[208,384]{1,0:T(8,128)(2,1)S(1)} %get-tuple-element.73), channel_id=1, source_target_pairs={{0,16},{4,20},{8,24},{12,28},{16,0},{20,4},{24,8},{28,12},{1,17},{... | collective-permute-start | bytes 479240 | tf_op jit(solution)/shard_map/ppermute | solution.py:458
  106.1 13.3 %collective-permute-start.20 = (bf16[208,384]{1,0:T(8,128)(2,1)S(1)}, bf16[208,384]{1,0:T(8,128)(2,1)S(1)}, u32[]{:S(2)}, u32[]{:S(2)}) collective-permute-start(bf16[208,384]{1,0:T(8,128)(2,1)S(1)} %get-tuple-element.74), channel_id=1, source_target_pairs={{0,24},{4,28},{8,16},{12,20},{16,8},{20,12},{24,0},{28,4},{1,25},{... | collective-permute-start | bytes 479240 | tf_op jit(solution)/shard_map/ppermute | solution.py:458
  119.5 0.6 copy-start.11
  120.1 7.5 %copy-start.9 = (bf16[192,384]{1,0:T(8,128)(2,1)}, bf16[192,384]{1,0:T(8,128)(2,1)S(1)}, u32[]{:S(2)}) copy-start(bf16[192,384]{1,0:T(8,128)(2,1)S(1)} %get-tuple-element.76.refs_0_) | copy-start | bytes 442372
  120.1 5.1 %collective-permute-start.21 = (bf16[192,384]{1,0:T(8,128)(2,1)S(1)}, bf16[192,384]{1,0:T(8,128)(2,1)S(1)}, u32[]{:S(2)}, u32[]{:S(2)}) collective-permute-start(bf16[192,384]{1,0:T(8,128)(2,1)S(1)} %get-tuple-element.76.refs_0_), channel_id=1, source_target_pairs={{0,2},{1,3},{2,0},{3,1},{4,6},{5,7},{6,4},{7,5},{8,10},{9,11},{10,... | collective-permute-start | bytes 442376 | tf_op jit(solution)/shard_map/ppermute | solution.py:458
  121.5 6.1 %collective-permute-start.22 = (bf16[192,384]{1,0:T(8,128)(2,1)S(1)}, bf16[192,384]{1,0:T(8,128)(2,1)S(1)}, u32[]{:S(2)}, u32[]{:S(2)}) collective-permute-start(bf16[192,384]{1,0:T(8,128)(2,1)S(1)} %get-tuple-element.76.refs_0_), channel_id=1, source_target_pairs={{0,1},{1,0},{2,3},{3,2},{4,5},{5,4},{6,7},{7,6},{8,9},{9,8},{10,11... | collective-permute-start | bytes 442376 | tf_op jit(solution)/shard_map/ppermute | solution.py:458
  125.2 2.4 %copy-start.14 = (bf16[192,384]{1,0:T(8,128)(2,1)}, bf16[192,384]{1,0:T(8,128)(2,1)S(1)}, u32[]{:S(2)}) copy-start(bf16[192,384]{1,0:T(8,128)(2,1)S(1)} %collective-permute-done.21.refs_1_) | copy-start | bytes 442372
  125.2 2.4 %collective-permute-start.23 = (bf16[192,384]{1,0:T(8,128)(2,1)S(1)}, bf16[192,384]{1,0:T(8,128)(2,1)S(1)}, u32[]{:S(2)}, u32[]{:S(2)}) collective-permute-start(bf16[192,384]{1,0:T(8,128)(2,1)S(1)} %collective-permute-done.21.refs_1_), channel_id=1, source_target_pairs={{0,1},{1,0},{2,3},{3,2},{4,5},{5,4},{6,7},{7,6},{8,9},{9,8},{10,11... | collective-permute-start | bytes 442376 | tf_op jit(solution)/shard_map/ppermute | solution.py:458
  127.6 0.7 copy-start.15
  127.6 0.7 copy-start.16
